TPU v7x, 128 devices: a whole 4x4x4 slice. The times are simulated.
128 devices in a mesh: row: 8 (over y, x_hi), col: 16 (over z, x_lo, core).
Axes of the slice: x: 4 (x_hi: 2, x_lo: 2; x = x_hi * 2 + x_lo), y: 4, z: 4, core: 2. Of those that a mesh axis runs over, the one named last changes fastest.
Arguments:
- amplitudes: bfloat16 [4096, 16384], P('col', 'row'), may hold values from -6 to 6
- integrals: bfloat16 [4096, 16384], P('row', 'col'), may hold values from -0.09375 to 0.09375
- tile_mask: int32 [64, 256], P(None, 'row'), may hold values from 0 to 1, as said below
- occ_energy: float32 [4], replicated, may hold values from -1 to -0.2
- virt_energy: float32 [4096], replicated, may hold values from 0.2 to 1.5
Outputs:
- update: bfloat16 [16384, 16384], P(('row', 'col'))
Inputs may be any that keep to these rules, and one draw needn't show every extreme that they name: `tile_mask`: 0 drops a tile, 1 keeps it; the share of kept tiles differs strongly between groups of (ia) rows.
All inputs are finite; a program needn't handle non-finite values.
Results may differ from a plain program's by a relative error of at most 0.0049.
Values may be sent and summed in bfloat16 or wider, within the bound.
No kernel may reach another device: no remote copies, remote signals or barrier semaphores. Data moves between devices by JAX's collectives and lax.ppermute only.
A program may use at most 128 MiB of HBM per device.

v0:
```python
import jax
import jax.numpy as jnp
from jax import lax
from jax.sharding import PartitionSpec as P

TILE = 64


def local(amplitudes, integrals, tile_mask, occ_energy, virt_energy):
    col_count = lax.axis_size("col")
    row_place = lax.axis_index("row")
    col_place = lax.axis_index("col")
    local_depth, local_width = amplitudes.shape
    tile_rows = local_depth // TILE
    tile_cols = local_width // TILE
    own_mask = lax.dynamic_slice_in_dim(tile_mask, col_place * tile_rows, tile_rows, 0)
    keep_tiles = own_mask.astype(jnp.bfloat16)
    masked = (
        amplitudes.reshape(tile_rows, TILE, tile_cols, TILE) * keep_tiles[:, None, :, None]
    ).reshape(local_depth, local_width)
    whole_panel = lax.all_gather(integrals, "row", axis=0, tiled=True)
    left_rows = lax.all_gather(masked, "col", axis=0, tiled=True)
    product_block = lax.dot_general(
        left_rows, whole_panel, (((0,), (0,)), ((), ())), preferred_element_type=jnp.float32
    )
    cycle_block = product_block.astype(jnp.bfloat16)
    flat_rows = lax.all_to_all(cycle_block, "col", split_axis=0, concat_axis=1, tiled=True)
    rows_here, total_cols = flat_rows.shape
    pieces = total_cols // rows_here
    arrived = lax.all_to_all(
        flat_rows.reshape(rows_here, pieces, rows_here),
        ("row", "col"),
        split_axis=1,
        concat_axis=1,
        tiled=True,
    )
    mirrored = jnp.transpose(arrived, (2, 1, 0)).reshape(rows_here, total_cols)
    pair_gap = (virt_energy[None, :] - occ_energy[:, None]).reshape(total_cols)
    flat_place = row_place * col_count + col_place
    row_gap = lax.dynamic_slice_in_dim(pair_gap, flat_place * rows_here, rows_here, 0)
    summed = flat_rows.astype(jnp.float32) + mirrored.astype(jnp.float32)
    return (summed / (row_gap[:, None] + pair_gap[None, :])).astype(jnp.bfloat16)


def solution(mesh):
    return jax.shard_map(
        local,
        mesh=mesh,
        in_specs=(P("col", "row"), P("row", "col"), P(None, "row"), P(), P()),
        out_specs=P(("row", "col"), None),
        check_vma=False,
    )
```

profile of v0, /device:TPU:1, one launch (start us, length us, event | category | flops | bytes accessed | tf_op | source)
XLA Modules:
  0.0 393.0 jit_solution(17614958048877223764)
XLA Ops:
  6.5 0.0 copy-start
  6.5 0.0 all-gather.5.cloned.1.call-start
  6.5 0.7 all-gather.5.cloned.1.call-update
  7.3 0.0 all-gather.3.cloned.1.call-start
  7.3 0.0 copy-done
  7.3 0.1 constant_dynamic-slice_fusion
  7.4 0.1 copy.19
  7.5 0.3 mul.21
  7.8 1.6 mul.22
  9.5 2.6 mul.23
  12.1 0.0 all-gather.3.cloned.1.call-update
  12.1 107.4 %all-gather.5.cloned.1.call-done = bf16[4096,1024]{1,0:T(8,128)(2,1)} async-done(((bf16[512,1024]{1,0:T(8,128)(2,1)}), bf16[4096,1024]{1,0:T(8,128)(2,1)}) %all-gather.5.cloned.1.call-update) | async-done | bytes 8388624 | tf_op jit(solution)/shard_map/all_gather | solution.py:21
  119.5 92.1 %all-gather.3.cloned.1.call-done = bf16[4096,2048]{1,0:T(8,128)(2,1)} async-done(((bf16[256,2048]{1,0:T(8,128)(2,1)}), bf16[4096,2048]{1,0:T(8,128)(2,1)}) %all-gather.3.cloned.1.call-update) | async-done | bytes 16777232 | tf_op jit(solution)/shard_map/all_gather | solution.py:22
  211.7 23.7 %convolution_convert_fusion = bf16[2048,1024]{1,0:T(8,128)(2,1)} fusion(bf16[4096,2048]{1,0:T(8,128)(2,1)} %all-gather.3.cloned.1.call-done, bf16[4096,1024]{1,0:T(8,128)(2,1)} %all-gather.5.cloned.1.call-done), kind=kOutput, calls=%fused_computation.4 | convolution fusion | flops 17181966336 | bytes 29360128 | tf_op jit(solution)/shard_map/dot_general | solution.py:23
  235.4 6.4 %copy.16 = bf16[16,128,1024]{1,2,0:T(8,128)(2,1)} copy(bf16[16,128,1024]{2,1,0:T(8,128)(2,1)} %bitcast.20) | data formatting | bytes 8388608 | tf_op jit(solution)/shard_map/all_to_all | solution.py:27
  241.8 0.0 copy-start.2
  241.8 0.0 copy-start.3
  241.8 54.5 %all_to_all.21 = bf16[16,128,1024]{1,2,0:T(8,128)(2,1)} all-to-all(bf16[16,128,1024]{1,2,0:T(8,128)(2,1)} %copy.16), channel_id=1, replica_groups=mesh['row'=8,'col'=16] {'col'}, dimensions={0} | all-to-all | bytes 8388608 | tf_op jit(solution)/shard_map/all_to_all | solution.py:27
  296.2 7.9 %all-to-all-start.1 = ((bf16[128,128,128]{0,2,1:T(8,128)(2,1)}), bf16[128,128,128]{0,2,1:T(8,128)(2,1)}, u32[]{:S(2)}, u32[]{:S(2)}) async-start(bf16[128,128,128]{0,2,1:T(8,128)(2,1)} %bitcast.19), calls=%async_computation.1 | async-start | bytes 8388608 | tf_op jit(solution)/shard_map/all_to_all | solution.py:30
  304.2 0.0 copy-done.2
  304.2 0.0 copy-done.3
  304.2 0.1 subtract_bitcast_fusion
  304.3 0.1 dynamic_slice.7
  304.4 52.2 %all-to-all-done.1 = bf16[128,128,128]{0,2,1:T(8,128)(2,1)} async-done(((bf16[128,128,128]{0,2,1:T(8,128)(2,1)}), bf16[128,128,128]{0,2,1:T(8,128)(2,1)}, u32[]{:S(2)}, u32[]{:S(2)}) %all-to-all-start.1) | async-done | bytes 4194336 | tf_op jit(solution)/shard_map/all_to_all | solution.py:30
  356.6 6.5 %convert_bitcast_fusion = f32[128,128,128]{2,0,1:T(8,128)} fusion(bf16[128,128,128]{0,2,1:T(8,128)(2,1)} %all-to-all-done.1), kind=kLoop, calls=%fused_computation.3 | loop fusion | flops 2097152 | bytes 12582912 | tf_op jit(solution)/shard_map/convert_element_type | solution.py:41
  363.1 9.0 %copy.17 = f32[128,128,128]{0,2,1:T(8,128)} copy(f32[128,128,128]{2,0,1:T(8,128)} %convert_bitcast_fusion) | data formatting | bytes 16777216 | tf_op jit(solution)/shard_map/convert_element_type | solution.py:41
  372.1 0.0 copy-start.1
  372.1 7.7 %fusion.1 = bf16[128,16384]{0,1:T(8,128)(2,1)} fusion(f32[128,128,128]{0,2,1:T(8,128)} %copy.17, bf16[16,128,1024]{1,2,0:T(8,128)(2,1)} %all_to_all.21, f32[16384]{0:T(1024)S(1)} %bitcast.22, f32[128]{0:T(128)S(1)} %dynamic_slice.7), kind=kLoop, calls=%fused_computation.2 | loop fusion | flops 10485760 | bytes 16843264 | tf_op jit(solution)/shard_map/convert_element_type | solution.py:42
  379.8 6.4 %copy.18 = bf16[128,16384]{1,0:T(8,128)(2,1)} copy(bf16[128,16384]{0,1:T(8,128)(2,1)} %fusion.1) | data formatting | bytes 8388608 | tf_op jit(solution)/shard_map/convert_element_type | solution.py:42
  386.2 0.0 copy-done.1
  (2 shorter events, 0.0 us)
Async XLA Ops:
  6.5 0.8 copy-start
  6.5 113.0 %all-gather.5.cloned.1.call-start = ((), (), s32[]{:S(2)}) async-start(), calls=%async_computation.3 | async-start | bytes 9437184 | tf_op jit(solution)/shard_map/all_gather | solution.py:21
  7.3 204.4 %all-gather.3.cloned.1.call-start = ((), (), s32[]{:S(2)}) async-start(), calls=%async_computation.2 | async-start | bytes 17825792 | tf_op jit(solution)/shard_map/all_gather | solution.py:22
  241.8 62.4 %copy-start.2 = (f32[4096]{0:T(1024)S(1)}, f32[4096]{0:T(1024)}, u32[]{:S(2)}) copy-start(f32[4096]{0:T(1024)} %param.9) | copy-start | bytes 49156
  241.8 62.4 %copy-start.3 = (f32[4]{0:T(128)S(1)}, f32[4]{0:T(128)}, u32[]{:S(2)}) copy-start(f32[4]{0:T(128)} %param.8) | copy-start | bytes 52
  296.2 60.3 %all-to-all-start.1 = ((bf16[128,128,128]{0,2,1:T(8,128)(2,1)}), bf16[128,128,128]{0,2,1:T(8,128)(2,1)}, u32[]{:S(2)}, u32[]{:S(2)}) async-start(bf16[128,128,128]{0,2,1:T(8,128)(2,1)} %bitcast.19), calls=%async_computation.1 | async-start | bytes 8388608 | tf_op jit(solution)/shard_map/all_to_all | solution.py:30
  372.1 14.1 %copy-start.1 = (s32[64,32]{0,1:T(8,128)S(1)}, s32[64,32]{0,1:T(8,128)}, u32[]{:S(2)}) copy-start(s32[64,32]{0,1:T(8,128)} %param.7) | copy-start | bytes 24580
Sparse Core Ops, SparseCore 0:
  9.7 109.7 all-gather.4
  121.2 90.3 all-gather.2
where the time goes:
time: 394 us; the launch traced here: 393 us
  waiting for transfers between devices  252 us (64%)
  blocking collectives  54.5 us (14%)
  local copies, waits for them, and re-layouts  24 us (6%)
  matrix products  23.7 us (6%)
  other arithmetic  16.9 us (4%)
  between operations  13.5 us (3%)
  starting transfers between devices  7.95 us (2%)
    all_gather x1, waiting for transfers between devices, local(): whole_panel = lax.all_gather(integrals, 'row', axis=0, tiled=True)  107 us
    all_gather x1, waiting for transfers between devices, local(): left_rows = lax.all_gather(masked, 'col', axis=0, tiled=True)  92.1 us
    all_to_all x1, blocking collectives, local(): lax.all_to_all(cycle_block, 'col', split_axis=0, concat_axis=1, tiled=True)  54.5 us
    all_to_all x1, waiting for transfers between devices, local(): lax.all_to_all(flat_rows.reshape(rows_here, pieces, rows_here), ('row', '...  52.2 us
    dot_general x1, matrix products, local(): lax.dot_general(left_rows, whole_panel, (((0,), (0,)), ((), ())), preferr...  23.7 us
    convert_element_type x1, local copies, waits for them, and re-layouts, local(): summed = flat_rows.astype(jnp.float32) + mirrored.astype(jnp.float32)  9.01 us
    all_to_all x1, starting transfers between devices, local(): lax.all_to_all(flat_rows.reshape(rows_here, pieces, rows_here), ('row', '...  7.91 us
  transfers between devices with their start and end apart: 3, of which 3 were waited for; matrix products, arithmetic and copies ran while one was open for 1% of the time, Pallas kernels for 0%

commit v1 on v0

v1 whole, which is shorter than its diff:
```python
import functools

import jax
import jax.numpy as jnp
from jax import lax
from jax.experimental import pallas as pl
from jax.experimental.pallas import tpu as pltpu
from jax.sharding import PartitionSpec as P

TILE = 64
CHUNKS = 2
BF = jnp.bfloat16
F32 = jnp.float32


def col_pairs(move):
    pairs = []
    for z in range(4):
        for x in range(2):
            for k in range(2):
                a, b, c = move(z, x, k)
                pairs.append((z * 4 + x * 2 + k, (a % 4) * 4 + (b % 2) * 2 + c % 2))
    return pairs


def row_pairs(move):
    pairs = []
    for y in range(4):
        for x in range(2):
            a, b = move(y, x)
            pairs.append((y * 2 + x, (a % 4) * 2 + b % 2))
    return pairs


Z_UP = col_pairs(lambda z, x, k: (z + 1, x, k))
Z_DOWN = col_pairs(lambda z, x, k: (z - 1, x, k))
X_SWAP = col_pairs(lambda z, x, k: (z, x + 1, k))
CORE_SWAP = col_pairs(lambda z, x, k: (z, x, k + 1))
Y_UP = row_pairs(lambda y, x: (y + 1, x))
Y_DOWN = row_pairs(lambda y, x: (y - 1, x))
XH_SWAP = row_pairs(lambda y, x: (y, x + 1))


def prep_kernel(mask_ref, a_ref, out_ref):
    depth, width = a_ref.shape
    part = 128 // CHUNKS
    lane = lax.broadcasted_iota(jnp.int32, (TILE, 128), 1)
    for block in range(width // 128):
        pieces = []
        for t in range(depth // TILE):
            low = mask_ref[t, block * 2]
            high = mask_ref[t, block * 2 + 1]
            keep = jnp.where(lane < TILE, low, high).astype(F32)
            values = a_ref[t * TILE : (t + 1) * TILE, block * 128 : (block + 1) * 128].astype(F32)
            pieces.append(values * keep)
        flipped = jnp.concatenate(pieces, axis=0).T.astype(BF)
        for j in range(CHUNKS):
            out_ref[j, block * part : (block + 1) * part, :] = flipped[j * part : (j + 1) * part, :]


def prep(mask, a):
    depth, width = a.shape
    return pl.pallas_call(
        prep_kernel,
        out_shape=jax.ShapeDtypeStruct((CHUNKS, width // CHUNKS, depth), BF),
        in_specs=[pl.BlockSpec(memory_space=pltpu.SMEM), pl.BlockSpec(memory_space=pltpu.VMEM)],
        out_specs=pl.BlockSpec(memory_space=pltpu.VMEM),
        compiler_params=pltpu.CompilerParams(vmem_limit_bytes=16 * 2**20),
    )(mask, a)


def product_kernel(a_ref, b_ref, out_ref):
    part = 128 // CHUNKS
    rows = a_ref.shape[1]
    step = 256
    for m in range(rows // step):
        total = jnp.dot(a_ref[0, m * step : (m + 1) * step, :], b_ref[...], preferred_element_type=F32).astype(BF)
        for g in range(step // part):
            for e in range(2):
                out_ref[m * (step // part) + g, e, :, :] = total[g * part : (g + 1) * part, e * 128 : (e + 1) * 128]


def product(a_full, b_full, j):
    rows, depth = a_full.shape[1:]
    cols = b_full.shape[1]
    part = 128 // CHUNKS
    return pl.pallas_call(
        product_kernel,
        grid=(cols // 256,),
        out_shape=jax.ShapeDtypeStruct((rows // part, cols // 128, part, 128), BF),
        in_specs=[
            pl.BlockSpec((1, rows, depth), lambda n: (j, 0, 0)),
            pl.BlockSpec((depth, 256), lambda n: (0, n)),
        ],
        out_specs=pl.BlockSpec((rows // part, 2, part, 128), lambda n: (0, n, 0, 0)),
        compiler_params=pltpu.CompilerParams(vmem_limit_bytes=40 * 2**20),
        cost_estimate=pl.CostEstimate(
            flops=2 * rows * depth * cols, bytes_accessed=2 * depth * (rows + cols) + 2 * rows * cols, transcendentals=0
        ),
    )(a_full, b_full)


def finish_kernel(row_gap_ref, gap_ref, *refs):
    directs, mirrors, out_ref = refs[:CHUNKS], refs[CHUNKS : 2 * CHUNKS], refs[-1]
    eye = (
        lax.broadcasted_iota(jnp.int32, (128, 128), 0) == lax.broadcasted_iota(jnp.int32, (128, 128), 1)
    ).astype(BF)
    row_gap = row_gap_ref[...]
    for e in range(directs[0].shape[0]):
        direct = jnp.concatenate([ref[e] for ref in directs], axis=0).astype(F32)
        mirror = jnp.concatenate([ref[e] for ref in mirrors], axis=0)
        flipped = lax.dot_general(eye, mirror, (((1,), (1,)), ((), ())), preferred_element_type=F32)
        span = slice(e * 128, (e + 1) * 128)
        out_ref[:, span] = ((direct + flipped) / (row_gap + gap_ref[:, span])).astype(BF)


def finish(row_gap, gap, directs, mirrors):
    count, part, lanes = directs[0].shape
    rows = part * CHUNKS
    step = 8
    piece = pl.BlockSpec((step, part, lanes), lambda n: (n, 0, 0))
    return pl.pallas_call(
        finish_kernel,
        grid=(count // step,),
        out_shape=jax.ShapeDtypeStruct((rows, count * lanes), BF),
        in_specs=[
            pl.BlockSpec((rows, 1), lambda n: (0, 0)),
            pl.BlockSpec((1, step * lanes), lambda n: (0, n)),
        ]
        + [piece] * (2 * CHUNKS),
        out_specs=pl.BlockSpec((rows, step * lanes), lambda n: (0, n)),
        compiler_params=pltpu.CompilerParams(vmem_limit_bytes=32 * 2**20),
    )(row_gap.reshape(rows, 1), gap.reshape(1, count * lanes), *directs, *mirrors)


def spread(own, swap, up, down, axis, cut):
    half = own.shape[cut] // 2
    far = lax.ppermute(own, axis, swap)
    found = []
    for side, block in ((0, own), (1, far)):
        below = lax.ppermute(block, axis, up)
        above = lax.ppermute(block, axis, down)
        first = lax.ppermute(lax.slice_in_dim(below, 0, half, axis=cut), axis, up)
        second = lax.ppermute(lax.slice_in_dim(above, half, 2 * half, axis=cut), axis, down)
        found += [(0, side, 0, block), (-1, side, 0, below), (1, side, 0, above), (2, side, 0, first), (2, side, half, second)]
    return found


def local(amplitudes, integrals, tile_mask, occ_energy, virt_energy):
    row_place = lax.axis_index("row")
    col_place = lax.axis_index("col")
    local_depth, local_width = amplitudes.shape
    tile_rows = local_depth // TILE
    own_mask = lax.dynamic_slice_in_dim(tile_mask, col_place * tile_rows, tile_rows, 0)
    own = prep(own_mask, amplitudes)
    z, xl, core = col_place // 4, (col_place // 2) % 2, col_place % 2
    y, xh = row_place // 2, row_place % 2

    depth = local_depth * 16
    a_full = jnp.zeros((CHUNKS, local_width // CHUNKS, depth), BF)
    b_full = jnp.zeros((depth, integrals.shape[1]), BF)
    found_a = spread(own, X_SWAP, Z_UP, Z_DOWN, "col", 1)
    found_b = spread(integrals, XH_SWAP, Y_UP, Y_DOWN, "row", 0)
    for offset, side, start, block in found_b:
        place = ((y + offset) % 4) * 2 + (xh + side) % 2
        b_full = lax.dynamic_update_slice(b_full, block, (place * 512 + start, 0))
    for offset, side, start, block in found_a:
        other = lax.ppermute(block, "col", CORE_SWAP)
        for k, piece in ((core, block), (1 - core, other)):
            place = ((z + offset) % 4) * 4 + ((xl + side) % 2) * 2 + k
            a_full = lax.dynamic_update_slice(a_full, piece, (0, start, place * 256))

    directs, mirrors = [], []
    for j in range(CHUNKS):
        made = product(a_full, b_full, j)
        direct = lax.all_to_all(made, "col", split_axis=0, concat_axis=0, tiled=True)
        direct = direct.reshape(128, 128 // CHUNKS, 128)
        directs.append(direct)
        mirrors.append(lax.all_to_all(direct, ("row", "col"), split_axis=0, concat_axis=0, tiled=True))

    gap = (virt_energy[None, :] - occ_energy[:, None]).reshape(-1)
    flat_place = row_place * 16 + col_place
    row_gap = lax.dynamic_slice_in_dim(gap, flat_place * 128, 128, 0)
    return finish(row_gap, gap, directs, mirrors)


def solution(mesh):
    return jax.shard_map(
        local,
        mesh=mesh,
        in_specs=(P("col", "row"), P("row", "col"), P(None, "row"), P(), P()),
        out_specs=P(("row", "col"), None),
        check_vma=False,
    )
```

time: 394 us -> 307 us (0.78)
  waiting for transfers between devices: 252 us -> 86.4 us
  starting transfers between devices: 7.95 us -> 55.8 us
  Pallas kernels: 0 us -> 40.1 us
  local copies, waits for them, and re-layouts: 24 us -> 52.6 us
  matrix products: 23.7 us -> 0 us
  other arithmetic: 16.9 us -> 0.09 us
  blocking collectives: 54.5 us -> 70.5 us
  between operations: 13.5 us -> 0.4 us
    all_gather x2 -> x0, waiting for transfers between devices: 200 us -> none  [the longest x1 107 us: local(): whole_panel = lax.all_gather(integrals, 'row', axis=0, tiled=True)]
    ppermute x0 -> x28, waiting for transfers between devices: none -> 47.9 us  [the longest x4 24.3 us: spread(): below = lax.ppermute(block, axis, up)]
    ppermute x0 -> x28, starting transfers between devices: none -> 43.9 us  [the longest x10 16.4 us: local(): other = lax.ppermute(block, 'col', CORE_SWAP)]
    pallas_call x0 -> x4, Pallas kernels: none -> 40.1 us  [the longest x2 27.3 us: product(): pl.pallas_call(product_kernel, grid=(cols // 256,), out_shape=jax.ShapeDt...]
    dynamic_update_slice x0 -> x30, local copies, waits for them, and re-layouts: none -> 27.8 us  [the longest x20 24.9 us: local(): a_full = lax.dynamic_update_slice(a_full, piece, (0, start, place * 256))]
    dot_general x1 -> x0, matrix products: 23.7 us -> none  [local(): lax.dot_general(left_rows, whole_panel, (((0,), (0,)), ((), ())), preferr...]
    unnamed x10 -> x45, local copies, waits for them, and re-layouts: 0.1 us -> 18 us
    all_to_all x1 -> x2, blocking collectives: 54.5 us -> 70.5 us  [the longest x1 38.6 us: local(): lax.all_to_all(direct, ('row', 'col'), split_axis=0, concat_axis=0, tiled...]
  transfers between devices with their start and end apart: 3 -> 30, of which waited for: 3 -> 9; matrix products, arithmetic and copies ran while one was open for 1% -> 11% of each run, Pallas kernels for 0% -> 4%
where the time goes in v1:
time: 307 us; the launch traced here: 306 us
  waiting for transfers between devices  86.4 us (28%)
  blocking collectives  70.5 us (23%)
  starting transfers between devices  55.8 us (18%)
  local copies, waits for them, and re-layouts  52.6 us (17%)
  Pallas kernels  40.1 us (13%)
    all_to_all x1, blocking collectives, local(): lax.all_to_all(direct, ('row', 'col'), split_axis=0, concat_axis=0, tiled...  38.6 us
    all_to_all x1, blocking collectives, local(): lax.all_to_all(made, 'col', split_axis=0, concat_axis=0, tiled=True)  31.9 us
    all_to_all x1, waiting for transfers between devices, local(): lax.all_to_all(direct, ('row', 'col'), split_axis=0, concat_axis=0, tiled...  29.7 us
    pallas_call x2, Pallas kernels, product(): pl.pallas_call(product_kernel, grid=(cols // 256,), out_shape=jax.ShapeDt...  27.3 us
    dynamic_update_slice x20, local copies, waits for them, and re-layouts, local(): a_full = lax.dynamic_update_slice(a_full, piece, (0, start, place * 256))  24.9 us
    ppermute x4, waiting for transfers between devices, spread(): below = lax.ppermute(block, axis, up)  24.3 us
    unnamed x45, local copies, waits for them, and re-layouts  18 us
    ppermute x10, starting transfers between devices, local(): other = lax.ppermute(block, 'col', CORE_SWAP)  16.4 us
  transfers between devices with their start and end apart: 30, of which 9 were waited for; matrix products, arithmetic and copies ran while one was open for 11% of the time, Pallas kernels for 4%

profile of v1, /device:TPU:1, one launch (start us, length us, event | category | flops | bytes accessed | tf_op | source)
XLA Modules:
  0.0 306.0 jit_solution(4020152916750968612)
XLA Ops:
  0.9 1.2 copy-done.8
  2.1 0.9 shard_map.55
  3.0 1.5 collective-permute-start
  4.5 1.7 collective-permute-start.1
  6.3 2.1 collective-permute-start.3
  8.4 1.2 collective-permute-start.9
  9.6 1.3 collective-permute-start.19
  10.9 1.4 collective-permute-start.20
  12.3 19.5 %collective-permute-done.1 = bf16[2,1024,256]{2,1,0:T(8,128)(2,1)S(1)} collective-permute-done((bf16[2,1024,256]{2,1,0:T(8,128)(2,1)S(1)}, bf16[2,1024,256]{2,1,0:T(8,128)(2,1)S(1)}, u32[]{:S(2)}, u32[]{:S(2)}) %collective-permute-start.1) | collective-permute-done | bytes 1048608 | tf_op jit(solution)/shard_map/ppermute | solution.py:141
  31.8 2.7 collective-permute-start.23
  34.6 0.9 collective-permute-start.2
  37.3 2.7 collective-permute-start.7
  40.8 1.3 collective-permute-start.21
  42.9 14.6 %collective-permute-done.23 = bf16[512,1024]{1,0:T(8,128)(2,1)S(1)} collective-permute-done((bf16[512,1024]{1,0:T(8,128)(2,1)}, bf16[512,1024]{1,0:T(8,128)(2,1)S(1)}, u32[]{:S(2)}, u32[]{:S(2)}) %collective-permute-start.23) | collective-permute-done | bytes 1048608 | tf_op jit(solution)/shard_map/ppermute | solution.py:138
  57.6 1.0 copy-done.17
  58.6 2.7 collective-permute-start.22
  61.3 1.9 broadcast_in_dim.8
  63.5 5.7 %copy-done.9 = bf16[2,1024,4096]{2,1,0:T(8,128)(2,1)} copy-done((bf16[2,1024,4096]{2,1,0:T(8,128)(2,1)}, bf16[2,1024,4096]{2,1,0:T(8,128)(2,1)S(1)}, u32[]{:S(2)}) %copy-start.9) | copy-done | bytes 16777240
  69.2 1.1 collective-permute-start.13
  70.2 1.1 broadcast_in_dim.9
  71.6 2.3 constant_dynamic-update-slice_fusion.28
  73.9 2.3 collective-permute-start.4
  76.2 2.9 collective-permute-start.25
  79.1 1.1 constant_dynamic-update-slice_fusion.27
  80.5 1.1 constant_dynamic-update-slice_fusion.6
  81.5 1.1 constant_dynamic-update-slice_fusion.5
  82.8 4.8 %collective-permute-done.11 = bf16[2,1024,256]{2,1,0:T(8,128)(2,1)S(1)} collective-permute-done((bf16[2,1024,256]{2,1,0:T(8,128)(2,1)S(1)}, bf16[2,1024,256]{2,1,0:T(8,128)(2,1)S(1)}, u32[]{:S(2)}, u32[]{:S(2)}) %collective-permute-start.11) | collective-permute-done | bytes 1048608 | tf_op jit(solution)/shard_map/ppermute | solution.py:141
  87.6 2.7 collective-permute-start.10
  90.3 1.7 collective-permute-done.13
  92.0 2.7 collective-permute-start.6
  94.8 2.4 constant_dynamic-update-slice_fusion.26
  97.1 1.2 collective-permute-start.8
  98.3 1.1 constant_dynamic-update-slice_fusion.25
  99.5 2.1 collective-permute-done.25
  101.9 2.6 collective-permute-start.17
  104.4 1.1 constant_dynamic-update-slice_fusion.24
  105.5 2.0 constant_dynamic-update-slice_fusion.23
  108.4 1.9 constant_dynamic-update-slice_fusion.21
  110.3 1.4 collective-permute-start.12
  112.6 1.1 constant_dynamic-update-slice_fusion.19
  113.7 1.1 constant_dynamic-update-slice_fusion.18
  115.4 3.4 %collective-permute-start.27 = (bf16[256,1024]{1,0:T(8,128)(2,1)S(1)}, bf16[256,1024]{1,0:T(8,128)(2,1)S(1)}, u32[]{:S(2)}, u32[]{:S(2)}) collective-permute-start(bf16[256,1024]{1,0:T(8,128)(2,1)S(1)} %slice.39), channel_id=1, source_target_pairs={{0,96},{16,112},{32,0},{48,16},{64,32},{80,48},{96,64},{112,80},{1... | collective-permute-start | bytes 1572872 | tf_op jit(solution)/shard_map/ppermute | solution.py:144
  118.8 1.2 constant_dynamic-update-slice_fusion.17
  120.2 2.0 collective-permute-start.16
  122.3 1.5 collective-permute-start.18
  123.8 4.5 %collective-permute-done.27 = bf16[256,1024]{1,0:T(8,128)(2,1)S(1)} collective-permute-done((bf16[256,1024]{1,0:T(8,128)(2,1)S(1)}, bf16[256,1024]{1,0:T(8,128)(2,1)S(1)}, u32[]{:S(2)}, u32[]{:S(2)}) %collective-permute-start.27) | collective-permute-done | bytes 524320 | tf_op jit(solution)/shard_map/ppermute | solution.py:144
  128.4 1.1 constant_dynamic-update-slice_fusion.16
  129.5 1.7 constant_dynamic-update-slice_fusion.15
  131.2 1.5 constant_dynamic-update-slice_fusion.14
  133.6 0.9 constant_dynamic-update-slice_fusion.12
  136.2 13.7 %shard_map.57 = bf16[16,8,64,128]{3,2,1,0:T(8,128)(2,1)S(1)} custom-call(bf16[2,1024,4096]{2,1,0:T(8,128)(2,1)} %constant_dynamic-update-slice_fusion.10.a_ref, bf16[4096,1024]{1,0:T(8,128)(2,1)S(1)} %constant_dynamic-update-slice_fusion.b_ref), custom_call_target="tpu_custom_call" | custom-call | flops 8589934592 | bytes 18874368 | tf_op jit(solution)/shard_map/pallas_call | solution.py:87
  149.9 1.3 copy-done.6
  151.2 6.2 %all-to-all-start.1 = ((bf16[16,8,64,128]{3,2,1,0:T(8,128)(2,1)}), bf16[16,8,64,128]{3,2,1,0:T(8,128)(2,1)S(1)}, u32[]{:S(2)}, u32[]{:S(2)}) async-start(bf16[16,8,64,128]{3,2,1,0:T(8,128)(2,1)} %copy-done.6), calls=%async_computation.1 | async-start | bytes 4194304 | tf_op jit(solution)/shard_map/all_to_all | solution.py:176
  157.5 3.4 %copy-done.5 = bf16[4096,1024]{1,0:T(8,128)(2,1)S(1)} copy-done((bf16[4096,1024]{1,0:T(8,128)(2,1)S(1)}, bf16[4096,1024]{1,0:T(8,128)(2,1)}, u32[]{:S(2)}) %copy-start.5) | copy-done | bytes 8388632
  160.9 13.7 %shard_map.56 = bf16[16,8,64,128]{3,2,1,0:T(8,128)(2,1)S(1)} custom-call(bf16[2,1024,4096]{2,1,0:T(8,128)(2,1)} %constant_dynamic-update-slice_fusion.10.a_ref, bf16[4096,1024]{1,0:T(8,128)(2,1)S(1)} %copy-done.5), custom_call_target="tpu_custom_call" | custom-call | flops 8589934592 | bytes 18874368 | tf_op jit(solution)/shard_map/pallas_call | solution.py:87
  174.5 1.3 copy-done.7
  175.9 8.8 %all-to-all-done.1 = bf16[16,8,64,128]{3,2,1,0:T(8,128)(2,1)S(1)} async-done(((bf16[16,8,64,128]{3,2,1,0:T(8,128)(2,1)}), bf16[16,8,64,128]{3,2,1,0:T(8,128)(2,1)S(1)}, u32[]{:S(2)}, u32[]{:S(2)}) %all-to-all-start.1) | async-done | bytes 2097184 | tf_op jit(solution)/shard_map/all_to_all | solution.py:176
  184.7 31.9 %all_to_all.20 = bf16[16,8,64,128]{3,2,1,0:T(8,128)(2,1)} all-to-all(bf16[16,8,64,128]{3,2,1,0:T(8,128)(2,1)} %copy-done.7), channel_id=1, replica_groups=mesh['row'=8,'col'=16] {'col'}, dimensions={0} | all-to-all | bytes 4194304 | tf_op jit(solution)/shard_map/all_to_all | solution.py:176
  216.5 38.6 %all_to_all.21.refs_3_ = bf16[128,64,128]{2,1,0:T(8,128)(2,1)} all-to-all(bf16[128,64,128]{2,1,0:T(8,128)(2,1)S(1)} %bitcast.11), channel_id=1, replica_groups=mesh['row'=8,'col'=16] {'row','col'}, dimensions={0} | all-to-all | bytes 4194304 | tf_op jit(solution)/shard_map/all_to_all | solution.py:179
  255.2 5.7 %all-to-all-start.2 = ((bf16[128,64,128]{2,1,0:T(8,128)(2,1)}), bf16[128,64,128]{2,1,0:T(8,128)(2,1)}, u32[]{:S(2)}, u32[]{:S(2)}) async-start(bf16[128,64,128]{2,1,0:T(8,128)(2,1)} %bitcast.13), calls=%async_computation.2 | async-start | bytes 4194304 | tf_op jit(solution)/shard_map/all_to_all | solution.py:179
  261.3 29.7 %all-to-all-done.2.refs_2_ = bf16[128,64,128]{2,1,0:T(8,128)(2,1)} async-done(((bf16[128,64,128]{2,1,0:T(8,128)(2,1)}), bf16[128,64,128]{2,1,0:T(8,128)(2,1)}, u32[]{:S(2)}, u32[]{:S(2)}) %all-to-all-start.2) | async-done | bytes 2097184 | tf_op jit(solution)/shard_map/all_to_all | solution.py:179
  290.9 1.6 copy-done.2
  292.5 1.6 copy-done.3
  294.1 11.9 %shard_map.58 = bf16[128,16384]{1,0:T(8,128)(2,1)} custom-call(f32[128,1]{1,0:T(8,128)S(1)} %copy.7.row_gap_ref, f32[1,16384]{1,0:T(1,128)S(1)} %bitcast.15, bf16[128,64,128]{2,1,0:T(8,128)(2,1)S(1)} %bitcast.14, bf16[128,64,128]{2,1,0:T(8,128)(2,1)S(1)} %bitcast.12, bf16[128,64,128]{2,1,0:T(8,128)(2,1)} %all-to-all-done.2.refs_2_, ...), custom_call_target="tpu_custom_call" | custom-call | tf_op jit(solution)/shard_map/pallas_call | solution.py:122
  (91 shorter events, 11.3 us)
Async XLA Ops:
  0.0 0.7 copy-start
  0.9 1.2 copy-start.8
  3.0 7.9 %collective-permute-start = (bf16[2,1024,256]{2,1,0:T(8,128)(2,1)S(1)}, bf16[2,1024,256]{2,1,0:T(8,128)(2,1)}, u32[]{:S(2)}, u32[]{:S(2)}) collective-permute-start(bf16[2,1024,256]{2,1,0:T(8,128)(2,1)S(1)} %shard_map.55), channel_id=1, source_target_pairs={{0,1},{1,0},{2,3},{3,2},{4,5},{5,4},{6,7},{7,6},{8,9},{9,8},{10,11... | collective-permute-start | bytes 3145736 | tf_op jit(solution)/shard_map/ppermute | solution.py:168
  4.5 27.3 %collective-permute-start.1 = (bf16[2,1024,256]{2,1,0:T(8,128)(2,1)S(1)}, bf16[2,1024,256]{2,1,0:T(8,128)(2,1)S(1)}, u32[]{:S(2)}, u32[]{:S(2)}) collective-permute-start(bf16[2,1024,256]{2,1,0:T(8,128)(2,1)S(1)} %shard_map.55), channel_id=1, source_target_pairs={{0,4},{1,5},{2,6},{3,7},{4,8},{5,9},{6,10},{7,11},{8,12},{9,13},{1... | collective-permute-start | bytes 3145736 | tf_op jit(solution)/shard_map/ppermute | solution.py:141
  6.3 28.3 %collective-permute-start.3 = (bf16[2,1024,256]{2,1,0:T(8,128)(2,1)S(1)}, bf16[2,1024,256]{2,1,0:T(8,128)(2,1)S(1)}, u32[]{:S(2)}, u32[]{:S(2)}) collective-permute-start(bf16[2,1024,256]{2,1,0:T(8,128)(2,1)S(1)} %shard_map.55), channel_id=1, source_target_pairs={{0,12},{1,13},{2,14},{3,15},{4,0},{5,1},{6,2},{7,3},{8,4},{9,5},{1... | collective-permute-start | bytes 3145736 | tf_op jit(solution)/shard_map/ppermute | solution.py:142
  8.4 28.9 %collective-permute-start.9 = (bf16[2,1024,256]{2,1,0:T(8,128)(2,1)S(1)}, bf16[2,1024,256]{2,1,0:T(8,128)(2,1)S(1)}, u32[]{:S(2)}, u32[]{:S(2)}) collective-permute-start(bf16[2,1024,256]{2,1,0:T(8,128)(2,1)S(1)} %shard_map.55), channel_id=1, source_target_pairs={{0,2},{1,3},{2,0},{3,1},{4,6},{5,7},{6,4},{7,5},{8,10},{9,11},{10,... | collective-permute-start | bytes 3145736 | tf_op jit(solution)/shard_map/ppermute | solution.py:138
  9.6 27.7 %collective-permute-start.19 = (bf16[512,1024]{1,0:T(8,128)(2,1)}, bf16[512,1024]{1,0:T(8,128)(2,1)S(1)}, u32[]{:S(2)}, u32[]{:S(2)}) collective-permute-start(bf16[512,1024]{1,0:T(8,128)(2,1)} %param.6), channel_id=1, source_target_pairs={{0,32},{16,48},{32,64},{48,80},{64,96},{80,112},{96,0},{112,16},{1... | collective-permute-start | bytes 3145736 | tf_op jit(solution)/shard_map/ppermute | solution.py:141
  10.9 29.9 %collective-permute-start.20 = (bf16[512,1024]{1,0:T(8,128)(2,1)}, bf16[512,1024]{1,0:T(8,128)(2,1)S(1)}, u32[]{:S(2)}, u32[]{:S(2)}) collective-permute-start(bf16[512,1024]{1,0:T(8,128)(2,1)} %param.6), channel_id=1, source_target_pairs={{0,96},{16,112},{32,0},{48,16},{64,32},{80,48},{96,64},{112,80},{1... | collective-permute-start | bytes 3145736 | tf_op jit(solution)/shard_map/ppermute | solution.py:142
  31.8 25.8 %collective-permute-start.23 = (bf16[512,1024]{1,0:T(8,128)(2,1)}, bf16[512,1024]{1,0:T(8,128)(2,1)S(1)}, u32[]{:S(2)}, u32[]{:S(2)}) collective-permute-start(bf16[512,1024]{1,0:T(8,128)(2,1)} %param.6), channel_id=1, source_target_pairs={{0,16},{16,0},{32,48},{48,32},{64,80},{80,64},{96,112},{112,96},{1... | collective-permute-start | bytes 3145736 | tf_op jit(solution)/shard_map/ppermute | solution.py:138
  34.6 41.6 %collective-permute-start.2 = (bf16[2,1024,256]{2,1,0:T(8,128)(2,1)S(1)}, bf16[2,1024,256]{2,1,0:T(8,128)(2,1)}, u32[]{:S(2)}, u32[]{:S(2)}) collective-permute-start(bf16[2,1024,256]{2,1,0:T(8,128)(2,1)S(1)} %collective-permute-done.1), channel_id=1, source_target_pairs={{0,1},{1,0},{2,3},{3,2},{4,5},{5,4},{6,7},{7,6},{8,9},{9,8},{10,11... | collective-permute-start | bytes 3145736 | tf_op jit(solution)/shard_map/ppermute | solution.py:168
  37.3 5.7 %copy-start.15 = (bf16[2,1024,256]{2,1,0:T(8,128)(2,1)}, bf16[2,1024,256]{2,1,0:T(8,128)(2,1)S(1)}, u32[]{:S(2)}) copy-start(bf16[2,1024,256]{2,1,0:T(8,128)(2,1)S(1)} %collective-permute-done.9) | copy-start | bytes 3145732
  37.3 26.1 %collective-permute-start.5 = (bf16[2,512,256]{2,1,0:T(8,128)(2,1)}, bf16[2,512,256]{2,1,0:T(8,128)(2,1)}, u32[]{:S(2)}, u32[]{:S(2)}) collective-permute-start(bf16[2,512,256]{2,1,0:T(8,128)(2,1)} %slice.32), channel_id=1, source_target_pairs={{0,4},{1,5},{2,6},{3,7},{4,8},{5,9},{6,10},{7,11},{8,12},{9,13},{1... | collective-permute-start | bytes 1572872 | tf_op jit(solution)/shard_map/ppermute | solution.py:143
  37.3 2.7 copy-start.10
  37.3 26.2 %collective-permute-start.7 = (bf16[2,512,256]{2,1,0:T(8,128)(2,1)}, bf16[2,512,256]{2,1,0:T(8,128)(2,1)}, u32[]{:S(2)}, u32[]{:S(2)}) collective-permute-start(bf16[2,512,256]{2,1,0:T(8,128)(2,1)} %slice.33), channel_id=1, source_target_pairs={{0,12},{1,13},{2,14},{3,15},{4,0},{5,1},{6,2},{7,3},{8,4},{9,5},{1... | collective-permute-start | bytes 1572872 | tf_op jit(solution)/shard_map/ppermute | solution.py:144
  40.8 1.3 copy-start.12
  40.8 30.7 %collective-permute-start.21 = (bf16[256,1024]{1,0:T(8,128)(2,1)}, bf16[256,1024]{1,0:T(8,128)(2,1)}, u32[]{:S(2)}, u32[]{:S(2)}) collective-permute-start(bf16[256,1024]{1,0:T(8,128)(2,1)} %slice.36), channel_id=1, source_target_pairs={{0,32},{16,48},{32,64},{48,80},{64,96},{80,112},{96,0},{112,16},{1... | collective-permute-start | bytes 1572872 | tf_op jit(solution)/shard_map/ppermute | solution.py:143
  57.6 1.0 copy-start.17
  58.6 15.3 %collective-permute-start.22 = (bf16[256,1024]{1,0:T(8,128)(2,1)}, bf16[256,1024]{1,0:T(8,128)(2,1)}, u32[]{:S(2)}, u32[]{:S(2)}) collective-permute-start(bf16[256,1024]{1,0:T(8,128)(2,1)} %slice.37), channel_id=1, source_target_pairs={{0,96},{16,112},{32,0},{48,16},{64,32},{80,48},{96,64},{112,80},{1... | collective-permute-start | bytes 1572872 | tf_op jit(solution)/shard_map/ppermute | solution.py:144
  61.3 2.1 copy-start.16
  61.3 10.0 %copy-start.14 = (bf16[512,1024]{1,0:T(8,128)(2,1)S(1)}, bf16[512,1024]{1,0:T(8,128)(2,1)}, u32[]{:S(2)}) copy-start(bf16[512,1024]{1,0:T(8,128)(2,1)} %param.6) | copy-start | bytes 3145732
  61.3 10.1 %copy-start.18 = (bf16[512,1024]{1,0:T(8,128)(2,1)S(1)}, bf16[512,1024]{1,0:T(8,128)(2,1)}, u32[]{:S(2)}) copy-start(bf16[512,1024]{1,0:T(8,128)(2,1)} %copy-done.17) | copy-start | bytes 3145732
  61.3 18.9 %copy-start.11 = (bf16[512,1024]{1,0:T(8,128)(2,1)S(1)}, bf16[512,1024]{1,0:T(8,128)(2,1)}, u32[]{:S(2)}) copy-start(bf16[512,1024]{1,0:T(8,128)(2,1)} %copy-done.10) | copy-start | bytes 3145732
  61.3 19.0 %copy-start.13 = (bf16[512,1024]{1,0:T(8,128)(2,1)S(1)}, bf16[512,1024]{1,0:T(8,128)(2,1)}, u32[]{:S(2)}) copy-start(bf16[512,1024]{1,0:T(8,128)(2,1)} %copy-done.12) | copy-start | bytes 3145732
  63.4 5.8 %copy-start.9 = (bf16[2,1024,4096]{2,1,0:T(8,128)(2,1)}, bf16[2,1024,4096]{2,1,0:T(8,128)(2,1)S(1)}, u32[]{:S(2)}) copy-start(bf16[2,1024,4096]{2,1,0:T(8,128)(2,1)S(1)} %constant_dynamic-update-slice_fusion.29) | copy-start | bytes 50331652
  63.4 24.1 %collective-permute-start.11 = (bf16[2,1024,256]{2,1,0:T(8,128)(2,1)S(1)}, bf16[2,1024,256]{2,1,0:T(8,128)(2,1)S(1)}, u32[]{:S(2)}, u32[]{:S(2)}) collective-permute-start(bf16[2,1024,256]{2,1,0:T(8,128)(2,1)S(1)} %copy-done.16), channel_id=1, source_target_pairs={{0,4},{1,5},{2,6},{3,7},{4,8},{5,9},{6,10},{7,11},{8,12},{9,13},{1... | collective-permute-start | bytes 3145736 | tf_op jit(solution)/shard_map/ppermute | solution.py:141
  69.2 22.8 %collective-permute-start.13 = (bf16[2,1024,256]{2,1,0:T(8,128)(2,1)S(1)}, bf16[2,1024,256]{2,1,0:T(8,128)(2,1)S(1)}, u32[]{:S(2)}, u32[]{:S(2)}) collective-permute-start(bf16[2,1024,256]{2,1,0:T(8,128)(2,1)S(1)} %copy-done.16), channel_id=1, source_target_pairs={{0,12},{1,13},{2,14},{3,15},{4,0},{5,1},{6,2},{7,3},{8,4},{9,5},{1... | collective-permute-start | bytes 3145736 | tf_op jit(solution)/shard_map/ppermute | solution.py:142
  71.5 25.7 %collective-permute-start.24 = (bf16[512,1024]{1,0:T(8,128)(2,1)S(1)}, bf16[512,1024]{1,0:T(8,128)(2,1)S(1)}, u32[]{:S(2)}, u32[]{:S(2)}) collective-permute-start(bf16[512,1024]{1,0:T(8,128)(2,1)S(1)} %copy-done.18), channel_id=1, source_target_pairs={{0,32},{16,48},{32,64},{48,80},{64,96},{80,112},{96,0},{112,16},{1... | collective-permute-start | bytes 3145736 | tf_op jit(solution)/shard_map/ppermute | solution.py:141
  73.9 28.0 %collective-permute-start.4 = (bf16[2,1024,256]{2,1,0:T(8,128)(2,1)S(1)}, bf16[2,1024,256]{2,1,0:T(8,128)(2,1)S(1)}, u32[]{:S(2)}, u32[]{:S(2)}) collective-permute-start(bf16[2,1024,256]{2,1,0:T(8,128)(2,1)S(1)} %collective-permute-done.3), channel_id=1, source_target_pairs={{0,1},{1,0},{2,3},{3,2},{4,5},{5,4},{6,7},{7,6},{8,9},{9,8},{10,11... | collective-permute-start | bytes 3145736 | tf_op jit(solution)/shard_map/ppermute | solution.py:168
  76.2 25.4 %collective-permute-start.25 = (bf16[512,1024]{1,0:T(8,128)(2,1)S(1)}, bf16[512,1024]{1,0:T(8,128)(2,1)S(1)}, u32[]{:S(2)}, u32[]{:S(2)}) collective-permute-start(bf16[512,1024]{1,0:T(8,128)(2,1)S(1)} %copy-done.18), channel_id=1, source_target_pairs={{0,96},{16,112},{32,0},{48,16},{64,32},{80,48},{96,64},{112,80},{1... | collective-permute-start | bytes 3145736 | tf_op jit(solution)/shard_map/ppermute | solution.py:142
  87.6 26.1 %collective-permute-start.10 = (bf16[2,1024,256]{2,1,0:T(8,128)(2,1)S(1)}, bf16[2,1024,256]{2,1,0:T(8,128)(2,1)S(1)}, u32[]{:S(2)}, u32[]{:S(2)}) collective-permute-start(bf16[2,1024,256]{2,1,0:T(8,128)(2,1)S(1)} %copy-done.16), channel_id=1, source_target_pairs={{0,1},{1,0},{2,3},{3,2},{4,5},{5,4},{6,7},{7,6},{8,9},{9,8},{10,11... | collective-permute-start | bytes 3145736 | tf_op jit(solution)/shard_map/ppermute | solution.py:168
  92.0 15.5 %collective-permute-start.6 = (bf16[2,512,256]{2,1,0:T(8,128)(2,1)}, bf16[2,512,256]{2,1,0:T(8,128)(2,1)S(1)}, u32[]{:S(2)}, u32[]{:S(2)}) collective-permute-start(bf16[2,512,256]{2,1,0:T(8,128)(2,1)} %collective-permute-done.5), channel_id=1, source_target_pairs={{0,1},{1,0},{2,3},{3,2},{4,5},{5,4},{6,7},{7,6},{8,9},{9,8},{10,11... | collective-permute-start | bytes 1572872 | tf_op jit(solution)/shard_map/ppermute | solution.py:168
  97.1 13.2 %collective-permute-start.8 = (bf16[2,512,256]{2,1,0:T(8,128)(2,1)}, bf16[2,512,256]{2,1,0:T(8,128)(2,1)S(1)}, u32[]{:S(2)}, u32[]{:S(2)}) collective-permute-start(bf16[2,512,256]{2,1,0:T(8,128)(2,1)} %collective-permute-done.7), channel_id=1, source_target_pairs={{0,1},{1,0},{2,3},{3,2},{4,5},{5,4},{6,7},{7,6},{8,9},{9,8},{10,11... | collective-permute-start | bytes 1572872 | tf_op jit(solution)/shard_map/ppermute | solution.py:168
  101.6 13.8 %collective-permute-start.15 = (bf16[2,512,256]{2,1,0:T(8,128)(2,1)S(1)}, bf16[2,512,256]{2,1,0:T(8,128)(2,1)S(1)}, u32[]{:S(2)}, u32[]{:S(2)}) collective-permute-start(bf16[2,512,256]{2,1,0:T(8,128)(2,1)S(1)} %slice.34), channel_id=1, source_target_pairs={{0,4},{1,5},{2,6},{3,7},{4,8},{5,9},{6,10},{7,11},{8,12},{9,13},{1... | collective-permute-start | bytes 1572872 | tf_op jit(solution)/shard_map/ppermute | solution.py:143
  101.9 18.4 %collective-permute-start.17 = (bf16[2,512,256]{2,1,0:T(8,128)(2,1)S(1)}, bf16[2,512,256]{2,1,0:T(8,128)(2,1)S(1)}, u32[]{:S(2)}, u32[]{:S(2)}) collective-permute-start(bf16[2,512,256]{2,1,0:T(8,128)(2,1)S(1)} %slice.35), channel_id=1, source_target_pairs={{0,12},{1,13},{2,14},{3,15},{4,0},{5,1},{6,2},{7,3},{8,4},{9,5},{1... | collective-permute-start | bytes 1572872 | tf_op jit(solution)/shard_map/ppermute | solution.py:144
  107.5 14.8 %collective-permute-start.26 = (bf16[256,1024]{1,0:T(8,128)(2,1)S(1)}, bf16[256,1024]{1,0:T(8,128)(2,1)S(1)}, u32[]{:S(2)}, u32[]{:S(2)}) collective-permute-start(bf16[256,1024]{1,0:T(8,128)(2,1)S(1)} %slice.38), channel_id=1, source_target_pairs={{0,32},{16,48},{32,64},{48,80},{64,96},{80,112},{96,0},{112,16},{1... | collective-permute-start | bytes 1572872 | tf_op jit(solution)/shard_map/ppermute | solution.py:143
  110.3 18.0 %collective-permute-start.12 = (bf16[2,1024,256]{2,1,0:T(8,128)(2,1)S(1)}, bf16[2,1024,256]{2,1,0:T(8,128)(2,1)S(1)}, u32[]{:S(2)}, u32[]{:S(2)}) collective-permute-start(bf16[2,1024,256]{2,1,0:T(8,128)(2,1)S(1)} %collective-permute-done.11), channel_id=1, source_target_pairs={{0,1},{1,0},{2,3},{3,2},{4,5},{5,4},{6,7},{7,6},{8,9},{9,8},{10,11... | collective-permute-start | bytes 3145736 | tf_op jit(solution)/shard_map/ppermute | solution.py:168
  113.7 17.5 %collective-permute-start.14 = (bf16[2,1024,256]{2,1,0:T(8,128)(2,1)S(1)}, bf16[2,1024,256]{2,1,0:T(8,128)(2,1)S(1)}, u32[]{:S(2)}, u32[]{:S(2)}) collective-permute-start(bf16[2,1024,256]{2,1,0:T(8,128)(2,1)S(1)} %collective-permute-done.13), channel_id=1, source_target_pairs={{0,1},{1,0},{2,3},{3,2},{4,5},{5,4},{6,7},{7,6},{8,9},{9,8},{10,11... | collective-permute-start | bytes 3145736 | tf_op jit(solution)/shard_map/ppermute | solution.py:168
  115.4 12.9 %collective-permute-start.27 = (bf16[256,1024]{1,0:T(8,128)(2,1)S(1)}, bf16[256,1024]{1,0:T(8,128)(2,1)S(1)}, u32[]{:S(2)}, u32[]{:S(2)}) collective-permute-start(bf16[256,1024]{1,0:T(8,128)(2,1)S(1)} %slice.39), channel_id=1, source_target_pairs={{0,96},{16,112},{32,0},{48,16},{64,32},{80,48},{96,64},{112,80},{1... | collective-permute-start | bytes 1572872 | tf_op jit(solution)/shard_map/ppermute | solution.py:144
  120.2 13.3 %collective-permute-start.16 = (bf16[2,512,256]{2,1,0:T(8,128)(2,1)S(1)}, bf16[2,512,256]{2,1,0:T(8,128)(2,1)S(1)}, u32[]{:S(2)}, u32[]{:S(2)}) collective-permute-start(bf16[2,512,256]{2,1,0:T(8,128)(2,1)S(1)} %collective-permute-done.15), channel_id=1, source_target_pairs={{0,1},{1,0},{2,3},{3,2},{4,5},{5,4},{6,7},{7,6},{8,9},{9,8},{10,11... | collective-permute-start | bytes 1572872 | tf_op jit(solution)/shard_map/ppermute | solution.py:168
  122.3 13.0 %collective-permute-start.18 = (bf16[2,512,256]{2,1,0:T(8,128)(2,1)S(1)}, bf16[2,512,256]{2,1,0:T(8,128)(2,1)S(1)}, u32[]{:S(2)}, u32[]{:S(2)}) collective-permute-start(bf16[2,512,256]{2,1,0:T(8,128)(2,1)S(1)} %collective-permute-done.17), channel_id=1, source_target_pairs={{0,1},{1,0},{2,3},{3,2},{4,5},{5,4},{6,7},{7,6},{8,9},{9,8},{10,11... | collective-permute-start | bytes 1572872 | tf_op jit(solution)/shard_map/ppermute | solution.py:168
  128.3 7.9 %copy-start.4 = (bf16[4096,1024]{1,0:T(8,128)(2,1)}, bf16[4096,1024]{1,0:T(8,128)(2,1)S(1)}, u32[]{:S(2)}) copy-start(bf16[4096,1024]{1,0:T(8,128)(2,1)S(1)} %constant_dynamic-update-slice_fusion.b_ref) | copy-start | bytes 25165828
  149.9 1.3 copy-start.6
  151.2 33.4 %all-to-all-start.1 = ((bf16[16,8,64,128]{3,2,1,0:T(8,128)(2,1)}), bf16[16,8,64,128]{3,2,1,0:T(8,128)(2,1)S(1)}, u32[]{:S(2)}, u32[]{:S(2)}) async-start(bf16[16,8,64,128]{3,2,1,0:T(8,128)(2,1)} %copy-done.6), calls=%async_computation.1 | async-start | bytes 4194304 | tf_op jit(solution)/shard_map/all_to_all | solution.py:176
  157.5 3.4 %copy-start.5 = (bf16[4096,1024]{1,0:T(8,128)(2,1)S(1)}, bf16[4096,1024]{1,0:T(8,128)(2,1)}, u32[]{:S(2)}) copy-start(bf16[4096,1024]{1,0:T(8,128)(2,1)} %copy-done.4) | copy-start | bytes 25165828
  160.8 100.0 %copy-start.19 = (f32[4096]{0:T(1024)S(1)}, f32[4096]{0:T(1024)}, u32[]{:S(2)}) copy-start(f32[4096]{0:T(1024)} %param.9) | copy-start | bytes 49156
  160.9 100.0 %copy-start.20 = (f32[4]{0:T(128)S(1)}, f32[4]{0:T(128)}, u32[]{:S(2)}) copy-start(f32[4]{0:T(128)} %param.8) | copy-start | bytes 52
  160.9 145.1 %copy-start.1 = (s32[64,32]{0,1:T(8,128)S(1)}, s32[64,32]{0,1:T(8,128)}, u32[]{:S(2)}) copy-start(s32[64,32]{0,1:T(8,128)} %param.7) | copy-start | bytes 24580
  174.5 1.3 copy-start.7
  255.2 35.7 %all-to-all-start.2 = ((bf16[128,64,128]{2,1,0:T(8,128)(2,1)}), bf16[128,64,128]{2,1,0:T(8,128)(2,1)}, u32[]{:S(2)}, u32[]{:S(2)}) async-start(bf16[128,64,128]{2,1,0:T(8,128)(2,1)} %bitcast.13), calls=%async_computation.2 | async-start | bytes 4194304 | tf_op jit(solution)/shard_map/all_to_all | solution.py:179
  290.9 1.6 copy-start.2
  292.5 1.6 copy-start.3

commit v2 on v1

v2 whole, which is shorter than its diff:
```python
import functools

import jax
import jax.numpy as jnp
from jax import lax
from jax.experimental import pallas as pl
from jax.experimental.pallas import tpu as pltpu
from jax.sharding import PartitionSpec as P

TILE = 64
CHUNKS = 1
BF = jnp.bfloat16
F32 = jnp.float32


def col_pairs(move):
    pairs = []
    for z in range(4):
        for x in range(2):
            for k in range(2):
                a, b, c = move(z, x, k)
                pairs.append((z * 4 + x * 2 + k, (a % 4) * 4 + (b % 2) * 2 + c % 2))
    return pairs


def row_pairs(move):
    pairs = []
    for y in range(4):
        for x in range(2):
            a, b = move(y, x)
            pairs.append((y * 2 + x, (a % 4) * 2 + b % 2))
    return pairs


Z_UP = col_pairs(lambda z, x, k: (z + 1, x, k))
Z_DOWN = col_pairs(lambda z, x, k: (z - 1, x, k))
X_SWAP = col_pairs(lambda z, x, k: (z, x + 1, k))
CORE_SWAP = col_pairs(lambda z, x, k: (z, x, k + 1))
Y_UP = row_pairs(lambda y, x: (y + 1, x))
Y_DOWN = row_pairs(lambda y, x: (y - 1, x))
XH_SWAP = row_pairs(lambda y, x: (y, x + 1))


def prep_kernel(mask_ref, a_ref, out_ref):
    depth, width = a_ref.shape
    lane = lax.broadcasted_iota(jnp.int32, (TILE, 128), 1)
    half = width // 256
    for block in range(width // 128):
        pieces = []
        for t in range(depth // TILE):
            low = mask_ref[t, block * 2]
            high = mask_ref[t, block * 2 + 1]
            keep = jnp.where(lane < TILE, low, high).astype(F32)
            values = a_ref[t * TILE : (t + 1) * TILE, block * 128 : (block + 1) * 128].astype(F32)
            pieces.append(values * keep)
        row = (block % half) * 128
        out_ref[block // half, row : row + 128, :] = jnp.concatenate(pieces, axis=0).T.astype(BF)


def prep(mask, a):
    depth, width = a.shape
    return pl.pallas_call(
        prep_kernel,
        out_shape=jax.ShapeDtypeStruct((2, width // 2, depth), BF),
        in_specs=[pl.BlockSpec(memory_space=pltpu.SMEM), pl.BlockSpec(memory_space=pltpu.VMEM)],
        out_specs=pl.BlockSpec(memory_space=pltpu.VMEM),
        compiler_params=pltpu.CompilerParams(vmem_limit_bytes=16 * 2**20),
    )(mask, a)


def product_kernel(j, h, taken, *refs):
    a_refs, b_refs = refs[:8], refs[8:16]
    out_ref, a_buf, b_buf, total, taken_buf, out_buf, a_sem, b_sem, t_sem, o_sem = refs[-10:]
    depth, group, wide = 256, 2, 512
    cols = total.shape[1]
    base = 8 * j if taken else 0
    row_place, col_place = lax.axis_index("row"), lax.axis_index("col")
    z, xl = col_place // 4, (col_place // 2) % 2
    y, xh = row_place // 2, row_place % 2

    def a_copy(t):
        at = j if a_refs[t].shape[0] == 2 else 0
        return pltpu.make_async_copy(a_refs[t].at[at], a_buf.at[:, pl.ds(t * depth, depth)], a_sem.at[t])

    def b_copy(src, spot):
        return pltpu.make_async_copy(src, b_buf.at[spot], b_sem.at[spot])

    for t in range(8):
        a_copy(t).start()
        side, offset = t // 4, (0, -1, 1, 2)[t % 4]
        apart = (y + offset - z + 8) % 4
        slot = jnp.where(apart == 1, 2, jnp.where(apart == 2, 3, jnp.where(apart == 3, 1, 0)))
        place = ((xh + xl + side) % 2) * 4 + slot
        b_copy(b_refs[t].at[h if b_refs[t].shape[0] == 2 else 0], place).start()
    if taken:
        pltpu.make_async_copy(refs[16], taken_buf, t_sem).start()
    for t in range(0, 8, group):
        for u in range(t, t + group):
            a_copy(u).wait()
            b_copy(b_refs[0].at[0], u).wait()
        last = t + group == 8
        if last and taken:
            pltpu.make_async_copy(refs[16], taken_buf, t_sem).wait()
        for n in range(cols // wide):
            span = slice(n * wide, (n + 1) * wide)
            deep = b_buf[t : t + group, :, span].reshape(group * depth, wide)
            part = jnp.dot(a_buf[:, t * depth : (t + group) * depth], deep, preferred_element_type=F32)
            if t > 0:
                part = part + total[:, span]
            if not last:
                total[:, span] = part
                continue
            for e in range(wide // 128):
                k = n * (wide // 128) + e
                for g in range(8):
                    piece = part[g * 128 : (g + 1) * 128, e * 128 : (e + 1) * 128]
                    if taken:
                        piece = piece + taken_buf[g, k].astype(F32)
                    out_buf[k, g] = piece.astype(BF)
                pltpu.make_async_copy(out_buf.at[k], out_ref.at[pl.ds(base, 8), k], o_sem.at[k]).start()
    for k in range(cols // 128):
        pltpu.make_async_copy(out_buf.at[k], out_ref.at[pl.ds(base, 8), k], o_sem.at[k]).wait()


def product(a_shards, b_shards, j, h, taken=None, begun=None, also=()):
    rows, depth, cols = 1024, 2048, 1024
    extra = [x for x in (taken, begun) if x is not None] + list(also)
    return pl.pallas_call(
        functools.partial(product_kernel, j, h, taken is not None),
        in_specs=[pl.BlockSpec(memory_space=pl.ANY)] * (16 + len(extra)),
        out_specs=pl.BlockSpec(memory_space=pl.ANY),
        out_shape=jax.ShapeDtypeStruct((8 if taken is None else 16, 8, 128, 128), BF),
        scratch_shapes=[
            pltpu.VMEM((rows, depth), BF),
            pltpu.VMEM((8, 256, cols), BF),
            pltpu.VMEM((rows, cols), F32),
            pltpu.VMEM((8, 8, 128, 128), BF),
            pltpu.VMEM((8, 8, 128, 128), BF),
            pltpu.SemaphoreType.DMA((8,)),
            pltpu.SemaphoreType.DMA((8,)),
            pltpu.SemaphoreType.DMA,
            pltpu.SemaphoreType.DMA((8,)),
        ],
        input_output_aliases={} if begun is None else {17: 0},
        compiler_params=pltpu.CompilerParams(vmem_limit_bytes=60 * 2**20),
        cost_estimate=pl.CostEstimate(
            flops=2 * rows * depth * cols, bytes_accessed=2 * depth * (rows + cols) + 2 * rows * cols, transcendentals=0
        ),
    )(*a_shards, *b_shards, *extra)


def finish_kernel(row_gap_ref, gap_ref, *refs):
    directs, mirrors, out_ref = refs[:CHUNKS], refs[CHUNKS : 2 * CHUNKS], refs[-1]
    eye = (
        lax.broadcasted_iota(jnp.int32, (128, 128), 0) == lax.broadcasted_iota(jnp.int32, (128, 128), 1)
    ).astype(BF)
    row_gap = row_gap_ref[...]
    for e in range(directs[0].shape[0]):
        direct = jnp.concatenate([ref[e] for ref in directs], axis=0).astype(F32)
        mirror = jnp.concatenate([ref[e] for ref in mirrors], axis=0)
        flipped = lax.dot_general(eye, mirror, (((1,), (1,)), ((), ())), preferred_element_type=F32)
        span = slice(e * 128, (e + 1) * 128)
        out_ref[:, span] = ((direct + flipped) / (row_gap + gap_ref[:, span])).astype(BF)


def finish(row_gap, gap, directs, mirrors):
    count, part, lanes = directs[0].shape
    rows = part * CHUNKS
    step = 16
    piece = pl.BlockSpec((step, part, lanes), lambda n: (n, 0, 0))
    return pl.pallas_call(
        finish_kernel,
        grid=(count // step,),
        out_shape=jax.ShapeDtypeStruct((rows, count * lanes), BF),
        in_specs=[
            pl.BlockSpec((rows, 1), lambda n: (0, 0)),
            pl.BlockSpec((1, step * lanes), lambda n: (0, n)),
        ]
        + [piece] * (2 * CHUNKS),
        out_specs=pl.BlockSpec((rows, step * lanes), lambda n: (0, n)),
        compiler_params=pltpu.CompilerParams(vmem_limit_bytes=56 * 2**20),
    )(row_gap.reshape(rows, 1), gap.reshape(1, count * lanes), *directs, *mirrors)


def gate(values, others):
    def body(*refs):
        del refs

    return pl.pallas_call(
        body,
        out_shape=[jax.ShapeDtypeStruct(x.shape, x.dtype) for x in values],
        in_specs=[pl.BlockSpec(memory_space=pl.ANY)] * (len(values) + len(others)),
        out_specs=[pl.BlockSpec(memory_space=pl.ANY)] * len(values),
        input_output_aliases={i: i for i in range(len(values))},
    )(*values, *others)


def local(amplitudes, integrals, tile_mask, occ_energy, virt_energy):
    row_place = lax.axis_index("row")
    col_place = lax.axis_index("col")
    tile_rows = amplitudes.shape[0] // TILE
    move = lambda block, pairs: lax.ppermute(block, "col" if len(pairs) == 16 else "row", pairs)

    core = col_place % 2
    kept = lax.dynamic_slice_in_dim(integrals, core * 256, 256, 0)
    passed = lax.dynamic_slice_in_dim(integrals, (1 - core) * 256, 256, 0)
    b_own = jnp.stack([kept, move(passed, CORE_SWAP)])
    own_mask = lax.dynamic_slice_in_dim(tile_mask, col_place * tile_rows, tile_rows, 0)
    a_own = prep(own_mask, amplitudes)

    a_far = move(a_own, X_SWAP)
    a_below, a_above = move(a_own, Z_UP), move(a_own, Z_DOWN)
    b_below, b_above = move(b_own, Y_UP), move(b_own, Y_DOWN)
    b_first, b_second = move(b_below[:1], Y_UP), move(b_above[1:], Y_DOWN)
    far_below, far_above = move(a_far, Z_UP), move(a_far, Z_DOWN)
    b_far = move(b_own, XH_SWAP)
    b_far_below, b_far_above = move(b_far, Y_UP), move(b_far, Y_DOWN)
    a_below, a_above, far_below, far_above = gate((a_below, a_above, far_below, far_above), (b_far,))
    a_first, a_second = move(a_below[:1], Z_UP), move(a_above[1:], Z_DOWN)
    b_far_first, b_far_second = move(b_first, XH_SWAP), move(b_second, XH_SWAP)
    far_first, far_second = move(far_above[:1], Z_DOWN), move(far_below[1:], Z_UP)
    a_of = lambda j: [
        a_own, a_below, a_above, (a_first, a_second)[j], a_far, far_below, far_above, (far_first, far_second)[j],
    ]
    b_of = lambda h: [
        b_own, b_below, b_above, (b_first, b_second)[h], b_far, b_far_below, b_far_above, (b_far_first, b_far_second)[h],
    ]
    taken = [move(product(a_of(0), b_of(1), 0, 1, also=(b_first,)), CORE_SWAP)]
    taken.append(move(product(a_of(1), b_of(1), 1, 1, also=(b_far_first,)), CORE_SWAP))
    made = product(a_of(0), b_of(0), 0, 0, taken[0])
    made = product(a_of(1), b_of(0), 1, 0, taken[1], made)
    direct = lax.all_to_all(made, "col", split_axis=0, concat_axis=0, tiled=True).reshape(128, 128, 128)
    mirror = lax.all_to_all(direct, ("row", "col"), split_axis=0, concat_axis=0, tiled=True)

    gap = (virt_energy[None, :] - occ_energy[:, None]).reshape(-1)
    flat_place = row_place * 16 + col_place
    row_gap = lax.dynamic_slice_in_dim(gap, flat_place * 128, 128, 0)
    return finish(row_gap, gap, [direct], [mirror])


def solution(mesh):
    return jax.shard_map(
        local,
        mesh=mesh,
        in_specs=(P("col", "row"), P("row", "col"), P(None, "row"), P(), P()),
        out_specs=P(("row", "col"), None),
        check_vma=False,
    )
```

time: 307 us -> 252 us (0.82)
  local copies, waits for them, and re-layouts: 52.6 us -> 14.1 us
  starting transfers between devices: 55.8 us -> 40.7 us
  blocking collectives: 70.5 us -> 60.1 us
  waiting for transfers between devices: 86.4 us -> 93 us
    all_to_all x1 -> x0, blocking collectives: 38.6 us -> none  [local(): lax.all_to_all(direct, ('row', 'col'), split_axis=0, concat_axis=0, tiled...]
    all_to_all x1, blocking collectives: 31.9 us -> 60.1 us  [local(): lax.all_to_all(made, 'col', split_axis=0, concat_axis=0, tiled=True)]
    dynamic_update_slice x30 -> x0, local copies, waits for them, and re-layouts: 27.8 us -> none  [the longest x20 24.9 us: local(): a_full = lax.dynamic_update_slice(a_full, piece, (0, start, place * 256))]
    all_to_all x1, waiting for transfers between devices: 29.7 us -> 50.8 us  [local(): lax.all_to_all(direct, ('row', 'col'), split_axis=0, concat_axis=0, tiled...]
    unnamed x45 -> x39, local copies, waits for them, and re-layouts: 18 us -> 5.18 us
    ppermute x28 -> x21, starting transfers between devices: 43.9 us -> 33.6 us  [local(): lax.ppermute(block, 'col' if len(pairs) == 16 else 'row', pairs)]
    all_to_all x1 -> x0, waiting for transfers between devices: 8.82 us -> none  [local(): lax.all_to_all(made, 'col', split_axis=0, concat_axis=0, tiled=True)]
    all_to_all x1 -> x0, starting transfers between devices: 6.22 us -> none  [local(): lax.all_to_all(made, 'col', split_axis=0, concat_axis=0, tiled=True)]
  transfers between devices with their start and end apart: 30 -> 22, of which waited for: 9 -> 9; matrix products, arithmetic and copies ran while one was open for 11% -> 3% of each run, Pallas kernels for 4% -> 10%
where the time goes in v2:
time: 252 us; the launch traced here: 251 us
  waiting for transfers between devices  93 us (37%)
  blocking collectives  60.1 us (24%)
  Pallas kernels  42.8 us (17%)
  starting transfers between devices  40.7 us (16%)
  local copies, waits for them, and re-layouts  14.1 us (6%)
    all_to_all x1, blocking collectives, local(): lax.all_to_all(made, 'col', split_axis=0, concat_axis=0, tiled=True)  60.1 us
    all_to_all x1, waiting for transfers between devices, local(): lax.all_to_all(direct, ('row', 'col'), split_axis=0, concat_axis=0, tiled...  50.8 us
    ppermute x21, waiting for transfers between devices, local(): lax.ppermute(block, 'col' if len(pairs) == 16 else 'row', pairs)  42.3 us
    ppermute x21, starting transfers between devices, local(): lax.ppermute(block, 'col' if len(pairs) == 16 else 'row', pairs)  33.6 us
    pallas_call x4, Pallas kernels, product(): pl.pallas_call(functools.partial(product_kernel, j, h, taken is not None)...  32.7 us
    pallas_call x1, Pallas kernels, finish(): pl.pallas_call(finish_kernel, grid=(count // step,), out_shape=jax.ShapeD...  9.17 us
    all_to_all x1, starting transfers between devices, local(): lax.all_to_all(direct, ('row', 'col'), split_axis=0, concat_axis=0, tiled...  7.13 us
    unnamed x39, local copies, waits for them, and re-layouts  5.18 us
  transfers between devices with their start and end apart: 22, of which 9 were waited for; matrix products, arithmetic and copies ran while one was open for 3% of the time, Pallas kernels for 10%

profile of v2, /device:TPU:1, one launch (start us, length us, event | category | flops | bytes accessed | tf_op | source)
XLA Modules:
  0.0 251.2 jit_solution(9630150170760096684)
XLA Ops:
  0.0 1.3 dynamic-slice_bitcast_fusion
  1.3 1.5 collective-permute-start.5
  2.8 0.1 constant_dynamic-slice_fusion.1
  2.9 0.1 copy.13.mask_ref
  2.9 1.2 copy-done.2
  4.2 0.9 shard_map.55.refs_0_
  5.1 1.4 collective-permute-start.2
  6.5 0.0 collective-permute-done.5
  6.5 0.1 pad_maximum_fusion.refs_8_
  6.6 2.8 %collective-permute-start.10 = (bf16[2,256,1024]{2,1,0:T(8,128)(2,1)S(1)}, bf16[2,256,1024]{2,1,0:T(8,128)(2,1)S(1)}, u32[]{:S(2)}, u32[]{:S(2)}) collective-permute-start(bf16[2,256,1024]{2,1,0:T(8,128)(2,1)S(1)} %pad_maximum_fusion.refs_8_), channel_id=1, source_target_pairs={{0,96},{16,112},{32,0},{48,16},{64,32},{80,48},{96,64},{112,80},{1... | collective-permute-start | bytes 3145736 | tf_op jit(solution)/shard_map/ppermute | solution.py:202
  9.4 0.0 collective-permute-start.9
  9.4 1.6 collective-permute-start
  11.1 2.1 collective-permute-start.1
  13.2 16.8 %collective-permute-done.2.refs_4_ = bf16[2,1024,256]{2,1,0:T(8,128)(2,1)S(1)} collective-permute-done((bf16[2,1024,256]{2,1,0:T(8,128)(2,1)S(1)}, bf16[2,1024,256]{2,1,0:T(8,128)(2,1)S(1)}, u32[]{:S(2)}, u32[]{:S(2)}) %collective-permute-start.2) | collective-permute-done | bytes 1048608 | tf_op jit(solution)/shard_map/ppermute | solution.py:202
  30.0 2.8 %collective-permute-start.6 = (bf16[2,256,1024]{2,1,0:T(8,128)(2,1)S(1)}, bf16[2,256,1024]{2,1,0:T(8,128)(2,1)}, u32[]{:S(2)}, u32[]{:S(2)}) collective-permute-start(bf16[2,256,1024]{2,1,0:T(8,128)(2,1)S(1)} %pad_maximum_fusion.refs_8_), channel_id=1, source_target_pairs={{0,16},{16,0},{32,48},{48,32},{64,80},{80,64},{96,112},{112,96},{1... | collective-permute-start | bytes 3145736 | tf_op jit(solution)/shard_map/ppermute | solution.py:202
  32.8 0.0 collective-permute-done.10.refs_10_
  32.8 1.6 collective-permute-start.3
  34.4 0.3 collective-permute-done.9.refs_9_
  34.8 3.8 %collective-permute-start.4 = (bf16[2,1024,256]{2,1,0:T(8,128)(2,1)S(1)}, bf16[2,1024,256]{2,1,0:T(8,128)(2,1)}, u32[]{:S(2)}, u32[]{:S(2)}) collective-permute-start(bf16[2,1024,256]{2,1,0:T(8,128)(2,1)S(1)} %collective-permute-done.2.refs_4_), channel_id=1, source_target_pairs={{0,12},{1,13},{2,14},{3,15},{4,0},{5,1},{6,2},{7,3},{8,4},{9,5},{1... | collective-permute-start | bytes 3145736 | tf_op jit(solution)/shard_map/ppermute | solution.py:202
  38.5 0.9 slice.25
  39.4 0.8 slice.24
  40.2 0.0 collective-permute-done.refs_0_
  40.2 0.9 collective-permute-start.15
  41.1 0.0 collective-permute-done.1.refs_1_
  41.1 0.7 collective-permute-start.11
  41.7 13.7 %collective-permute-done.6.refs_4_.refs_12_ = bf16[2,256,1024]{2,1,0:T(8,128)(2,1)} collective-permute-done((bf16[2,256,1024]{2,1,0:T(8,128)(2,1)S(1)}, bf16[2,256,1024]{2,1,0:T(8,128)(2,1)}, u32[]{:S(2)}, u32[]{:S(2)}) %collective-permute-start.6) | collective-permute-done | bytes 1048608 | tf_op jit(solution)/shard_map/ppermute | solution.py:202
  55.5 1.4 collective-permute-start.12
  56.8 2.2 collective-permute-done.3.refs_2_
  59.1 2.7 %collective-permute-start.13 = (bf16[2,256,1024]{2,1,0:T(8,128)(2,1)}, bf16[2,256,1024]{2,1,0:T(8,128)(2,1)}, u32[]{:S(2)}, u32[]{:S(2)}) collective-permute-start(bf16[2,256,1024]{2,1,0:T(8,128)(2,1)} %collective-permute-done.6.refs_4_.refs_12_), channel_id=1, source_target_pairs={{0,96},{16,112},{32,0},{48,16},{64,32},{80,48},{96,64},{112,80},{1... | collective-permute-start | bytes 3145736 | tf_op jit(solution)/shard_map/ppermute | solution.py:202
  61.8 0.0 collective-permute-done.4.refs_3_
  61.9 1.1 slice.22
  62.9 0.1 collective-permute-start.18
  63.0 1.1 slice.23
  64.1 2.7 %collective-permute-start.19 = (bf16[1,1024,256]{2,1,0:T(8,128)(2,1)S(1)}, bf16[1,1024,256]{2,1,0:T(8,128)(2,1)S(1)}, u32[]{:S(2)}, u32[]{:S(2)}) collective-permute-start(bf16[1,1024,256]{2,1,0:T(8,128)(2,1)S(1)} %slice.23), channel_id=1, source_target_pairs={{0,12},{1,13},{2,14},{3,15},{4,0},{5,1},{6,2},{7,3},{8,4},{9,5},{1... | collective-permute-start | bytes 1572872 | tf_op jit(solution)/shard_map/ppermute | solution.py:202
  66.8 0.0 collective-permute-done.11.refs_16_.refs_11_
  66.8 1.9 collective-permute-start.16
  68.8 1.9 slice.18
  70.6 1.1 slice.19
  71.7 4.1 %collective-permute-done.18.refs_3_ = bf16[1,1024,256]{2,1,0:T(8,128)(2,1)S(1)} collective-permute-done((bf16[1,1024,256]{2,1,0:T(8,128)(2,1)S(1)}, bf16[1,1024,256]{2,1,0:T(8,128)(2,1)S(1)}, u32[]{:S(2)}, u32[]{:S(2)}) %collective-permute-start.18) | collective-permute-done | bytes 524320 | tf_op jit(solution)/shard_map/ppermute | solution.py:202
  75.8 0.0 collective-permute-start.7
  75.8 0.0 collective-permute-done.19.refs_7_
  75.8 2.0 collective-permute-start.14
  77.8 1.6 collective-permute-done.16.refs_15_
  79.4 0.8 collective-permute-done.12.refs_13_
  80.2 2.7 %collective-permute-done.13.refs_14_ = bf16[2,256,1024]{2,1,0:T(8,128)(2,1)} collective-permute-done((bf16[2,256,1024]{2,1,0:T(8,128)(2,1)}, bf16[2,256,1024]{2,1,0:T(8,128)(2,1)}, u32[]{:S(2)}, u32[]{:S(2)}) %collective-permute-start.13) | collective-permute-done | bytes 1048608 | tf_op jit(solution)/shard_map/ppermute | solution.py:202
  82.9 8.0 %shard_map.58 = bf16[8,8,128,128]{3,2,1,0:T(8,128)(2,1)} custom-call(bf16[2,1024,256]{2,1,0:T(8,128)(2,1)} %copy-done.1, bf16[2,1024,256]{2,1,0:T(8,128)(2,1)} %get-tuple-element.9.refs_1_, bf16[2,1024,256]{2,1,0:T(8,128)(2,1)} %get-tuple-element.10.refs_2_, bf16[1,1024,256]{2,1,0:T(8,128)(2,1)} %copy-done.11, bf16[2,1024,256]{2,1,0:T(8,128)(2,1)} %copy-done.8, ...), custom_call_target="tpu_custom_call" | custom-call | flops 4294967296 | bytes 10485760 | tf_op jit(solution)/shard_map/pallas_call | solution.py:128
  91.0 3.2 %collective-permute-start.20 = (bf16[8,8,128,128]{3,2,1,0:T(8,128)(2,1)}, bf16[8,8,128,128]{3,2,1,0:T(8,128)(2,1)}, u32[]{:S(2)}, u32[]{:S(2)}) collective-permute-start(bf16[8,8,128,128]{3,2,1,0:T(8,128)(2,1)} %shard_map.58), channel_id=1, source_target_pairs={{0,1},{1,0},{2,3},{3,2},{4,5},{5,4},{6,7},{7,6},{8,9},{9,8},{10,11... | collective-permute-start | bytes 6291464 | tf_op jit(solution)/shard_map/ppermute | solution.py:202
  94.1 0.0 collective-permute-done.14.refs_16_.refs_15_
  94.2 0.8 copy-done.9
  95.0 0.2 copy-done.12
  95.2 0.8 copy-done.14
  95.9 8.0 %shard_map.57 = bf16[8,8,128,128]{3,2,1,0:T(8,128)(2,1)} custom-call(bf16[2,1024,256]{2,1,0:T(8,128)(2,1)} %copy-done.1, bf16[2,1024,256]{2,1,0:T(8,128)(2,1)} %get-tuple-element.9.refs_1_, bf16[2,1024,256]{2,1,0:T(8,128)(2,1)} %get-tuple-element.10.refs_2_, bf16[1,1024,256]{2,1,0:T(8,128)(2,1)} %copy-done.12, bf16[2,1024,256]{2,1,0:T(8,128)(2,1)} %copy-done.8, ...), custom_call_target="tpu_custom_call" | custom-call | flops 4294967296 | bytes 10485760 | tf_op jit(solution)/shard_map/pallas_call | solution.py:128
  104.0 0.4 collective-permute-start.17
  104.4 8.3 %shard_map.59.refs_17_ = bf16[16,8,128,128]{3,2,1,0:T(8,128)(2,1)} custom-call(bf16[2,1024,256]{2,1,0:T(8,128)(2,1)} %copy-done.1, bf16[2,1024,256]{2,1,0:T(8,128)(2,1)} %get-tuple-element.9.refs_1_, bf16[2,1024,256]{2,1,0:T(8,128)(2,1)} %get-tuple-element.10.refs_2_, bf16[1,1024,256]{2,1,0:T(8,128)(2,1)} %copy-done.11, bf16[2,1024,256]{2,1,0:T(8,128)(2,1)} %copy-done.8, ...), custom_call_target="tpu_custom_call" | custom-call | flops 4294967296 | bytes 10485760 | tf_op jit(solution)/shard_map/pallas_call | solution.py:128
  112.7 1.4 copy-done.10
  114.1 8.3 %shard_map.60 = bf16[16,8,128,128]{3,2,1,0:T(8,128)(2,1)} custom-call(bf16[2,1024,256]{2,1,0:T(8,128)(2,1)} %copy-done.1, bf16[2,1024,256]{2,1,0:T(8,128)(2,1)} %get-tuple-element.9.refs_1_, bf16[2,1024,256]{2,1,0:T(8,128)(2,1)} %get-tuple-element.10.refs_2_, bf16[1,1024,256]{2,1,0:T(8,128)(2,1)} %copy-done.12, ...), custom_call_target="tpu_custom_call", output_to_operand_aliasing={{}: (17, {})} | custom-call | flops 4294967296 | bytes 10485760 | tf_op jit(solution)/shard_map/pallas_call | solution.py:128
  122.4 60.1 %all_to_all.10 = bf16[16,8,128,128]{3,2,1,0:T(8,128)(2,1)} all-to-all(bf16[16,8,128,128]{3,2,1,0:T(8,128)(2,1)} %shard_map.60), channel_id=1, replica_groups=mesh['row'=8,'col'=16] {'col'}, dimensions={0} | all-to-all | bytes 8388608 | tf_op jit(solution)/shard_map/all_to_all | solution.py:232
  182.5 7.1 %all-to-all-start.1 = ((bf16[128,128,128]{2,1,0:T(8,128)(2,1)}), bf16[128,128,128]{2,1,0:T(8,128)(2,1)}, u32[]{:S(2)}, u32[]{:S(2)}) async-start(bf16[128,128,128]{2,1,0:T(8,128)(2,1)} %bitcast.13), calls=%async_computation.1 | async-start | bytes 8388608 | tf_op jit(solution)/shard_map/all_to_all | solution.py:233
  189.6 0.1 subtract_bitcast_fusion
  189.8 0.1 dynamic-slice_bitcast_fusion.1
  189.8 0.7 copy.12.row_gap_ref
  190.6 0.7 copy.15
  191.3 50.8 %all-to-all-done.1.refs_1_ = bf16[128,128,128]{2,1,0:T(8,128)(2,1)} async-done(((bf16[128,128,128]{2,1,0:T(8,128)(2,1)}), bf16[128,128,128]{2,1,0:T(8,128)(2,1)}, u32[]{:S(2)}, u32[]{:S(2)}) %all-to-all-start.1) | async-done | bytes 4194336 | tf_op jit(solution)/shard_map/all_to_all | solution.py:233
  242.0 9.2 %shard_map.61 = bf16[128,16384]{1,0:T(8,128)(2,1)} custom-call(f32[128,1]{1,0:T(8,128)} %copy.12.row_gap_ref, f32[1,16384]{1,0:T(1,128)} %bitcast.16, bf16[128,128,128]{2,1,0:T(8,128)(2,1)} %bitcast.14, bf16[128,128,128]{2,1,0:T(8,128)(2,1)} %all-to-all-done.1.refs_1_), custom_call_target="tpu_custom_call" | custom-call | tf_op jit(solution)/shard_map/pallas_call | solution.py:171
  (39 shorter events, 0.1 us)
Async XLA Ops:
  0.0 2.8 %copy-start = (s32[64,32]{0,1:T(8,128)S(1)}, s32[64,32]{0,1:T(8,128)}, u32[]{:S(2)}) copy-start(s32[64,32]{0,1:T(8,128)} %param.7) | copy-start | bytes 24580
  1.3 5.2 %collective-permute-start.5 = (bf16[256,1024]{1,0:T(8,128)(2,1)S(1)}, bf16[256,1024]{1,0:T(8,128)(2,1)S(1)}, u32[]{:S(2)}, u32[]{:S(2)}) collective-permute-start(bf16[256,1024]{1,0:T(8,128)(2,1)S(1)} %get-tuple-element.14), channel_id=1, source_target_pairs={{0,1},{1,0},{2,3},{3,2},{4,5},{5,4},{6,7},{7,6},{8,9},{9,8},{10,11... | collective-permute-start | bytes 1572872 | tf_op jit(solution)/shard_map/ppermute | solution.py:202
  2.9 1.2 copy-start.2
  5.1 56.7 %copy-start.1 = (bf16[2,1024,256]{2,1,0:T(8,128)(2,1)}, bf16[2,1024,256]{2,1,0:T(8,128)(2,1)S(1)}, u32[]{:S(2)}) copy-start(bf16[2,1024,256]{2,1,0:T(8,128)(2,1)S(1)} %shard_map.55.refs_0_) | copy-start | bytes 3145732
  5.1 24.8 %collective-permute-start.2 = (bf16[2,1024,256]{2,1,0:T(8,128)(2,1)S(1)}, bf16[2,1024,256]{2,1,0:T(8,128)(2,1)S(1)}, u32[]{:S(2)}, u32[]{:S(2)}) collective-permute-start(bf16[2,1024,256]{2,1,0:T(8,128)(2,1)S(1)} %shard_map.55.refs_0_), channel_id=1, source_target_pairs={{0,2},{1,3},{2,0},{3,1},{4,6},{5,7},{6,4},{7,5},{8,10},{9,11},{10,... | collective-permute-start | bytes 3145736 | tf_op jit(solution)/shard_map/ppermute | solution.py:202
  6.6 34.5 %copy-start.5 = (bf16[2,256,1024]{2,1,0:T(8,128)(2,1)}, bf16[2,256,1024]{2,1,0:T(8,128)(2,1)S(1)}, u32[]{:S(2)}) copy-start(bf16[2,256,1024]{2,1,0:T(8,128)(2,1)S(1)} %pad_maximum_fusion.refs_8_) | copy-start | bytes 3145732
  6.6 26.2 %collective-permute-start.10 = (bf16[2,256,1024]{2,1,0:T(8,128)(2,1)S(1)}, bf16[2,256,1024]{2,1,0:T(8,128)(2,1)S(1)}, u32[]{:S(2)}, u32[]{:S(2)}) collective-permute-start(bf16[2,256,1024]{2,1,0:T(8,128)(2,1)S(1)} %pad_maximum_fusion.refs_8_), channel_id=1, source_target_pairs={{0,96},{16,112},{32,0},{48,16},{64,32},{80,48},{96,64},{112,80},{1... | collective-permute-start | bytes 3145736 | tf_op jit(solution)/shard_map/ppermute | solution.py:202
  9.4 25.3 %collective-permute-start.9 = (bf16[2,256,1024]{2,1,0:T(8,128)(2,1)S(1)}, bf16[2,256,1024]{2,1,0:T(8,128)(2,1)S(1)}, u32[]{:S(2)}, u32[]{:S(2)}) collective-permute-start(bf16[2,256,1024]{2,1,0:T(8,128)(2,1)S(1)} %pad_maximum_fusion.refs_8_), channel_id=1, source_target_pairs={{0,32},{16,48},{32,64},{48,80},{64,96},{80,112},{96,0},{112,16},{1... | collective-permute-start | bytes 3145736 | tf_op jit(solution)/shard_map/ppermute | solution.py:202
  9.4 30.8 %collective-permute-start = (bf16[2,1024,256]{2,1,0:T(8,128)(2,1)S(1)}, bf16[2,1024,256]{2,1,0:T(8,128)(2,1)S(1)}, u32[]{:S(2)}, u32[]{:S(2)}) collective-permute-start(bf16[2,1024,256]{2,1,0:T(8,128)(2,1)S(1)} %shard_map.55.refs_0_), channel_id=1, source_target_pairs={{0,4},{1,5},{2,6},{3,7},{4,8},{5,9},{6,10},{7,11},{8,12},{9,13},{1... | collective-permute-start | bytes 3145736 | tf_op jit(solution)/shard_map/ppermute | solution.py:202
  11.1 30.0 %collective-permute-start.1 = (bf16[2,1024,256]{2,1,0:T(8,128)(2,1)S(1)}, bf16[2,1024,256]{2,1,0:T(8,128)(2,1)S(1)}, u32[]{:S(2)}, u32[]{:S(2)}) collective-permute-start(bf16[2,1024,256]{2,1,0:T(8,128)(2,1)S(1)} %shard_map.55.refs_0_), channel_id=1, source_target_pairs={{0,12},{1,13},{2,14},{3,15},{4,0},{5,1},{6,2},{7,3},{8,4},{9,5},{1... | collective-permute-start | bytes 3145736 | tf_op jit(solution)/shard_map/ppermute | solution.py:202
  30.0 29.1 %copy-start.8 = (bf16[2,1024,256]{2,1,0:T(8,128)(2,1)}, bf16[2,1024,256]{2,1,0:T(8,128)(2,1)S(1)}, u32[]{:S(2)}) copy-start(bf16[2,1024,256]{2,1,0:T(8,128)(2,1)S(1)} %collective-permute-done.2.refs_4_) | copy-start | bytes 3145732
  30.0 25.5 %collective-permute-start.6 = (bf16[2,256,1024]{2,1,0:T(8,128)(2,1)S(1)}, bf16[2,256,1024]{2,1,0:T(8,128)(2,1)}, u32[]{:S(2)}, u32[]{:S(2)}) collective-permute-start(bf16[2,256,1024]{2,1,0:T(8,128)(2,1)S(1)} %pad_maximum_fusion.refs_8_), channel_id=1, source_target_pairs={{0,16},{16,0},{32,48},{48,32},{64,80},{80,64},{96,112},{112,96},{1... | collective-permute-start | bytes 3145736 | tf_op jit(solution)/shard_map/ppermute | solution.py:202
  32.8 22.7 %copy-start.6 = (bf16[2,256,1024]{2,1,0:T(8,128)(2,1)}, bf16[2,256,1024]{2,1,0:T(8,128)(2,1)S(1)}, u32[]{:S(2)}) copy-start(bf16[2,256,1024]{2,1,0:T(8,128)(2,1)S(1)} %collective-permute-done.10.refs_10_) | copy-start | bytes 3145732
  32.8 26.3 %collective-permute-start.3 = (bf16[2,1024,256]{2,1,0:T(8,128)(2,1)S(1)}, bf16[2,1024,256]{2,1,0:T(8,128)(2,1)}, u32[]{:S(2)}, u32[]{:S(2)}) collective-permute-start(bf16[2,1024,256]{2,1,0:T(8,128)(2,1)S(1)} %collective-permute-done.2.refs_4_), channel_id=1, source_target_pairs={{0,4},{1,5},{2,6},{3,7},{4,8},{5,9},{6,10},{7,11},{8,12},{9,13},{1... | collective-permute-start | bytes 3145736 | tf_op jit(solution)/shard_map/ppermute | solution.py:202
  34.8 22.1 %copy-start.7 = (bf16[2,256,1024]{2,1,0:T(8,128)(2,1)}, bf16[2,256,1024]{2,1,0:T(8,128)(2,1)S(1)}, u32[]{:S(2)}) copy-start(bf16[2,256,1024]{2,1,0:T(8,128)(2,1)S(1)} %collective-permute-done.9.refs_9_) | copy-start | bytes 3145732
  34.8 27.1 %collective-permute-start.4 = (bf16[2,1024,256]{2,1,0:T(8,128)(2,1)S(1)}, bf16[2,1024,256]{2,1,0:T(8,128)(2,1)}, u32[]{:S(2)}, u32[]{:S(2)}) collective-permute-start(bf16[2,1024,256]{2,1,0:T(8,128)(2,1)S(1)} %collective-permute-done.2.refs_4_), channel_id=1, source_target_pairs={{0,12},{1,13},{2,14},{3,15},{4,0},{5,1},{6,2},{7,3},{8,4},{9,5},{1... | collective-permute-start | bytes 3145736 | tf_op jit(solution)/shard_map/ppermute | solution.py:202
  40.2 21.6 %copy-start.3 = (bf16[2,1024,256]{2,1,0:T(8,128)(2,1)}, bf16[2,1024,256]{2,1,0:T(8,128)(2,1)S(1)}, u32[]{:S(2)}) copy-start(bf16[2,1024,256]{2,1,0:T(8,128)(2,1)S(1)} %collective-permute-done.refs_0_) | copy-start | bytes 3145732
  40.2 23.9 %collective-permute-start.15 = (bf16[1,256,1024]{2,1,0:T(8,128)(2,1)}, bf16[1,256,1024]{2,1,0:T(8,128)(2,1)}, u32[]{:S(2)}, u32[]{:S(2)}) collective-permute-start(bf16[1,256,1024]{2,1,0:T(8,128)(2,1)} %slice.25), channel_id=1, source_target_pairs={{0,96},{16,112},{32,0},{48,16},{64,32},{80,48},{96,64},{112,80},{1... | collective-permute-start | bytes 1572872 | tf_op jit(solution)/shard_map/ppermute | solution.py:202
  41.1 20.7 %copy-start.4 = (bf16[2,1024,256]{2,1,0:T(8,128)(2,1)}, bf16[2,1024,256]{2,1,0:T(8,128)(2,1)S(1)}, u32[]{:S(2)}) copy-start(bf16[2,1024,256]{2,1,0:T(8,128)(2,1)S(1)} %collective-permute-done.1.refs_1_) | copy-start | bytes 3145732
  41.1 25.8 %collective-permute-start.11 = (bf16[1,256,1024]{2,1,0:T(8,128)(2,1)}, bf16[1,256,1024]{2,1,0:T(8,128)(2,1)}, u32[]{:S(2)}, u32[]{:S(2)}) collective-permute-start(bf16[1,256,1024]{2,1,0:T(8,128)(2,1)} %slice.24), channel_id=1, source_target_pairs={{0,32},{16,48},{32,64},{48,80},{64,96},{80,112},{96,0},{112,16},{1... | collective-permute-start | bytes 1572872 | tf_op jit(solution)/shard_map/ppermute | solution.py:202
  55.5 24.8 %collective-permute-start.12 = (bf16[2,256,1024]{2,1,0:T(8,128)(2,1)}, bf16[2,256,1024]{2,1,0:T(8,128)(2,1)}, u32[]{:S(2)}, u32[]{:S(2)}) collective-permute-start(bf16[2,256,1024]{2,1,0:T(8,128)(2,1)} %collective-permute-done.6.refs_4_.refs_12_), channel_id=1, source_target_pairs={{0,32},{16,48},{32,64},{48,80},{64,96},{80,112},{96,0},{112,16},{1... | collective-permute-start | bytes 3145736 | tf_op jit(solution)/shard_map/ppermute | solution.py:202
  59.1 23.8 %collective-permute-start.13 = (bf16[2,256,1024]{2,1,0:T(8,128)(2,1)}, bf16[2,256,1024]{2,1,0:T(8,128)(2,1)}, u32[]{:S(2)}, u32[]{:S(2)}) collective-permute-start(bf16[2,256,1024]{2,1,0:T(8,128)(2,1)} %collective-permute-done.6.refs_4_.refs_12_), channel_id=1, source_target_pairs={{0,96},{16,112},{32,0},{48,16},{64,32},{80,48},{96,64},{112,80},{1... | collective-permute-start | bytes 3145736 | tf_op jit(solution)/shard_map/ppermute | solution.py:202
  62.9 12.8 %collective-permute-start.18 = (bf16[1,1024,256]{2,1,0:T(8,128)(2,1)S(1)}, bf16[1,1024,256]{2,1,0:T(8,128)(2,1)S(1)}, u32[]{:S(2)}, u32[]{:S(2)}) collective-permute-start(bf16[1,1024,256]{2,1,0:T(8,128)(2,1)S(1)} %slice.22), channel_id=1, source_target_pairs={{0,4},{1,5},{2,6},{3,7},{4,8},{5,9},{6,10},{7,11},{8,12},{9,13},{1... | collective-permute-start | bytes 1572872 | tf_op jit(solution)/shard_map/ppermute | solution.py:202
  64.1 11.7 %collective-permute-start.19 = (bf16[1,1024,256]{2,1,0:T(8,128)(2,1)S(1)}, bf16[1,1024,256]{2,1,0:T(8,128)(2,1)S(1)}, u32[]{:S(2)}, u32[]{:S(2)}) collective-permute-start(bf16[1,1024,256]{2,1,0:T(8,128)(2,1)S(1)} %slice.23), channel_id=1, source_target_pairs={{0,12},{1,13},{2,14},{3,15},{4,0},{5,1},{6,2},{7,3},{8,4},{9,5},{1... | collective-permute-start | bytes 1572872 | tf_op jit(solution)/shard_map/ppermute | solution.py:202
  66.8 12.6 %collective-permute-start.16 = (bf16[1,256,1024]{2,1,0:T(8,128)(2,1)}, bf16[1,256,1024]{2,1,0:T(8,128)(2,1)S(1)}, u32[]{:S(2)}, u32[]{:S(2)}) collective-permute-start(bf16[1,256,1024]{2,1,0:T(8,128)(2,1)} %collective-permute-done.15.refs_11_), channel_id=1, source_target_pairs={{0,16},{16,0},{32,48},{48,32},{64,80},{80,64},{96,112},{112,96},{1... | collective-permute-start | bytes 1572872 | tf_op jit(solution)/shard_map/ppermute | solution.py:202
  75.8 7.1 %copy-start.11 = (bf16[1,1024,256]{2,1,0:T(8,128)(2,1)}, bf16[1,1024,256]{2,1,0:T(8,128)(2,1)S(1)}, u32[]{:S(2)}) copy-start(bf16[1,1024,256]{2,1,0:T(8,128)(2,1)S(1)} %collective-permute-done.18.refs_3_) | copy-start | bytes 1572868
  75.8 18.4 %collective-permute-start.7 = (bf16[1,1024,256]{2,1,0:T(8,128)(2,1)}, bf16[1,1024,256]{2,1,0:T(8,128)(2,1)S(1)}, u32[]{:S(2)}, u32[]{:S(2)}) collective-permute-start(bf16[1,1024,256]{2,1,0:T(8,128)(2,1)} %slice.18), channel_id=1, source_target_pairs={{0,12},{1,13},{2,14},{3,15},{4,0},{5,1},{6,2},{7,3},{8,4},{9,5},{1... | collective-permute-start | bytes 1572872 | tf_op jit(solution)/shard_map/ppermute | solution.py:202
  75.8 7.1 %copy-start.13 = (bf16[1,1024,256]{2,1,0:T(8,128)(2,1)}, bf16[1,1024,256]{2,1,0:T(8,128)(2,1)S(1)}, u32[]{:S(2)}) copy-start(bf16[1,1024,256]{2,1,0:T(8,128)(2,1)S(1)} %collective-permute-done.19.refs_7_) | copy-start | bytes 1572868
  75.8 18.3 %collective-permute-start.14 = (bf16[1,256,1024]{2,1,0:T(8,128)(2,1)}, bf16[1,256,1024]{2,1,0:T(8,128)(2,1)S(1)}, u32[]{:S(2)}, u32[]{:S(2)}) collective-permute-start(bf16[1,256,1024]{2,1,0:T(8,128)(2,1)} %collective-permute-done.11.refs_16_.refs_11_), channel_id=1, source_target_pairs={{0,16},{16,0},{32,48},{48,32},{64,80},{80,64},{96,112},{112,96},{1... | collective-permute-start | bytes 1572872 | tf_op jit(solution)/shard_map/ppermute | solution.py:202
  79.4 3.5 %copy-start.15 = (bf16[1,256,1024]{2,1,0:T(8,128)(2,1)}, bf16[1,256,1024]{2,1,0:T(8,128)(2,1)S(1)}, u32[]{:S(2)}) copy-start(bf16[1,256,1024]{2,1,0:T(8,128)(2,1)S(1)} %collective-permute-done.16.refs_15_) | copy-start | bytes 1572868
  79.4 14.7 %collective-permute-start.8 = (bf16[1,1024,256]{2,1,0:T(8,128)(2,1)S(1)}, bf16[1,1024,256]{2,1,0:T(8,128)(2,1)S(1)}, u32[]{:S(2)}, u32[]{:S(2)}) collective-permute-start(bf16[1,1024,256]{2,1,0:T(8,128)(2,1)S(1)} %slice.19), channel_id=1, source_target_pairs={{0,4},{1,5},{2,6},{3,7},{4,8},{5,9},{6,10},{7,11},{8,12},{9,13},{1... | collective-permute-start | bytes 1572872 | tf_op jit(solution)/shard_map/ppermute | solution.py:202
  91.0 13.4 %collective-permute-start.20 = (bf16[8,8,128,128]{3,2,1,0:T(8,128)(2,1)}, bf16[8,8,128,128]{3,2,1,0:T(8,128)(2,1)}, u32[]{:S(2)}, u32[]{:S(2)}) collective-permute-start(bf16[8,8,128,128]{3,2,1,0:T(8,128)(2,1)} %shard_map.58), channel_id=1, source_target_pairs={{0,1},{1,0},{2,3},{3,2},{4,5},{5,4},{6,7},{7,6},{8,9},{9,8},{10,11... | collective-permute-start | bytes 6291464 | tf_op jit(solution)/shard_map/ppermute | solution.py:202
  94.1 0.8 copy-start.9
  94.2 1.0 copy-start.12
  95.2 0.8 copy-start.14
  104.0 8.7 %collective-permute-start.17 = (bf16[8,8,128,128]{3,2,1,0:T(8,128)(2,1)}, bf16[8,8,128,128]{3,2,1,0:T(8,128)(2,1)S(1)}, u32[]{:S(2)}, u32[]{:S(2)}) collective-permute-start(bf16[8,8,128,128]{3,2,1,0:T(8,128)(2,1)} %shard_map.57), channel_id=1, source_target_pairs={{0,1},{1,0},{2,3},{3,2},{4,5},{5,4},{6,7},{7,6},{8,9},{9,8},{10,11... | collective-permute-start | bytes 6291464 | tf_op jit(solution)/shard_map/ppermute | solution.py:202
  112.7 1.4 copy-start.10
  182.5 7.2 %copy-start.16 = (f32[4096]{0:T(1024)S(1)}, f32[4096]{0:T(1024)}, u32[]{:S(2)}) copy-start(f32[4096]{0:T(1024)} %param.9) | copy-start | bytes 49156
  182.5 7.2 %copy-start.17 = (f32[4]{0:T(128)S(1)}, f32[4]{0:T(128)}, u32[]{:S(2)}) copy-start(f32[4]{0:T(128)} %param.8) | copy-start | bytes 52
  182.5 59.5 %all-to-all-start.1 = ((bf16[128,128,128]{2,1,0:T(8,128)(2,1)}), bf16[128,128,128]{2,1,0:T(8,128)(2,1)}, u32[]{:S(2)}, u32[]{:S(2)}) async-start(bf16[128,128,128]{2,1,0:T(8,128)(2,1)} %bitcast.13), calls=%async_computation.1 | async-start | bytes 8388608 | tf_op jit(solution)/shard_map/all_to_all | solution.py:233

commit v3 on v2

--- a/solution.py
+++ b/solution.py
@@ -204,7 +204,8 @@
     core = col_place % 2
     kept = lax.dynamic_slice_in_dim(integrals, core * 256, 256, 0)
     passed = lax.dynamic_slice_in_dim(integrals, (1 - core) * 256, 256, 0)
-    b_own = jnp.stack([kept, move(passed, CORE_SWAP)])
+    b_kept, b_other = kept[None], move(passed, CORE_SWAP)[None]
+    b_own = jnp.concatenate([b_kept, b_other])
     own_mask = lax.dynamic_slice_in_dim(tile_mask, col_place * tile_rows, tile_rows, 0)
     a_own = prep(own_mask, amplitudes)
 
@@ -213,9 +214,9 @@
     b_below, b_above = move(b_own, Y_UP), move(b_own, Y_DOWN)
     b_first, b_second = move(b_below[:1], Y_UP), move(b_above[1:], Y_DOWN)
     far_below, far_above = move(a_far, Z_UP), move(a_far, Z_DOWN)
-    b_far = move(b_own, XH_SWAP)
-    b_far_below, b_far_above = move(b_far, Y_UP), move(b_far, Y_DOWN)
-    a_below, a_above, far_below, far_above = gate((a_below, a_above, far_below, far_above), (b_far,))
+    b_far = [move(x, XH_SWAP) for x in gate((b_kept, b_other), (a_far,))]
+    b_far_below, b_far_above = [move(x, Y_UP) for x in b_far], [move(x, Y_DOWN) for x in b_far]
+    a_below, a_above, far_below, far_above = gate((a_below, a_above, far_below, far_above), (b_far[1],))
     a_first, a_second = move(a_below[:1], Z_UP), move(a_above[1:], Z_DOWN)
     b_far_first, b_far_second = move(b_first, XH_SWAP), move(b_second, XH_SWAP)
     far_first, far_second = move(far_above[:1], Z_DOWN), move(far_below[1:], Z_UP)
@@ -223,10 +224,11 @@
         a_own, a_below, a_above, (a_first, a_second)[j], a_far, far_below, far_above, (far_first, far_second)[j],
     ]
     b_of = lambda h: [
-        b_own, b_below, b_above, (b_first, b_second)[h], b_far, b_far_below, b_far_above, (b_far_first, b_far_second)[h],
+        b_own, b_below, b_above, (b_first, b_second)[h],
+        b_far[h], b_far_below[h], b_far_above[h], (b_far_first, b_far_second)[h],
     ]
-    taken = [move(product(a_of(0), b_of(1), 0, 1, also=(b_first,)), CORE_SWAP)]
-    taken.append(move(product(a_of(1), b_of(1), 1, 1, also=(b_far_first,)), CORE_SWAP))
+    taken = [move(product(a_of(0), b_of(1), 0, 1, also=(b_first, b_far[0])), CORE_SWAP)]
+    taken.append(move(product(a_of(1), b_of(1), 1, 1, also=(b_far_first, b_far_below[0], b_far_above[0])), CORE_SWAP))
     made = product(a_of(0), b_of(0), 0, 0, taken[0])
     made = product(a_of(1), b_of(0), 1, 0, taken[1], made)
     direct = lax.all_to_all(made, "col", split_axis=0, concat_axis=0, tiled=True).reshape(128, 128, 128)

time: 252 us -> 251 us (level)
  waiting for transfers between devices: 93 us -> 83.9 us
  starting transfers between devices: 40.7 us -> 46.7 us
  local copies, waits for them, and re-layouts: 14.1 us -> 17.8 us
    ppermute x21 -> x24, waiting for transfers between devices: 42.3 us -> 33.1 us  [local(): lax.ppermute(block, 'col' if len(pairs) == 16 else 'row', pairs)]
    ppermute x21 -> x24, starting transfers between devices: 33.6 us -> 39.6 us  [local(): lax.ppermute(block, 'col' if len(pairs) == 16 else 'row', pairs)]
    unnamed x39 -> x35, local copies, waits for them, and re-layouts: 5.18 us -> 5.11 us
  transfers between devices with their start and end apart: 22 -> 25, of which waited for: 9 -> 7; matrix products, arithmetic and copies ran while one was open for 3% -> 5% of each run, Pallas kernels for 10% -> 10%
where the time goes in v3:
time: 251 us; the launch traced here: 250 us
  waiting for transfers between devices  83.9 us (33%)
  blocking collectives  57.7 us (23%)
  starting transfers between devices  46.7 us (19%)
  Pallas kernels  42.8 us (17%)
  local copies, waits for them, and re-layouts  17.8 us (7%)
    all_to_all x1, blocking collectives, local(): lax.all_to_all(made, 'col', split_axis=0, concat_axis=0, tiled=True)  57.7 us
    all_to_all x1, waiting for transfers between devices, local(): lax.all_to_all(direct, ('row', 'col'), split_axis=0, concat_axis=0, tiled...  50.8 us
    ppermute x24, starting transfers between devices, local(): lax.ppermute(block, 'col' if len(pairs) == 16 else 'row', pairs)  39.6 us
    ppermute x24, waiting for transfers between devices, local(): lax.ppermute(block, 'col' if len(pairs) == 16 else 'row', pairs)  33.1 us
    pallas_call x4, Pallas kernels, product(): pl.pallas_call(functools.partial(product_kernel, j, h, taken is not None)...  32.7 us
    pallas_call x1, Pallas kernels, finish(): pl.pallas_call(finish_kernel, grid=(count // step,), out_shape=jax.ShapeD...  9.17 us
    all_to_all x1, starting transfers between devices, local(): lax.all_to_all(direct, ('row', 'col'), split_axis=0, concat_axis=0, tiled...  7.04 us
    unnamed x35, local copies, waits for them, and re-layouts  5.11 us
  transfers between devices with their start and end apart: 25, of which 7 were waited for; matrix products, arithmetic and copies ran while one was open for 5% of the time, Pallas kernels for 10%

profile of v3, /device:TPU:1, one launch (start us, length us, event | category | flops | bytes accessed | tf_op | source)
XLA Modules:
  0.0 250.3 jit_solution(8297007541910427717)
XLA Ops:
  0.0 2.1 constant_dynamic-slice_fusion
  2.1 1.4 collective-permute-start.5
  3.5 0.1 constant_dynamic-slice_fusion.1
  3.6 0.1 copy.15.mask_ref
  3.7 1.2 copy-done.2
  4.9 0.9 shard_map.55.refs_0_
  5.8 1.4 collective-permute-start.2
  7.2 1.6 collective-permute-start
  8.8 0.0 collective-permute-done.5
  8.8 1.1 pad_maximum_fusion.refs_8_
  10.0 2.7 %collective-permute-start.10 = (bf16[2,256,1024]{2,1,0:T(8,128)(2,1)}, bf16[2,256,1024]{2,1,0:T(8,128)(2,1)}, u32[]{:S(2)}, u32[]{:S(2)}) collective-permute-start(bf16[2,256,1024]{2,1,0:T(8,128)(2,1)} %pad_maximum_fusion.refs_8_), channel_id=1, source_target_pairs={{0,96},{16,112},{32,0},{48,16},{64,32},{80,48},{96,64},{112,80},{1... | collective-permute-start | bytes 3145736 | tf_op jit(solution)/shard_map/ppermute | solution.py:202
  12.7 2.1 collective-permute-start.1
  14.9 0.0 collective-permute-start.9
  14.9 15.9 %collective-permute-done.2.refs_2_.refs_4_ = bf16[2,1024,256]{2,1,0:T(8,128)(2,1)} collective-permute-done((bf16[2,1024,256]{2,1,0:T(8,128)(2,1)S(1)}, bf16[2,1024,256]{2,1,0:T(8,128)(2,1)}, u32[]{:S(2)}, u32[]{:S(2)}) %collective-permute-start.2) | collective-permute-done | bytes 1048608 | tf_op jit(solution)/shard_map/ppermute | solution.py:202
  30.8 1.7 collective-permute-start.3
  32.5 1.9 collective-permute-done.refs_0_
  34.4 1.1 collective-permute-start.4
  35.5 2.5 collective-permute-start.6
  38.0 1.9 slice.25
  39.9 0.5 collective-permute-start.12
  40.4 9.1 %collective-permute-done.6.refs_4_.refs_12_ = bf16[1,256,1024]{2,1,0:T(8,128)(2,1)} collective-permute-done((bf16[1,256,1024]{2,1,0:T(8,128)(2,1)}, bf16[1,256,1024]{2,1,0:T(8,128)(2,1)}, u32[]{:S(2)}, u32[]{:S(2)}) %collective-permute-start.6) | collective-permute-done | bytes 524320 | tf_op jit(solution)/shard_map/ppermute | solution.py:202
  49.4 1.3 collective-permute-start.17
  50.7 0.0 collective-permute-done.9.refs_9_
  50.7 1.4 collective-permute-start.16
  52.2 1.9 slice.24
  54.0 3.6 %collective-permute-done.3.refs_2_ = bf16[2,1024,256]{2,1,0:T(8,128)(2,1)} collective-permute-done((bf16[2,1024,256]{2,1,0:T(8,128)(2,1)}, bf16[2,1024,256]{2,1,0:T(8,128)(2,1)}, u32[]{:S(2)}, u32[]{:S(2)}) %collective-permute-start.3) | collective-permute-done | bytes 1048608 | tf_op jit(solution)/shard_map/ppermute | solution.py:202
  57.6 1.3 collective-permute-start.11
  58.9 1.0 collective-permute-done.4.refs_3_
  59.9 1.5 collective-permute-start.18
  61.4 1.1 slice.22
  62.5 1.1 slice.23
  63.6 0.0 collective-permute-done.12.refs_17_.refs_12_
  63.6 0.1 collective-permute-start.21
  63.7 2.7 %collective-permute-start.22 = (bf16[1,1024,256]{2,1,0:T(8,128)(2,1)S(1)}, bf16[1,1024,256]{2,1,0:T(8,128)(2,1)S(1)}, u32[]{:S(2)}, u32[]{:S(2)}) collective-permute-start(bf16[1,1024,256]{2,1,0:T(8,128)(2,1)S(1)} %slice.23), channel_id=1, source_target_pairs={{0,12},{1,13},{2,14},{3,15},{4,0},{5,1},{6,2},{7,3},{8,4},{9,5},{1... | collective-permute-start | bytes 1572872 | tf_op jit(solution)/shard_map/ppermute | solution.py:202
  66.3 0.0 collective-permute-done.16.refs_11_
  66.3 2.5 collective-permute-start.19
  68.8 1.9 slice.18
  70.7 1.9 slice.19
  72.6 1.7 collective-permute-done.18.refs_14_
  74.2 0.3 collective-permute-start.13
  74.6 0.0 collective-permute-done.11.refs_16_.refs_11_
  74.6 2.4 collective-permute-start.14
  76.9 2.3 collective-permute-start.7
  79.2 2.5 collective-permute-start.15
  81.7 0.0 collective-permute-done.19.refs_15_
  81.7 0.0 collective-permute-start.8
  81.7 0.8 copy-done.12
  82.5 8.0 %shard_map.59 = bf16[8,8,128,128]{3,2,1,0:T(8,128)(2,1)} custom-call(bf16[2,1024,256]{2,1,0:T(8,128)(2,1)} %copy-done.1, bf16[2,1024,256]{2,1,0:T(8,128)(2,1)} %get-tuple-element.12.refs_1_, bf16[2,1024,256]{2,1,0:T(8,128)(2,1)} %get-tuple-element.13.refs_2_, bf16[1,1024,256]{2,1,0:T(8,128)(2,1)} %copy-done.10, ...), custom_call_target="tpu_custom_call" | custom-call | flops 4294967296 | bytes 10485760 | tf_op jit(solution)/shard_map/pallas_call | solution.py:128
  90.6 3.8 %collective-permute-start.23 = (bf16[8,8,128,128]{3,2,1,0:T(8,128)(2,1)}, bf16[8,8,128,128]{3,2,1,0:T(8,128)(2,1)S(1)}, u32[]{:S(2)}, u32[]{:S(2)}) collective-permute-start(bf16[8,8,128,128]{3,2,1,0:T(8,128)(2,1)} %shard_map.59), channel_id=1, source_target_pairs={{0,1},{1,0},{2,3},{3,2},{4,5},{5,4},{6,7},{7,6},{8,9},{9,8},{10,11... | collective-permute-start | bytes 6291464 | tf_op jit(solution)/shard_map/ppermute | solution.py:202
  94.4 0.8 copy-done.6
  95.1 0.2 copy-done.7
  95.3 8.0 %shard_map.58 = bf16[8,8,128,128]{3,2,1,0:T(8,128)(2,1)} custom-call(bf16[2,1024,256]{2,1,0:T(8,128)(2,1)} %copy-done.1, bf16[2,1024,256]{2,1,0:T(8,128)(2,1)} %get-tuple-element.12.refs_1_, bf16[2,1024,256]{2,1,0:T(8,128)(2,1)} %get-tuple-element.13.refs_2_, bf16[1,1024,256]{2,1,0:T(8,128)(2,1)} %collective-permute-done.7.refs_3_, ...), custom_call_target="tpu_custom_call" | custom-call | flops 4294967296 | bytes 10485760 | tf_op jit(solution)/shard_map/pallas_call | solution.py:128
  103.4 2.6 %collective-permute-start.20 = (bf16[8,8,128,128]{3,2,1,0:T(8,128)(2,1)}, bf16[8,8,128,128]{3,2,1,0:T(8,128)(2,1)}, u32[]{:S(2)}, u32[]{:S(2)}) collective-permute-start(bf16[8,8,128,128]{3,2,1,0:T(8,128)(2,1)} %shard_map.58), channel_id=1, source_target_pairs={{0,1},{1,0},{2,3},{3,2},{4,5},{5,4},{6,7},{7,6},{8,9},{9,8},{10,11... | collective-permute-start | bytes 6291464 | tf_op jit(solution)/shard_map/ppermute | solution.py:202
  106.0 1.4 copy-done.9
  107.3 8.3 %shard_map.60.refs_17_ = bf16[16,8,128,128]{3,2,1,0:T(8,128)(2,1)} custom-call(bf16[2,1024,256]{2,1,0:T(8,128)(2,1)} %copy-done.1, bf16[2,1024,256]{2,1,0:T(8,128)(2,1)} %get-tuple-element.12.refs_1_, bf16[2,1024,256]{2,1,0:T(8,128)(2,1)} %get-tuple-element.13.refs_2_, bf16[1,1024,256]{2,1,0:T(8,128)(2,1)} %copy-done.10, ...), custom_call_target="tpu_custom_call" | custom-call | flops 4294967296 | bytes 10485760 | tf_op jit(solution)/shard_map/pallas_call | solution.py:128
  115.7 8.3 %shard_map.61 = bf16[16,8,128,128]{3,2,1,0:T(8,128)(2,1)} custom-call(bf16[2,1024,256]{2,1,0:T(8,128)(2,1)} %copy-done.1, bf16[2,1024,256]{2,1,0:T(8,128)(2,1)} %get-tuple-element.12.refs_1_, bf16[2,1024,256]{2,1,0:T(8,128)(2,1)} %get-tuple-element.13.refs_2_, bf16[1,1024,256]{2,1,0:T(8,128)(2,1)} %collective-permute-done.7.refs_3_, ...), custom_call_target="tpu_custom_call", output_to_operand_aliasing={{}: (17, {})} | custom-call | flops 4294967296 | bytes 10485760 | tf_op jit(solution)/shard_map/pallas_call | solution.py:128
  124.0 57.7 %all_to_all.10 = bf16[16,8,128,128]{3,2,1,0:T(8,128)(2,1)} all-to-all(bf16[16,8,128,128]{3,2,1,0:T(8,128)(2,1)} %shard_map.61), channel_id=1, replica_groups=mesh['row'=8,'col'=16] {'col'}, dimensions={0} | all-to-all | bytes 8388608 | tf_op jit(solution)/shard_map/all_to_all | solution.py:234
  181.7 7.0 %all-to-all-start.1 = ((bf16[128,128,128]{2,1,0:T(8,128)(2,1)}), bf16[128,128,128]{2,1,0:T(8,128)(2,1)}, u32[]{:S(2)}, u32[]{:S(2)}) async-start(bf16[128,128,128]{2,1,0:T(8,128)(2,1)} %bitcast.13), calls=%async_computation.1 | async-start | bytes 8388608 | tf_op jit(solution)/shard_map/all_to_all | solution.py:235
  188.8 0.1 subtract_bitcast_fusion
  188.9 0.1 dynamic-slice_bitcast_fusion.1
  189.0 0.7 copy.14.row_gap_ref
  189.7 0.7 copy.17
  190.4 50.8 %all-to-all-done.1.refs_1_ = bf16[128,128,128]{2,1,0:T(8,128)(2,1)} async-done(((bf16[128,128,128]{2,1,0:T(8,128)(2,1)}), bf16[128,128,128]{2,1,0:T(8,128)(2,1)}, u32[]{:S(2)}, u32[]{:S(2)}) %all-to-all-start.1) | async-done | bytes 4194336 | tf_op jit(solution)/shard_map/all_to_all | solution.py:235
  241.2 9.2 %shard_map.62 = bf16[128,16384]{1,0:T(8,128)(2,1)} custom-call(f32[128,1]{1,0:T(8,128)} %copy.14.row_gap_ref, f32[1,16384]{1,0:T(1,128)} %bitcast.17, bf16[128,128,128]{2,1,0:T(8,128)(2,1)} %bitcast.14, bf16[128,128,128]{2,1,0:T(8,128)(2,1)} %all-to-all-done.1.refs_1_), custom_call_target="tpu_custom_call" | custom-call | tf_op jit(solution)/shard_map/pallas_call | solution.py:171
  (42 shorter events, 0.1 us)
Async XLA Ops:
  0.0 3.5 %copy-start = (s32[64,32]{0,1:T(8,128)S(1)}, s32[64,32]{0,1:T(8,128)}, u32[]{:S(2)}) copy-start(s32[64,32]{0,1:T(8,128)} %param.7) | copy-start | bytes 24580
  2.1 7.9 %copy-start.8 = (bf16[1,256,1024]{2,1,0:T(8,128)(2,1)}, bf16[1,256,1024]{2,1,0:T(8,128)(2,1)S(1)}, u32[]{:S(2)}) copy-start(bf16[1,256,1024]{2,1,0:T(8,128)(2,1)S(1)} %get-tuple-element.18.refs_0_) | copy-start | bytes 1572868
  2.1 6.8 %collective-permute-start.5 = (bf16[256,1024]{1,0:T(8,128)(2,1)}, bf16[256,1024]{1,0:T(8,128)(2,1)S(1)}, u32[]{:S(2)}, u32[]{:S(2)}) collective-permute-start(bf16[256,1024]{1,0:T(8,128)(2,1)} %get-tuple-element.17), channel_id=1, source_target_pairs={{0,1},{1,0},{2,3},{3,2},{4,5},{5,4},{6,7},{7,6},{8,9},{9,8},{10,11... | collective-permute-start | bytes 1572872 | tf_op jit(solution)/shard_map/ppermute | solution.py:202
  3.7 1.2 copy-start.2
  5.8 55.6 %copy-start.1 = (bf16[2,1024,256]{2,1,0:T(8,128)(2,1)}, bf16[2,1024,256]{2,1,0:T(8,128)(2,1)S(1)}, u32[]{:S(2)}) copy-start(bf16[2,1024,256]{2,1,0:T(8,128)(2,1)S(1)} %shard_map.55.refs_0_) | copy-start | bytes 3145732
  5.8 24.9 %collective-permute-start.2 = (bf16[2,1024,256]{2,1,0:T(8,128)(2,1)S(1)}, bf16[2,1024,256]{2,1,0:T(8,128)(2,1)}, u32[]{:S(2)}, u32[]{:S(2)}) collective-permute-start(bf16[2,1024,256]{2,1,0:T(8,128)(2,1)S(1)} %shard_map.55.refs_0_), channel_id=1, source_target_pairs={{0,2},{1,3},{2,0},{3,1},{4,6},{5,7},{6,4},{7,5},{8,10},{9,11},{10,... | collective-permute-start | bytes 3145736 | tf_op jit(solution)/shard_map/ppermute | solution.py:202
  7.2 27.2 %collective-permute-start = (bf16[2,1024,256]{2,1,0:T(8,128)(2,1)S(1)}, bf16[2,1024,256]{2,1,0:T(8,128)(2,1)S(1)}, u32[]{:S(2)}, u32[]{:S(2)}) collective-permute-start(bf16[2,1024,256]{2,1,0:T(8,128)(2,1)S(1)} %shard_map.55.refs_0_), channel_id=1, source_target_pairs={{0,4},{1,5},{2,6},{3,7},{4,8},{5,9},{6,10},{7,11},{8,12},{9,13},{1... | collective-permute-start | bytes 3145736 | tf_op jit(solution)/shard_map/ppermute | solution.py:202
  8.8 1.2 copy-start.13
  10.0 25.5 %collective-permute-start.10 = (bf16[2,256,1024]{2,1,0:T(8,128)(2,1)}, bf16[2,256,1024]{2,1,0:T(8,128)(2,1)}, u32[]{:S(2)}, u32[]{:S(2)}) collective-permute-start(bf16[2,256,1024]{2,1,0:T(8,128)(2,1)} %pad_maximum_fusion.refs_8_), channel_id=1, source_target_pairs={{0,96},{16,112},{32,0},{48,16},{64,32},{80,48},{96,64},{112,80},{1... | collective-permute-start | bytes 3145736 | tf_op jit(solution)/shard_map/ppermute | solution.py:202
  12.7 27.1 %collective-permute-start.1 = (bf16[2,1024,256]{2,1,0:T(8,128)(2,1)S(1)}, bf16[2,1024,256]{2,1,0:T(8,128)(2,1)S(1)}, u32[]{:S(2)}, u32[]{:S(2)}) collective-permute-start(bf16[2,1024,256]{2,1,0:T(8,128)(2,1)S(1)} %shard_map.55.refs_0_), channel_id=1, source_target_pairs={{0,12},{1,13},{2,14},{3,15},{4,0},{5,1},{6,2},{7,3},{8,4},{9,5},{1... | collective-permute-start | bytes 3145736 | tf_op jit(solution)/shard_map/ppermute | solution.py:202
  14.9 35.9 %collective-permute-start.9 = (bf16[2,256,1024]{2,1,0:T(8,128)(2,1)}, bf16[2,256,1024]{2,1,0:T(8,128)(2,1)}, u32[]{:S(2)}, u32[]{:S(2)}) collective-permute-start(bf16[2,256,1024]{2,1,0:T(8,128)(2,1)} %pad_maximum_fusion.refs_8_), channel_id=1, source_target_pairs={{0,32},{16,48},{32,64},{48,80},{64,96},{80,112},{96,0},{112,16},{1... | collective-permute-start | bytes 3145736 | tf_op jit(solution)/shard_map/ppermute | solution.py:202
  30.8 26.9 %collective-permute-start.3 = (bf16[2,1024,256]{2,1,0:T(8,128)(2,1)}, bf16[2,1024,256]{2,1,0:T(8,128)(2,1)}, u32[]{:S(2)}, u32[]{:S(2)}) collective-permute-start(bf16[2,1024,256]{2,1,0:T(8,128)(2,1)} %collective-permute-done.2.refs_2_.refs_4_), channel_id=1, source_target_pairs={{0,4},{1,5},{2,6},{3,7},{4,8},{5,9},{6,10},{7,11},{8,12},{9,13},{1... | collective-permute-start | bytes 3145736 | tf_op jit(solution)/shard_map/ppermute | solution.py:202
  34.4 27.0 %copy-start.3 = (bf16[2,1024,256]{2,1,0:T(8,128)(2,1)}, bf16[2,1024,256]{2,1,0:T(8,128)(2,1)S(1)}, u32[]{:S(2)}) copy-start(bf16[2,1024,256]{2,1,0:T(8,128)(2,1)S(1)} %collective-permute-done.refs_0_) | copy-start | bytes 3145732
  34.4 25.6 %collective-permute-start.4 = (bf16[2,1024,256]{2,1,0:T(8,128)(2,1)}, bf16[2,1024,256]{2,1,0:T(8,128)(2,1)}, u32[]{:S(2)}, u32[]{:S(2)}) collective-permute-start(bf16[2,1024,256]{2,1,0:T(8,128)(2,1)} %collective-permute-done.2.refs_2_.refs_4_), channel_id=1, source_target_pairs={{0,12},{1,13},{2,14},{3,15},{4,0},{5,1},{6,2},{7,3},{8,4},{9,5},{1... | collective-permute-start | bytes 3145736 | tf_op jit(solution)/shard_map/ppermute | solution.py:202
  35.5 13.9 %collective-permute-start.6 = (bf16[1,256,1024]{2,1,0:T(8,128)(2,1)}, bf16[1,256,1024]{2,1,0:T(8,128)(2,1)}, u32[]{:S(2)}, u32[]{:S(2)}) collective-permute-start(bf16[1,256,1024]{2,1,0:T(8,128)(2,1)} %get-tuple-element.11), channel_id=1, source_target_pairs={{0,16},{16,0},{32,48},{48,32},{64,80},{80,64},{96,112},{112,96},{1... | collective-permute-start | bytes 1572872 | tf_op jit(solution)/shard_map/ppermute | solution.py:202
  39.8 21.6 %copy-start.4 = (bf16[2,1024,256]{2,1,0:T(8,128)(2,1)}, bf16[2,1024,256]{2,1,0:T(8,128)(2,1)S(1)}, u32[]{:S(2)}) copy-start(bf16[2,1024,256]{2,1,0:T(8,128)(2,1)S(1)} %collective-permute-done.1.refs_1_) | copy-start | bytes 3145732
  39.9 23.7 %collective-permute-start.12 = (bf16[1,256,1024]{2,1,0:T(8,128)(2,1)}, bf16[1,256,1024]{2,1,0:T(8,128)(2,1)}, u32[]{:S(2)}, u32[]{:S(2)}) collective-permute-start(bf16[1,256,1024]{2,1,0:T(8,128)(2,1)} %get-tuple-element.16), channel_id=1, source_target_pairs={{0,16},{16,0},{32,48},{48,32},{64,80},{80,64},{96,112},{112,96},{1... | collective-permute-start | bytes 1572872 | tf_op jit(solution)/shard_map/ppermute | solution.py:202
  49.4 14.2 %collective-permute-start.17 = (bf16[1,256,1024]{2,1,0:T(8,128)(2,1)}, bf16[1,256,1024]{2,1,0:T(8,128)(2,1)}, u32[]{:S(2)}, u32[]{:S(2)}) collective-permute-start(bf16[1,256,1024]{2,1,0:T(8,128)(2,1)} %collective-permute-done.6.refs_4_.refs_12_), channel_id=1, source_target_pairs={{0,32},{16,48},{32,64},{48,80},{64,96},{80,112},{96,0},{112,16},{1... | collective-permute-start | bytes 1572872 | tf_op jit(solution)/shard_map/ppermute | solution.py:202
  50.7 15.6 %collective-permute-start.16 = (bf16[1,256,1024]{2,1,0:T(8,128)(2,1)}, bf16[1,256,1024]{2,1,0:T(8,128)(2,1)}, u32[]{:S(2)}, u32[]{:S(2)}) collective-permute-start(bf16[1,256,1024]{2,1,0:T(8,128)(2,1)} %slice.25), channel_id=1, source_target_pairs={{0,96},{16,112},{32,0},{48,16},{64,32},{80,48},{96,64},{112,80},{1... | collective-permute-start | bytes 1572872 | tf_op jit(solution)/shard_map/ppermute | solution.py:202
  57.6 16.9 %collective-permute-start.11 = (bf16[1,256,1024]{2,1,0:T(8,128)(2,1)}, bf16[1,256,1024]{2,1,0:T(8,128)(2,1)}, u32[]{:S(2)}, u32[]{:S(2)}) collective-permute-start(bf16[1,256,1024]{2,1,0:T(8,128)(2,1)} %slice.24), channel_id=1, source_target_pairs={{0,32},{16,48},{32,64},{48,80},{64,96},{80,112},{96,0},{112,16},{1... | collective-permute-start | bytes 1572872 | tf_op jit(solution)/shard_map/ppermute | solution.py:202
  59.9 14.3 %collective-permute-start.18 = (bf16[1,256,1024]{2,1,0:T(8,128)(2,1)}, bf16[1,256,1024]{2,1,0:T(8,128)(2,1)}, u32[]{:S(2)}, u32[]{:S(2)}) collective-permute-start(bf16[1,256,1024]{2,1,0:T(8,128)(2,1)} %collective-permute-done.6.refs_4_.refs_12_), channel_id=1, source_target_pairs={{0,96},{16,112},{32,0},{48,16},{64,32},{80,48},{96,64},{112,80},{1... | collective-permute-start | bytes 1572872 | tf_op jit(solution)/shard_map/ppermute | solution.py:202
  63.6 13.4 %collective-permute-start.21 = (bf16[1,1024,256]{2,1,0:T(8,128)(2,1)S(1)}, bf16[1,1024,256]{2,1,0:T(8,128)(2,1)S(1)}, u32[]{:S(2)}, u32[]{:S(2)}) collective-permute-start(bf16[1,1024,256]{2,1,0:T(8,128)(2,1)S(1)} %slice.22), channel_id=1, source_target_pairs={{0,4},{1,5},{2,6},{3,7},{4,8},{5,9},{6,10},{7,11},{8,12},{9,13},{1... | collective-permute-start | bytes 1572872 | tf_op jit(solution)/shard_map/ppermute | solution.py:202
  63.7 15.6 %collective-permute-start.22 = (bf16[1,1024,256]{2,1,0:T(8,128)(2,1)S(1)}, bf16[1,1024,256]{2,1,0:T(8,128)(2,1)S(1)}, u32[]{:S(2)}, u32[]{:S(2)}) collective-permute-start(bf16[1,1024,256]{2,1,0:T(8,128)(2,1)S(1)} %slice.23), channel_id=1, source_target_pairs={{0,12},{1,13},{2,14},{3,15},{4,0},{5,1},{6,2},{7,3},{8,4},{9,5},{1... | collective-permute-start | bytes 1572872 | tf_op jit(solution)/shard_map/ppermute | solution.py:202
  66.3 15.4 %collective-permute-start.19 = (bf16[1,256,1024]{2,1,0:T(8,128)(2,1)}, bf16[1,256,1024]{2,1,0:T(8,128)(2,1)S(1)}, u32[]{:S(2)}, u32[]{:S(2)}) collective-permute-start(bf16[1,256,1024]{2,1,0:T(8,128)(2,1)} %collective-permute-done.16.refs_11_), channel_id=1, source_target_pairs={{0,16},{16,0},{32,48},{48,32},{64,80},{80,64},{96,112},{112,96},{1... | collective-permute-start | bytes 1572872 | tf_op jit(solution)/shard_map/ppermute | solution.py:202
  74.2 16.3 %collective-permute-start.13 = (bf16[1,256,1024]{2,1,0:T(8,128)(2,1)}, bf16[1,256,1024]{2,1,0:T(8,128)(2,1)S(1)}, u32[]{:S(2)}, u32[]{:S(2)}) collective-permute-start(bf16[1,256,1024]{2,1,0:T(8,128)(2,1)} %collective-permute-done.12.refs_17_.refs_12_), channel_id=1, source_target_pairs={{0,32},{16,48},{32,64},{48,80},{64,96},{80,112},{96,0},{112,16},{1... | collective-permute-start | bytes 1572872 | tf_op jit(solution)/shard_map/ppermute | solution.py:202
  74.6 19.8 %collective-permute-start.14 = (bf16[1,256,1024]{2,1,0:T(8,128)(2,1)}, bf16[1,256,1024]{2,1,0:T(8,128)(2,1)S(1)}, u32[]{:S(2)}, u32[]{:S(2)}) collective-permute-start(bf16[1,256,1024]{2,1,0:T(8,128)(2,1)} %collective-permute-done.12.refs_17_.refs_12_), channel_id=1, source_target_pairs={{0,96},{16,112},{32,0},{48,16},{64,32},{80,48},{96,64},{112,80},{1... | collective-permute-start | bytes 1572872 | tf_op jit(solution)/shard_map/ppermute | solution.py:202
  76.9 4.8 %copy-start.10 = (bf16[1,1024,256]{2,1,0:T(8,128)(2,1)}, bf16[1,1024,256]{2,1,0:T(8,128)(2,1)S(1)}, u32[]{:S(2)}) copy-start(bf16[1,1024,256]{2,1,0:T(8,128)(2,1)S(1)} %collective-permute-done.21.refs_3_) | copy-start | bytes 1572868
  76.9 17.4 %collective-permute-start.7 = (bf16[1,1024,256]{2,1,0:T(8,128)(2,1)}, bf16[1,1024,256]{2,1,0:T(8,128)(2,1)}, u32[]{:S(2)}, u32[]{:S(2)}) collective-permute-start(bf16[1,1024,256]{2,1,0:T(8,128)(2,1)} %slice.18), channel_id=1, source_target_pairs={{0,12},{1,13},{2,14},{3,15},{4,0},{5,1},{6,2},{7,3},{8,4},{9,5},{1... | collective-permute-start | bytes 1572872 | tf_op jit(solution)/shard_map/ppermute | solution.py:202
  79.2 2.5 copy-start.11
  79.2 15.1 %collective-permute-start.15 = (bf16[1,256,1024]{2,1,0:T(8,128)(2,1)}, bf16[1,256,1024]{2,1,0:T(8,128)(2,1)S(1)}, u32[]{:S(2)}, u32[]{:S(2)}) collective-permute-start(bf16[1,256,1024]{2,1,0:T(8,128)(2,1)} %collective-permute-done.11.refs_16_.refs_11_), channel_id=1, source_target_pairs={{0,16},{16,0},{32,48},{48,32},{64,80},{80,64},{96,112},{112,96},{1... | collective-permute-start | bytes 1572872 | tf_op jit(solution)/shard_map/ppermute | solution.py:202
  81.7 0.8 copy-start.12
  81.7 12.7 %collective-permute-start.8 = (bf16[1,1024,256]{2,1,0:T(8,128)(2,1)}, bf16[1,1024,256]{2,1,0:T(8,128)(2,1)}, u32[]{:S(2)}, u32[]{:S(2)}) collective-permute-start(bf16[1,1024,256]{2,1,0:T(8,128)(2,1)} %slice.19), channel_id=1, source_target_pairs={{0,4},{1,5},{2,6},{3,7},{4,8},{5,9},{6,10},{7,11},{8,12},{9,13},{1... | collective-permute-start | bytes 1572872 | tf_op jit(solution)/shard_map/ppermute | solution.py:202
  90.6 3.8 %copy-start.5 = (bf16[1,256,1024]{2,1,0:T(8,128)(2,1)}, bf16[1,256,1024]{2,1,0:T(8,128)(2,1)S(1)}, u32[]{:S(2)}) copy-start(bf16[1,256,1024]{2,1,0:T(8,128)(2,1)S(1)} %collective-permute-done.13.refs_17_.refs_13_) | copy-start | bytes 1572868
  90.6 15.4 %collective-permute-start.23 = (bf16[8,8,128,128]{3,2,1,0:T(8,128)(2,1)}, bf16[8,8,128,128]{3,2,1,0:T(8,128)(2,1)S(1)}, u32[]{:S(2)}, u32[]{:S(2)}) collective-permute-start(bf16[8,8,128,128]{3,2,1,0:T(8,128)(2,1)} %shard_map.59), channel_id=1, source_target_pairs={{0,1},{1,0},{2,3},{3,2},{4,5},{5,4},{6,7},{7,6},{8,9},{9,8},{10,11... | collective-permute-start | bytes 6291464 | tf_op jit(solution)/shard_map/ppermute | solution.py:202
  94.3 0.8 copy-start.6
  94.4 1.0 copy-start.7
  103.4 12.3 %collective-permute-start.20 = (bf16[8,8,128,128]{3,2,1,0:T(8,128)(2,1)}, bf16[8,8,128,128]{3,2,1,0:T(8,128)(2,1)}, u32[]{:S(2)}, u32[]{:S(2)}) collective-permute-start(bf16[8,8,128,128]{3,2,1,0:T(8,128)(2,1)} %shard_map.58), channel_id=1, source_target_pairs={{0,1},{1,0},{2,3},{3,2},{4,5},{5,4},{6,7},{7,6},{8,9},{9,8},{10,11... | collective-permute-start | bytes 6291464 | tf_op jit(solution)/shard_map/ppermute | solution.py:202
  106.0 1.4 copy-start.9
  181.7 7.1 %copy-start.14 = (f32[4096]{0:T(1024)S(1)}, f32[4096]{0:T(1024)}, u32[]{:S(2)}) copy-start(f32[4096]{0:T(1024)} %param.9) | copy-start | bytes 49156
  181.7 7.1 %copy-start.15 = (f32[4]{0:T(128)S(1)}, f32[4]{0:T(128)}, u32[]{:S(2)}) copy-start(f32[4]{0:T(128)} %param.8) | copy-start | bytes 52
  181.7 59.4 %all-to-all-start.1 = ((bf16[128,128,128]{2,1,0:T(8,128)(2,1)}), bf16[128,128,128]{2,1,0:T(8,128)(2,1)}, u32[]{:S(2)}, u32[]{:S(2)}) async-start(bf16[128,128,128]{2,1,0:T(8,128)(2,1)} %bitcast.13), calls=%async_computation.1 | async-start | bytes 8388608 | tf_op jit(solution)/shard_map/all_to_all | solution.py:235

commit v4 on v3

--- a/solution.py
+++ b/solution.py
@@ -8,7 +8,6 @@
 from jax.sharding import PartitionSpec as P
 
 TILE = 64
-CHUNKS = 1
 BF = jnp.bfloat16
 F32 = jnp.float32
 
@@ -149,37 +148,58 @@
     )(*a_shards, *b_shards, *extra)
 
 
-def finish_kernel(row_gap_ref, gap_ref, *refs):
-    directs, mirrors, out_ref = refs[:CHUNKS], refs[CHUNKS : 2 * CHUNKS], refs[-1]
+STEPS = 8
+
+
+def finish_kernel(row_gap_ref, gap_ref, direct_ref, mirror_ref, out_ref, direct_buf, mirror_buf, out_buf, sems, out_sem):
     eye = (
         lax.broadcasted_iota(jnp.int32, (128, 128), 0) == lax.broadcasted_iota(jnp.int32, (128, 128), 1)
     ).astype(BF)
+    step = mirror_ref.shape[0] // STEPS
     row_gap = row_gap_ref[...]
-    for e in range(directs[0].shape[0]):
-        direct = jnp.concatenate([ref[e] for ref in directs], axis=0).astype(F32)
-        mirror = jnp.concatenate([ref[e] for ref in mirrors], axis=0)
-        flipped = lax.dot_general(eye, mirror, (((1,), (1,)), ((), ())), preferred_element_type=F32)
-        span = slice(e * 128, (e + 1) * 128)
-        out_ref[:, span] = ((direct + flipped) / (row_gap + gap_ref[:, span])).astype(BF)
-
-
-def finish(row_gap, gap, directs, mirrors):
-    count, part, lanes = directs[0].shape
-    rows = part * CHUNKS
-    step = 16
-    piece = pl.BlockSpec((step, part, lanes), lambda n: (n, 0, 0))
+
+    def take(n, k):
+        span = pl.ds(n * step, step)
+        src, buf = ((direct_ref, direct_buf), (mirror_ref, mirror_buf))[k]
+        return pltpu.make_async_copy(src.at[span], buf.at[span], sems.at[k, n])
+
+    def give(n):
+        span = pl.ds(n * step * 128, step * 128)
+        return pltpu.make_async_copy(out_buf.at[:, span], out_ref.at[:, span], out_sem.at[n])
+
+    for n in range(STEPS):
+        take(n, 0).start()
+        take(n, 1).start()
+    for n in range(STEPS):
+        take(n, 0).wait()
+        take(n, 1).wait()
+        for e in range(n * step, (n + 1) * step):
+            flipped = lax.dot_general(eye, mirror_buf[e], (((1,), (1,)), ((), ())), preferred_element_type=F32)
+            span = slice(e * 128, (e + 1) * 128)
+            total = direct_buf[e].astype(F32) + flipped
+            out_buf[:, span] = (total / (row_gap + gap_ref[:, span])).astype(BF)
+        give(n).start()
+    for n in range(STEPS):
+        give(n).wait()
+
+
+def finish(row_gap, gap, direct, mirror):
+    count, rows, lanes = direct.shape
+    vmem, anywhere = pl.BlockSpec(memory_space=pltpu.VMEM), pl.BlockSpec(memory_space=pl.ANY)
     return pl.pallas_call(
         finish_kernel,
-        grid=(count // step,),
         out_shape=jax.ShapeDtypeStruct((rows, count * lanes), BF),
-        in_specs=[
-            pl.BlockSpec((rows, 1), lambda n: (0, 0)),
-            pl.BlockSpec((1, step * lanes), lambda n: (0, n)),
-        ]
-        + [piece] * (2 * CHUNKS),
-        out_specs=pl.BlockSpec((rows, step * lanes), lambda n: (0, n)),
-        compiler_params=pltpu.CompilerParams(vmem_limit_bytes=56 * 2**20),
-    )(row_gap.reshape(rows, 1), gap.reshape(1, count * lanes), *directs, *mirrors)
+        in_specs=[vmem, vmem, anywhere, anywhere],
+        out_specs=anywhere,
+        scratch_shapes=[
+            pltpu.VMEM(direct.shape, BF),
+            pltpu.VMEM(mirror.shape, BF),
+            pltpu.VMEM((rows, count * lanes), BF),
+            pltpu.SemaphoreType.DMA((2, STEPS)),
+            pltpu.SemaphoreType.DMA((STEPS,)),
+        ],
+        compiler_params=pltpu.CompilerParams(vmem_limit_bytes=58 * 2**20),
+    )(row_gap.reshape(rows, 1), gap.reshape(1, count * lanes), direct, mirror)
 
 
 def gate(values, others):
@@ -237,7 +257,7 @@
     gap = (virt_energy[None, :] - occ_energy[:, None]).reshape(-1)
     flat_place = row_place * 16 + col_place
     row_gap = lax.dynamic_slice_in_dim(gap, flat_place * 128, 128, 0)
-    return finish(row_gap, gap, [direct], [mirror])
+    return finish(row_gap, gap, direct, mirror)
 
 
 def solution(mesh):

time: 251 us -> 249 us (level)
  no operation moved by 1% of the time
where the time goes in v4:
time: 249 us; the launch traced here: 248 us
  waiting for transfers between devices  83.9 us (34%)
  blocking collectives  57.7 us (23%)
  starting transfers between devices  46.7 us (19%)
  Pallas kernels  40.7 us (16%)
  local copies, waits for them, and re-layouts  17.8 us (7%)
    all_to_all x1, blocking collectives, local(): lax.all_to_all(made, 'col', split_axis=0, concat_axis=0, tiled=True)  57.7 us
    all_to_all x1, waiting for transfers between devices, local(): lax.all_to_all(direct, ('row', 'col'), split_axis=0, concat_axis=0, tiled...  50.8 us
    ppermute x24, starting transfers between devices, local(): lax.ppermute(block, 'col' if len(pairs) == 16 else 'row', pairs)  39.6 us
    ppermute x24, waiting for transfers between devices, local(): lax.ppermute(block, 'col' if len(pairs) == 16 else 'row', pairs)  33.1 us
    pallas_call x4, Pallas kernels, product(): pl.pallas_call(functools.partial(product_kernel, j, h, taken is not None)...  32.7 us
    all_to_all x1, starting transfers between devices, local(): lax.all_to_all(direct, ('row', 'col'), split_axis=0, concat_axis=0, tiled...  7.05 us
    pallas_call x1, Pallas kernels, finish(): pl.pallas_call(finish_kernel, out_shape=jax.ShapeDtypeStruct((rows, count...  7 us
    unnamed x35, local copies, waits for them, and re-layouts  5.11 us
  transfers between devices with their start and end apart: 25, of which 7 were waited for; matrix products, arithmetic and copies ran while one was open for 5% of the time, Pallas kernels for 10%

profile of v4, /device:TPU:1, one launch (start us, length us, event | category | flops | bytes accessed | tf_op | source)
XLA Modules:
  0.0 248.4 jit_solution(12326591544052517412)
XLA Ops:
  0.0 2.1 constant_dynamic-slice_fusion
  2.1 1.4 collective-permute-start.5
  3.5 0.1 constant_dynamic-slice_fusion.1
  3.6 0.1 copy.15.mask_ref
  3.7 1.2 copy-done.2
  4.9 0.9 shard_map.55.refs_0_
  5.8 1.4 collective-permute-start.2
  7.2 1.6 collective-permute-start
  8.8 1.1 pad_maximum_fusion.refs_8_
  10.0 2.7 %collective-permute-start.10 = (bf16[2,256,1024]{2,1,0:T(8,128)(2,1)}, bf16[2,256,1024]{2,1,0:T(8,128)(2,1)}, u32[]{:S(2)}, u32[]{:S(2)}) collective-permute-start(bf16[2,256,1024]{2,1,0:T(8,128)(2,1)} %pad_maximum_fusion.refs_8_), channel_id=1, source_target_pairs={{0,96},{16,112},{32,0},{48,16},{64,32},{80,48},{96,64},{112,80},{1... | collective-permute-start | bytes 3145736 | tf_op jit(solution)/shard_map/ppermute | solution.py:222
  12.7 2.1 collective-permute-start.1
  14.9 0.0 collective-permute-start.9
  14.9 15.9 %collective-permute-done.2.refs_2_.refs_4_ = bf16[2,1024,256]{2,1,0:T(8,128)(2,1)} collective-permute-done((bf16[2,1024,256]{2,1,0:T(8,128)(2,1)S(1)}, bf16[2,1024,256]{2,1,0:T(8,128)(2,1)}, u32[]{:S(2)}, u32[]{:S(2)}) %collective-permute-start.2) | collective-permute-done | bytes 1048608 | tf_op jit(solution)/shard_map/ppermute | solution.py:222
  30.8 1.7 collective-permute-start.3
  32.5 1.9 collective-permute-done.refs_0_
  34.4 1.1 collective-permute-start.4
  35.5 0.0 collective-permute-done.10.refs_10_
  35.5 2.5 collective-permute-start.6
  38.0 1.9 slice.25
  39.8 0.0 collective-permute-done.1.refs_1_
  39.9 0.5 collective-permute-start.12
  40.4 9.1 %collective-permute-done.6.refs_4_.refs_12_ = bf16[1,256,1024]{2,1,0:T(8,128)(2,1)} collective-permute-done((bf16[1,256,1024]{2,1,0:T(8,128)(2,1)}, bf16[1,256,1024]{2,1,0:T(8,128)(2,1)}, u32[]{:S(2)}, u32[]{:S(2)}) %collective-permute-start.6) | collective-permute-done | bytes 524320 | tf_op jit(solution)/shard_map/ppermute | solution.py:222
  49.4 1.3 collective-permute-start.17
  50.7 1.4 collective-permute-start.16
  52.2 1.9 slice.24
  54.0 3.6 %collective-permute-done.3.refs_2_ = bf16[2,1024,256]{2,1,0:T(8,128)(2,1)} collective-permute-done((bf16[2,1024,256]{2,1,0:T(8,128)(2,1)}, bf16[2,1024,256]{2,1,0:T(8,128)(2,1)}, u32[]{:S(2)}, u32[]{:S(2)}) %collective-permute-start.3) | collective-permute-done | bytes 1048608 | tf_op jit(solution)/shard_map/ppermute | solution.py:222
  57.6 1.3 collective-permute-start.11
  58.9 1.0 collective-permute-done.4.refs_3_
  59.9 1.5 collective-permute-start.18
  61.4 1.1 slice.22
  62.5 1.1 slice.23
  63.6 0.0 collective-permute-done.12.refs_17_.refs_12_
  63.6 0.1 collective-permute-start.21
  63.7 0.0 collective-permute-done.17.refs_13_
  63.7 2.7 %collective-permute-start.22 = (bf16[1,1024,256]{2,1,0:T(8,128)(2,1)S(1)}, bf16[1,1024,256]{2,1,0:T(8,128)(2,1)S(1)}, u32[]{:S(2)}, u32[]{:S(2)}) collective-permute-start(bf16[1,1024,256]{2,1,0:T(8,128)(2,1)S(1)} %slice.23), channel_id=1, source_target_pairs={{0,12},{1,13},{2,14},{3,15},{4,0},{5,1},{6,2},{7,3},{8,4},{9,5},{1... | collective-permute-start | bytes 1572872 | tf_op jit(solution)/shard_map/ppermute | solution.py:222
  66.3 2.5 collective-permute-start.19
  68.8 1.9 slice.18
  70.7 1.9 slice.19
  72.6 1.7 collective-permute-done.18.refs_14_
  74.2 0.3 collective-permute-start.13
  74.6 0.0 collective-permute-done.11.refs_16_.refs_11_
  74.6 2.4 collective-permute-start.14
  76.9 0.0 collective-permute-done.21.refs_3_
  76.9 2.3 collective-permute-start.7
  79.2 2.5 collective-permute-start.15
  81.7 0.0 collective-permute-start.8
  81.7 0.8 copy-done.12
  82.5 8.0 %shard_map.59 = bf16[8,8,128,128]{3,2,1,0:T(8,128)(2,1)} custom-call(bf16[2,1024,256]{2,1,0:T(8,128)(2,1)} %copy-done.1, bf16[2,1024,256]{2,1,0:T(8,128)(2,1)} %get-tuple-element.12.refs_1_, bf16[2,1024,256]{2,1,0:T(8,128)(2,1)} %get-tuple-element.13.refs_2_, bf16[1,1024,256]{2,1,0:T(8,128)(2,1)} %copy-done.10, ...), custom_call_target="tpu_custom_call" | custom-call | flops 4294967296 | bytes 10485760 | tf_op jit(solution)/shard_map/pallas_call | solution.py:127
  90.6 3.8 %collective-permute-start.23 = (bf16[8,8,128,128]{3,2,1,0:T(8,128)(2,1)}, bf16[8,8,128,128]{3,2,1,0:T(8,128)(2,1)S(1)}, u32[]{:S(2)}, u32[]{:S(2)}) collective-permute-start(bf16[8,8,128,128]{3,2,1,0:T(8,128)(2,1)} %shard_map.59), channel_id=1, source_target_pairs={{0,1},{1,0},{2,3},{3,2},{4,5},{5,4},{6,7},{7,6},{8,9},{9,8},{10,11... | collective-permute-start | bytes 6291464 | tf_op jit(solution)/shard_map/ppermute | solution.py:222
  94.4 0.8 copy-done.6
  95.1 0.2 copy-done.7
  95.3 8.0 %shard_map.58 = bf16[8,8,128,128]{3,2,1,0:T(8,128)(2,1)} custom-call(bf16[2,1024,256]{2,1,0:T(8,128)(2,1)} %copy-done.1, bf16[2,1024,256]{2,1,0:T(8,128)(2,1)} %get-tuple-element.12.refs_1_, bf16[2,1024,256]{2,1,0:T(8,128)(2,1)} %get-tuple-element.13.refs_2_, bf16[1,1024,256]{2,1,0:T(8,128)(2,1)} %collective-permute-done.7.refs_3_, ...), custom_call_target="tpu_custom_call" | custom-call | flops 4294967296 | bytes 10485760 | tf_op jit(solution)/shard_map/pallas_call | solution.py:127
  103.4 2.6 %collective-permute-start.20 = (bf16[8,8,128,128]{3,2,1,0:T(8,128)(2,1)}, bf16[8,8,128,128]{3,2,1,0:T(8,128)(2,1)}, u32[]{:S(2)}, u32[]{:S(2)}) collective-permute-start(bf16[8,8,128,128]{3,2,1,0:T(8,128)(2,1)} %shard_map.58), channel_id=1, source_target_pairs={{0,1},{1,0},{2,3},{3,2},{4,5},{5,4},{6,7},{7,6},{8,9},{9,8},{10,11... | collective-permute-start | bytes 6291464 | tf_op jit(solution)/shard_map/ppermute | solution.py:222
  106.0 1.4 copy-done.9
  107.3 8.3 %shard_map.60.refs_17_ = bf16[16,8,128,128]{3,2,1,0:T(8,128)(2,1)} custom-call(bf16[2,1024,256]{2,1,0:T(8,128)(2,1)} %copy-done.1, bf16[2,1024,256]{2,1,0:T(8,128)(2,1)} %get-tuple-element.12.refs_1_, bf16[2,1024,256]{2,1,0:T(8,128)(2,1)} %get-tuple-element.13.refs_2_, bf16[1,1024,256]{2,1,0:T(8,128)(2,1)} %copy-done.10, ...), custom_call_target="tpu_custom_call" | custom-call | flops 4294967296 | bytes 10485760 | tf_op jit(solution)/shard_map/pallas_call | solution.py:127
  115.7 8.3 %shard_map.61 = bf16[16,8,128,128]{3,2,1,0:T(8,128)(2,1)} custom-call(bf16[2,1024,256]{2,1,0:T(8,128)(2,1)} %copy-done.1, bf16[2,1024,256]{2,1,0:T(8,128)(2,1)} %get-tuple-element.12.refs_1_, bf16[2,1024,256]{2,1,0:T(8,128)(2,1)} %get-tuple-element.13.refs_2_, bf16[1,1024,256]{2,1,0:T(8,128)(2,1)} %collective-permute-done.7.refs_3_, ...), custom_call_target="tpu_custom_call", output_to_operand_aliasing={{}: (17, {})} | custom-call | flops 4294967296 | bytes 10485760 | tf_op jit(solution)/shard_map/pallas_call | solution.py:127
  124.0 57.7 %all_to_all.10 = bf16[16,8,128,128]{3,2,1,0:T(8,128)(2,1)} all-to-all(bf16[16,8,128,128]{3,2,1,0:T(8,128)(2,1)} %shard_map.61), channel_id=1, replica_groups=mesh['row'=8,'col'=16] {'col'}, dimensions={0} | all-to-all | bytes 8388608 | tf_op jit(solution)/shard_map/all_to_all | solution.py:254
  181.7 7.1 %all-to-all-start.1 = ((bf16[128,128,128]{2,1,0:T(8,128)(2,1)}), bf16[128,128,128]{2,1,0:T(8,128)(2,1)}, u32[]{:S(2)}, u32[]{:S(2)}) async-start(bf16[128,128,128]{2,1,0:T(8,128)(2,1)} %bitcast.13), calls=%async_computation.1 | async-start | bytes 8388608 | tf_op jit(solution)/shard_map/all_to_all | solution.py:255
  188.8 0.1 subtract_bitcast_fusion
  188.9 0.1 dynamic-slice_bitcast_fusion.1
  189.0 0.7 copy.14.row_gap_ref
  189.7 0.7 copy.17
  190.4 50.8 %all-to-all-done.1.mirror_ref = bf16[128,128,128]{2,1,0:T(8,128)(2,1)} async-done(((bf16[128,128,128]{2,1,0:T(8,128)(2,1)}), bf16[128,128,128]{2,1,0:T(8,128)(2,1)}, u32[]{:S(2)}, u32[]{:S(2)}) %all-to-all-start.1) | async-done | bytes 4194336 | tf_op jit(solution)/shard_map/all_to_all | solution.py:255
  241.2 7.0 %shard_map.62 = bf16[128,16384]{1,0:T(8,128)(2,1)} custom-call(f32[128,1]{1,0:T(8,128)} %copy.14.row_gap_ref, f32[1,16384]{1,0:T(1,128)} %bitcast.17, bf16[128,128,128]{2,1,0:T(8,128)(2,1)} %bitcast.14, bf16[128,128,128]{2,1,0:T(8,128)(2,1)} %all-to-all-done.1.mirror_ref), custom_call_target="tpu_custom_call" | custom-call | tf_op jit(solution)/shard_map/pallas_call | solution.py:189
  (42 shorter events, 0.1 us)
Async XLA Ops:
  0.0 3.5 %copy-start = (s32[64,32]{0,1:T(8,128)S(1)}, s32[64,32]{0,1:T(8,128)}, u32[]{:S(2)}) copy-start(s32[64,32]{0,1:T(8,128)} %param.7) | copy-start | bytes 24580
  2.1 7.9 %copy-start.8 = (bf16[1,256,1024]{2,1,0:T(8,128)(2,1)}, bf16[1,256,1024]{2,1,0:T(8,128)(2,1)S(1)}, u32[]{:S(2)}) copy-start(bf16[1,256,1024]{2,1,0:T(8,128)(2,1)S(1)} %get-tuple-element.18.refs_0_) | copy-start | bytes 1572868
  2.1 6.8 %collective-permute-start.5 = (bf16[256,1024]{1,0:T(8,128)(2,1)}, bf16[256,1024]{1,0:T(8,128)(2,1)S(1)}, u32[]{:S(2)}, u32[]{:S(2)}) collective-permute-start(bf16[256,1024]{1,0:T(8,128)(2,1)} %get-tuple-element.17), channel_id=1, source_target_pairs={{0,1},{1,0},{2,3},{3,2},{4,5},{5,4},{6,7},{7,6},{8,9},{9,8},{10,11... | collective-permute-start | bytes 1572872 | tf_op jit(solution)/shard_map/ppermute | solution.py:222
  3.7 1.2 copy-start.2
  5.8 55.6 %copy-start.1 = (bf16[2,1024,256]{2,1,0:T(8,128)(2,1)}, bf16[2,1024,256]{2,1,0:T(8,128)(2,1)S(1)}, u32[]{:S(2)}) copy-start(bf16[2,1024,256]{2,1,0:T(8,128)(2,1)S(1)} %shard_map.55.refs_0_) | copy-start | bytes 3145732
  5.8 24.9 %collective-permute-start.2 = (bf16[2,1024,256]{2,1,0:T(8,128)(2,1)S(1)}, bf16[2,1024,256]{2,1,0:T(8,128)(2,1)}, u32[]{:S(2)}, u32[]{:S(2)}) collective-permute-start(bf16[2,1024,256]{2,1,0:T(8,128)(2,1)S(1)} %shard_map.55.refs_0_), channel_id=1, source_target_pairs={{0,2},{1,3},{2,0},{3,1},{4,6},{5,7},{6,4},{7,5},{8,10},{9,11},{10,... | collective-permute-start | bytes 3145736 | tf_op jit(solution)/shard_map/ppermute | solution.py:222
  7.2 27.2 %collective-permute-start = (bf16[2,1024,256]{2,1,0:T(8,128)(2,1)S(1)}, bf16[2,1024,256]{2,1,0:T(8,128)(2,1)S(1)}, u32[]{:S(2)}, u32[]{:S(2)}) collective-permute-start(bf16[2,1024,256]{2,1,0:T(8,128)(2,1)S(1)} %shard_map.55.refs_0_), channel_id=1, source_target_pairs={{0,4},{1,5},{2,6},{3,7},{4,8},{5,9},{6,10},{7,11},{8,12},{9,13},{1... | collective-permute-start | bytes 3145736 | tf_op jit(solution)/shard_map/ppermute | solution.py:222
  8.8 1.2 copy-start.13
  10.0 25.5 %collective-permute-start.10 = (bf16[2,256,1024]{2,1,0:T(8,128)(2,1)}, bf16[2,256,1024]{2,1,0:T(8,128)(2,1)}, u32[]{:S(2)}, u32[]{:S(2)}) collective-permute-start(bf16[2,256,1024]{2,1,0:T(8,128)(2,1)} %pad_maximum_fusion.refs_8_), channel_id=1, source_target_pairs={{0,96},{16,112},{32,0},{48,16},{64,32},{80,48},{96,64},{112,80},{1... | collective-permute-start | bytes 3145736 | tf_op jit(solution)/shard_map/ppermute | solution.py:222
  12.7 27.1 %collective-permute-start.1 = (bf16[2,1024,256]{2,1,0:T(8,128)(2,1)S(1)}, bf16[2,1024,256]{2,1,0:T(8,128)(2,1)S(1)}, u32[]{:S(2)}, u32[]{:S(2)}) collective-permute-start(bf16[2,1024,256]{2,1,0:T(8,128)(2,1)S(1)} %shard_map.55.refs_0_), channel_id=1, source_target_pairs={{0,12},{1,13},{2,14},{3,15},{4,0},{5,1},{6,2},{7,3},{8,4},{9,5},{1... | collective-permute-start | bytes 3145736 | tf_op jit(solution)/shard_map/ppermute | solution.py:222
  14.9 35.9 %collective-permute-start.9 = (bf16[2,256,1024]{2,1,0:T(8,128)(2,1)}, bf16[2,256,1024]{2,1,0:T(8,128)(2,1)}, u32[]{:S(2)}, u32[]{:S(2)}) collective-permute-start(bf16[2,256,1024]{2,1,0:T(8,128)(2,1)} %pad_maximum_fusion.refs_8_), channel_id=1, source_target_pairs={{0,32},{16,48},{32,64},{48,80},{64,96},{80,112},{96,0},{112,16},{1... | collective-permute-start | bytes 3145736 | tf_op jit(solution)/shard_map/ppermute | solution.py:222
  30.8 26.9 %collective-permute-start.3 = (bf16[2,1024,256]{2,1,0:T(8,128)(2,1)}, bf16[2,1024,256]{2,1,0:T(8,128)(2,1)}, u32[]{:S(2)}, u32[]{:S(2)}) collective-permute-start(bf16[2,1024,256]{2,1,0:T(8,128)(2,1)} %collective-permute-done.2.refs_2_.refs_4_), channel_id=1, source_target_pairs={{0,4},{1,5},{2,6},{3,7},{4,8},{5,9},{6,10},{7,11},{8,12},{9,13},{1... | collective-permute-start | bytes 3145736 | tf_op jit(solution)/shard_map/ppermute | solution.py:222
  34.4 27.0 %copy-start.3 = (bf16[2,1024,256]{2,1,0:T(8,128)(2,1)}, bf16[2,1024,256]{2,1,0:T(8,128)(2,1)S(1)}, u32[]{:S(2)}) copy-start(bf16[2,1024,256]{2,1,0:T(8,128)(2,1)S(1)} %collective-permute-done.refs_0_) | copy-start | bytes 3145732
  34.4 25.6 %collective-permute-start.4 = (bf16[2,1024,256]{2,1,0:T(8,128)(2,1)}, bf16[2,1024,256]{2,1,0:T(8,128)(2,1)}, u32[]{:S(2)}, u32[]{:S(2)}) collective-permute-start(bf16[2,1024,256]{2,1,0:T(8,128)(2,1)} %collective-permute-done.2.refs_2_.refs_4_), channel_id=1, source_target_pairs={{0,12},{1,13},{2,14},{3,15},{4,0},{5,1},{6,2},{7,3},{8,4},{9,5},{1... | collective-permute-start | bytes 3145736 | tf_op jit(solution)/shard_map/ppermute | solution.py:222
  35.5 13.9 %collective-permute-start.6 = (bf16[1,256,1024]{2,1,0:T(8,128)(2,1)}, bf16[1,256,1024]{2,1,0:T(8,128)(2,1)}, u32[]{:S(2)}, u32[]{:S(2)}) collective-permute-start(bf16[1,256,1024]{2,1,0:T(8,128)(2,1)} %get-tuple-element.11), channel_id=1, source_target_pairs={{0,16},{16,0},{32,48},{48,32},{64,80},{80,64},{96,112},{112,96},{1... | collective-permute-start | bytes 1572872 | tf_op jit(solution)/shard_map/ppermute | solution.py:222
  39.8 21.6 %copy-start.4 = (bf16[2,1024,256]{2,1,0:T(8,128)(2,1)}, bf16[2,1024,256]{2,1,0:T(8,128)(2,1)S(1)}, u32[]{:S(2)}) copy-start(bf16[2,1024,256]{2,1,0:T(8,128)(2,1)S(1)} %collective-permute-done.1.refs_1_) | copy-start | bytes 3145732
  39.9 23.7 %collective-permute-start.12 = (bf16[1,256,1024]{2,1,0:T(8,128)(2,1)}, bf16[1,256,1024]{2,1,0:T(8,128)(2,1)}, u32[]{:S(2)}, u32[]{:S(2)}) collective-permute-start(bf16[1,256,1024]{2,1,0:T(8,128)(2,1)} %get-tuple-element.16), channel_id=1, source_target_pairs={{0,16},{16,0},{32,48},{48,32},{64,80},{80,64},{96,112},{112,96},{1... | collective-permute-start | bytes 1572872 | tf_op jit(solution)/shard_map/ppermute | solution.py:222
  49.4 14.2 %collective-permute-start.17 = (bf16[1,256,1024]{2,1,0:T(8,128)(2,1)}, bf16[1,256,1024]{2,1,0:T(8,128)(2,1)}, u32[]{:S(2)}, u32[]{:S(2)}) collective-permute-start(bf16[1,256,1024]{2,1,0:T(8,128)(2,1)} %collective-permute-done.6.refs_4_.refs_12_), channel_id=1, source_target_pairs={{0,32},{16,48},{32,64},{48,80},{64,96},{80,112},{96,0},{112,16},{1... | collective-permute-start | bytes 1572872 | tf_op jit(solution)/shard_map/ppermute | solution.py:222
  50.7 15.6 %collective-permute-start.16 = (bf16[1,256,1024]{2,1,0:T(8,128)(2,1)}, bf16[1,256,1024]{2,1,0:T(8,128)(2,1)}, u32[]{:S(2)}, u32[]{:S(2)}) collective-permute-start(bf16[1,256,1024]{2,1,0:T(8,128)(2,1)} %slice.25), channel_id=1, source_target_pairs={{0,96},{16,112},{32,0},{48,16},{64,32},{80,48},{96,64},{112,80},{1... | collective-permute-start | bytes 1572872 | tf_op jit(solution)/shard_map/ppermute | solution.py:222
  57.6 16.9 %collective-permute-start.11 = (bf16[1,256,1024]{2,1,0:T(8,128)(2,1)}, bf16[1,256,1024]{2,1,0:T(8,128)(2,1)}, u32[]{:S(2)}, u32[]{:S(2)}) collective-permute-start(bf16[1,256,1024]{2,1,0:T(8,128)(2,1)} %slice.24), channel_id=1, source_target_pairs={{0,32},{16,48},{32,64},{48,80},{64,96},{80,112},{96,0},{112,16},{1... | collective-permute-start | bytes 1572872 | tf_op jit(solution)/shard_map/ppermute | solution.py:222
  59.9 14.3 %collective-permute-start.18 = (bf16[1,256,1024]{2,1,0:T(8,128)(2,1)}, bf16[1,256,1024]{2,1,0:T(8,128)(2,1)}, u32[]{:S(2)}, u32[]{:S(2)}) collective-permute-start(bf16[1,256,1024]{2,1,0:T(8,128)(2,1)} %collective-permute-done.6.refs_4_.refs_12_), channel_id=1, source_target_pairs={{0,96},{16,112},{32,0},{48,16},{64,32},{80,48},{96,64},{112,80},{1... | collective-permute-start | bytes 1572872 | tf_op jit(solution)/shard_map/ppermute | solution.py:222
  63.6 13.4 %collective-permute-start.21 = (bf16[1,1024,256]{2,1,0:T(8,128)(2,1)S(1)}, bf16[1,1024,256]{2,1,0:T(8,128)(2,1)S(1)}, u32[]{:S(2)}, u32[]{:S(2)}) collective-permute-start(bf16[1,1024,256]{2,1,0:T(8,128)(2,1)S(1)} %slice.22), channel_id=1, source_target_pairs={{0,4},{1,5},{2,6},{3,7},{4,8},{5,9},{6,10},{7,11},{8,12},{9,13},{1... | collective-permute-start | bytes 1572872 | tf_op jit(solution)/shard_map/ppermute | solution.py:222
  63.7 15.6 %collective-permute-start.22 = (bf16[1,1024,256]{2,1,0:T(8,128)(2,1)S(1)}, bf16[1,1024,256]{2,1,0:T(8,128)(2,1)S(1)}, u32[]{:S(2)}, u32[]{:S(2)}) collective-permute-start(bf16[1,1024,256]{2,1,0:T(8,128)(2,1)S(1)} %slice.23), channel_id=1, source_target_pairs={{0,12},{1,13},{2,14},{3,15},{4,0},{5,1},{6,2},{7,3},{8,4},{9,5},{1... | collective-permute-start | bytes 1572872 | tf_op jit(solution)/shard_map/ppermute | solution.py:222
  66.3 15.4 %collective-permute-start.19 = (bf16[1,256,1024]{2,1,0:T(8,128)(2,1)}, bf16[1,256,1024]{2,1,0:T(8,128)(2,1)S(1)}, u32[]{:S(2)}, u32[]{:S(2)}) collective-permute-start(bf16[1,256,1024]{2,1,0:T(8,128)(2,1)} %collective-permute-done.16.refs_11_), channel_id=1, source_target_pairs={{0,16},{16,0},{32,48},{48,32},{64,80},{80,64},{96,112},{112,96},{1... | collective-permute-start | bytes 1572872 | tf_op jit(solution)/shard_map/ppermute | solution.py:222
  74.2 16.3 %collective-permute-start.13 = (bf16[1,256,1024]{2,1,0:T(8,128)(2,1)}, bf16[1,256,1024]{2,1,0:T(8,128)(2,1)S(1)}, u32[]{:S(2)}, u32[]{:S(2)}) collective-permute-start(bf16[1,256,1024]{2,1,0:T(8,128)(2,1)} %collective-permute-done.12.refs_17_.refs_12_), channel_id=1, source_target_pairs={{0,32},{16,48},{32,64},{48,80},{64,96},{80,112},{96,0},{112,16},{1... | collective-permute-start | bytes 1572872 | tf_op jit(solution)/shard_map/ppermute | solution.py:222
  74.6 19.8 %collective-permute-start.14 = (bf16[1,256,1024]{2,1,0:T(8,128)(2,1)}, bf16[1,256,1024]{2,1,0:T(8,128)(2,1)S(1)}, u32[]{:S(2)}, u32[]{:S(2)}) collective-permute-start(bf16[1,256,1024]{2,1,0:T(8,128)(2,1)} %collective-permute-done.12.refs_17_.refs_12_), channel_id=1, source_target_pairs={{0,96},{16,112},{32,0},{48,16},{64,32},{80,48},{96,64},{112,80},{1... | collective-permute-start | bytes 1572872 | tf_op jit(solution)/shard_map/ppermute | solution.py:222
  76.9 4.8 %copy-start.10 = (bf16[1,1024,256]{2,1,0:T(8,128)(2,1)}, bf16[1,1024,256]{2,1,0:T(8,128)(2,1)S(1)}, u32[]{:S(2)}) copy-start(bf16[1,1024,256]{2,1,0:T(8,128)(2,1)S(1)} %collective-permute-done.21.refs_3_) | copy-start | bytes 1572868
  76.9 17.4 %collective-permute-start.7 = (bf16[1,1024,256]{2,1,0:T(8,128)(2,1)}, bf16[1,1024,256]{2,1,0:T(8,128)(2,1)}, u32[]{:S(2)}, u32[]{:S(2)}) collective-permute-start(bf16[1,1024,256]{2,1,0:T(8,128)(2,1)} %slice.18), channel_id=1, source_target_pairs={{0,12},{1,13},{2,14},{3,15},{4,0},{5,1},{6,2},{7,3},{8,4},{9,5},{1... | collective-permute-start | bytes 1572872 | tf_op jit(solution)/shard_map/ppermute | solution.py:222
  79.2 2.5 copy-start.11
  79.2 15.1 %collective-permute-start.15 = (bf16[1,256,1024]{2,1,0:T(8,128)(2,1)}, bf16[1,256,1024]{2,1,0:T(8,128)(2,1)S(1)}, u32[]{:S(2)}, u32[]{:S(2)}) collective-permute-start(bf16[1,256,1024]{2,1,0:T(8,128)(2,1)} %collective-permute-done.11.refs_16_.refs_11_), channel_id=1, source_target_pairs={{0,16},{16,0},{32,48},{48,32},{64,80},{80,64},{96,112},{112,96},{1... | collective-permute-start | bytes 1572872 | tf_op jit(solution)/shard_map/ppermute | solution.py:222
  81.7 0.8 copy-start.12
  81.7 12.7 %collective-permute-start.8 = (bf16[1,1024,256]{2,1,0:T(8,128)(2,1)}, bf16[1,1024,256]{2,1,0:T(8,128)(2,1)}, u32[]{:S(2)}, u32[]{:S(2)}) collective-permute-start(bf16[1,1024,256]{2,1,0:T(8,128)(2,1)} %slice.19), channel_id=1, source_target_pairs={{0,4},{1,5},{2,6},{3,7},{4,8},{5,9},{6,10},{7,11},{8,12},{9,13},{1... | collective-permute-start | bytes 1572872 | tf_op jit(solution)/shard_map/ppermute | solution.py:222
  90.6 3.8 %copy-start.5 = (bf16[1,256,1024]{2,1,0:T(8,128)(2,1)}, bf16[1,256,1024]{2,1,0:T(8,128)(2,1)S(1)}, u32[]{:S(2)}) copy-start(bf16[1,256,1024]{2,1,0:T(8,128)(2,1)S(1)} %collective-permute-done.13.refs_17_.refs_13_) | copy-start | bytes 1572868
  90.6 15.4 %collective-permute-start.23 = (bf16[8,8,128,128]{3,2,1,0:T(8,128)(2,1)}, bf16[8,8,128,128]{3,2,1,0:T(8,128)(2,1)S(1)}, u32[]{:S(2)}, u32[]{:S(2)}) collective-permute-start(bf16[8,8,128,128]{3,2,1,0:T(8,128)(2,1)} %shard_map.59), channel_id=1, source_target_pairs={{0,1},{1,0},{2,3},{3,2},{4,5},{5,4},{6,7},{7,6},{8,9},{9,8},{10,11... | collective-permute-start | bytes 6291464 | tf_op jit(solution)/shard_map/ppermute | solution.py:222
  94.3 0.8 copy-start.6
  94.4 1.0 copy-start.7
  103.4 12.3 %collective-permute-start.20 = (bf16[8,8,128,128]{3,2,1,0:T(8,128)(2,1)}, bf16[8,8,128,128]{3,2,1,0:T(8,128)(2,1)}, u32[]{:S(2)}, u32[]{:S(2)}) collective-permute-start(bf16[8,8,128,128]{3,2,1,0:T(8,128)(2,1)} %shard_map.58), channel_id=1, source_target_pairs={{0,1},{1,0},{2,3},{3,2},{4,5},{5,4},{6,7},{7,6},{8,9},{9,8},{10,11... | collective-permute-start | bytes 6291464 | tf_op jit(solution)/shard_map/ppermute | solution.py:222
  106.0 1.4 copy-start.9
  181.7 7.1 %copy-start.14 = (f32[4096]{0:T(1024)S(1)}, f32[4096]{0:T(1024)}, u32[]{:S(2)}) copy-start(f32[4096]{0:T(1024)} %param.9) | copy-start | bytes 49156
  181.7 7.1 %copy-start.15 = (f32[4]{0:T(128)S(1)}, f32[4]{0:T(128)}, u32[]{:S(2)}) copy-start(f32[4]{0:T(128)} %param.8) | copy-start | bytes 52
  181.7 59.5 %all-to-all-start.1 = ((bf16[128,128,128]{2,1,0:T(8,128)(2,1)}), bf16[128,128,128]{2,1,0:T(8,128)(2,1)}, u32[]{:S(2)}, u32[]{:S(2)}) async-start(bf16[128,128,128]{2,1,0:T(8,128)(2,1)} %bitcast.13), calls=%async_computation.1 | async-start | bytes 8388608 | tf_op jit(solution)/shard_map/all_to_all | solution.py:255

commit v5 on v4

--- a/solution.py
+++ b/solution.py
@@ -84,13 +84,20 @@
     def b_copy(src, spot):
         return pltpu.make_async_copy(src, b_buf.at[spot], b_sem.at[spot])
 
-    for t in range(8):
-        a_copy(t).start()
-        side, offset = t // 4, (0, -1, 1, 2)[t % 4]
-        apart = (y + offset - z + 8) % 4
-        slot = jnp.where(apart == 1, 2, jnp.where(apart == 2, 3, jnp.where(apart == 3, 1, 0)))
-        place = ((xh + xl + side) % 2) * 4 + slot
-        b_copy(b_refs[t].at[h if b_refs[t].shape[0] == 2 else 0], place).start()
+    places = []
+    for side in range(2):
+        for offset in (0, -1, 1, 2):
+            apart = (y + offset - z + 8) % 4
+            slot = jnp.where(apart == 1, 2, jnp.where(apart == 2, 3, jnp.where(apart == 3, 1, 0)))
+            places.append(((xh + xl + side) % 2) * 4 + slot)
+
+    def start_b(t, u):
+        pl.when(places[t] == u)(lambda: b_copy(b_refs[t].at[h if b_refs[t].shape[0] == 2 else 0], u).start())
+
+    for u in range(8):
+        a_copy(u).start()
+        for t in range(8):
+            start_b(t, u)
     if taken:
         pltpu.make_async_copy(refs[16], taken_buf, t_sem).start()
     for t in range(0, 8, group):

time: 249 us -> 246 us (0.988)
  blocking collectives: 57.7 us -> 53.6 us
  Pallas kernels: 40.7 us -> 43.2 us
    all_to_all x1, blocking collectives: 57.7 us -> 53.6 us  [local(): lax.all_to_all(made, 'col', split_axis=0, concat_axis=0, tiled=True)]
    pallas_call x4, Pallas kernels: 32.7 us -> 35.3 us  [product(): pl.pallas_call(functools.partial(product_kernel, j, h, taken is not None)...]
  transfers between devices with their start and end apart: 25 -> 25, of which waited for: 7 -> 7; matrix products, arithmetic and copies ran while one was open for 5% -> 5% of each run, Pallas kernels for 10% -> 11%
where the time goes in v5:
time: 246 us; the launch traced here: 245 us
  waiting for transfers between devices  84 us (34%)
  blocking collectives  53.6 us (22%)
  starting transfers between devices  44.9 us (18%)
  Pallas kernels  43.2 us (18%)
  local copies, waits for them, and re-layouts  17.8 us (7%)
    all_to_all x1, blocking collectives, local(): lax.all_to_all(made, 'col', split_axis=0, concat_axis=0, tiled=True)  53.6 us
    all_to_all x1, waiting for transfers between devices, local(): lax.all_to_all(direct, ('row', 'col'), split_axis=0, concat_axis=0, tiled...  50.9 us
    ppermute x24, starting transfers between devices, local(): lax.ppermute(block, 'col' if len(pairs) == 16 else 'row', pairs)  39 us
    pallas_call x4, Pallas kernels, product(): pl.pallas_call(functools.partial(product_kernel, j, h, taken is not None)...  35.3 us
    ppermute x24, waiting for transfers between devices, local(): lax.ppermute(block, 'col' if len(pairs) == 16 else 'row', pairs)  33.1 us
    pallas_call x1, Pallas kernels, finish(): pl.pallas_call(finish_kernel, out_shape=jax.ShapeDtypeStruct((rows, count...  7 us
    all_to_all x1, starting transfers between devices, local(): lax.all_to_all(direct, ('row', 'col'), split_axis=0, concat_axis=0, tiled...  5.85 us
    unnamed x35, local copies, waits for them, and re-layouts  5.11 us
  transfers between devices with their start and end apart: 25, of which 7 were waited for; matrix products, arithmetic and copies ran while one was open for 5% of the time, Pallas kernels for 11%

profile of v5, /device:TPU:1, one launch (start us, length us, event | category | flops | bytes accessed | tf_op | source)
XLA Modules:
  0.0 245.2 jit_solution(15460403111972102940)
XLA Ops:
  0.0 2.1 constant_dynamic-slice_fusion
  2.1 1.4 collective-permute-start.5
  3.5 0.1 constant_dynamic-slice_fusion.1
  3.6 0.1 copy.15.mask_ref
  3.7 1.2 copy-done.2
  4.9 0.9 shard_map.55.refs_0_
  5.8 1.4 collective-permute-start.2
  7.2 1.6 collective-permute-start
  8.8 1.1 pad_maximum_fusion.refs_8_
  10.0 2.7 %collective-permute-start.10 = (bf16[2,256,1024]{2,1,0:T(8,128)(2,1)}, bf16[2,256,1024]{2,1,0:T(8,128)(2,1)}, u32[]{:S(2)}, u32[]{:S(2)}) collective-permute-start(bf16[2,256,1024]{2,1,0:T(8,128)(2,1)} %pad_maximum_fusion.refs_8_), channel_id=1, source_target_pairs={{0,96},{16,112},{32,0},{48,16},{64,32},{80,48},{96,64},{112,80},{1... | collective-permute-start | bytes 3145736 | tf_op jit(solution)/shard_map/ppermute | solution.py:229
  12.7 2.1 collective-permute-start.1
  14.9 0.0 collective-permute-start.9
  14.9 15.9 %collective-permute-done.2.refs_2_.refs_4_ = bf16[2,1024,256]{2,1,0:T(8,128)(2,1)} collective-permute-done((bf16[2,1024,256]{2,1,0:T(8,128)(2,1)S(1)}, bf16[2,1024,256]{2,1,0:T(8,128)(2,1)}, u32[]{:S(2)}, u32[]{:S(2)}) %collective-permute-start.2) | collective-permute-done | bytes 1048608 | tf_op jit(solution)/shard_map/ppermute | solution.py:229
  30.8 1.7 collective-permute-start.3
  32.5 1.9 collective-permute-done.refs_0_
  34.4 1.1 collective-permute-start.4
  35.5 0.0 collective-permute-done.10.refs_10_
  35.5 2.5 collective-permute-start.6
  38.0 1.9 slice.25
  39.8 0.0 collective-permute-done.1.refs_1_
  39.9 0.5 collective-permute-start.12
  40.4 9.1 %collective-permute-done.6.refs_4_.refs_12_ = bf16[1,256,1024]{2,1,0:T(8,128)(2,1)} collective-permute-done((bf16[1,256,1024]{2,1,0:T(8,128)(2,1)}, bf16[1,256,1024]{2,1,0:T(8,128)(2,1)}, u32[]{:S(2)}, u32[]{:S(2)}) %collective-permute-start.6) | collective-permute-done | bytes 524320 | tf_op jit(solution)/shard_map/ppermute | solution.py:229
  49.4 1.3 collective-permute-start.17
  50.7 1.4 collective-permute-start.16
  52.2 1.9 slice.24
  54.0 3.6 %collective-permute-done.3.refs_2_ = bf16[2,1024,256]{2,1,0:T(8,128)(2,1)} collective-permute-done((bf16[2,1024,256]{2,1,0:T(8,128)(2,1)}, bf16[2,1024,256]{2,1,0:T(8,128)(2,1)}, u32[]{:S(2)}, u32[]{:S(2)}) %collective-permute-start.3) | collective-permute-done | bytes 1048608 | tf_op jit(solution)/shard_map/ppermute | solution.py:229
  57.6 1.3 collective-permute-start.11
  58.9 1.0 collective-permute-done.4.refs_3_
  59.9 1.5 collective-permute-start.18
  61.4 1.1 slice.22
  62.5 1.1 slice.23
  63.6 0.0 collective-permute-done.12.refs_17_.refs_12_
  63.6 0.1 collective-permute-start.21
  63.7 0.0 collective-permute-done.17.refs_13_
  63.7 2.7 %collective-permute-start.22 = (bf16[1,1024,256]{2,1,0:T(8,128)(2,1)S(1)}, bf16[1,1024,256]{2,1,0:T(8,128)(2,1)S(1)}, u32[]{:S(2)}, u32[]{:S(2)}) collective-permute-start(bf16[1,1024,256]{2,1,0:T(8,128)(2,1)S(1)} %slice.23), channel_id=1, source_target_pairs={{0,12},{1,13},{2,14},{3,15},{4,0},{5,1},{6,2},{7,3},{8,4},{9,5},{1... | collective-permute-start | bytes 1572872 | tf_op jit(solution)/shard_map/ppermute | solution.py:229
  66.3 2.5 collective-permute-start.19
  68.8 1.9 slice.18
  70.7 1.9 slice.19
  72.6 1.7 collective-permute-done.18.refs_14_
  74.2 0.3 collective-permute-start.13
  74.6 2.4 collective-permute-start.14
  76.9 0.0 collective-permute-done.21.refs_3_
  76.9 2.3 collective-permute-start.7
  79.2 0.0 collective-permute-done.22.refs_7_
  79.2 2.5 collective-permute-start.15
  81.7 0.0 collective-permute-start.8
  81.7 0.8 copy-done.12
  82.5 8.7 %shard_map.59 = bf16[8,8,128,128]{3,2,1,0:T(8,128)(2,1)} custom-call(bf16[2,1024,256]{2,1,0:T(8,128)(2,1)} %copy-done.1, bf16[2,1024,256]{2,1,0:T(8,128)(2,1)} %get-tuple-element.12.refs_1_, bf16[2,1024,256]{2,1,0:T(8,128)(2,1)} %get-tuple-element.13.refs_2_, bf16[1,1024,256]{2,1,0:T(8,128)(2,1)} %copy-done.10, ...), custom_call_target="tpu_custom_call" | custom-call | flops 4294967296 | bytes 10485760 | tf_op jit(solution)/shard_map/pallas_call | solution.py:134
  91.2 3.8 %collective-permute-start.23 = (bf16[8,8,128,128]{3,2,1,0:T(8,128)(2,1)}, bf16[8,8,128,128]{3,2,1,0:T(8,128)(2,1)S(1)}, u32[]{:S(2)}, u32[]{:S(2)}) collective-permute-start(bf16[8,8,128,128]{3,2,1,0:T(8,128)(2,1)} %shard_map.59), channel_id=1, source_target_pairs={{0,1},{1,0},{2,3},{3,2},{4,5},{5,4},{6,7},{7,6},{8,9},{9,8},{10,11... | collective-permute-start | bytes 6291464 | tf_op jit(solution)/shard_map/ppermute | solution.py:229
  95.0 0.8 copy-done.6
  95.8 0.2 copy-done.7
  96.0 8.7 %shard_map.58 = bf16[8,8,128,128]{3,2,1,0:T(8,128)(2,1)} custom-call(bf16[2,1024,256]{2,1,0:T(8,128)(2,1)} %copy-done.1, bf16[2,1024,256]{2,1,0:T(8,128)(2,1)} %get-tuple-element.12.refs_1_, bf16[2,1024,256]{2,1,0:T(8,128)(2,1)} %get-tuple-element.13.refs_2_, bf16[1,1024,256]{2,1,0:T(8,128)(2,1)} %collective-permute-done.7.refs_3_, ...), custom_call_target="tpu_custom_call" | custom-call | flops 4294967296 | bytes 10485760 | tf_op jit(solution)/shard_map/pallas_call | solution.py:134
  104.6 2.0 collective-permute-start.20
  106.6 1.4 copy-done.9
  108.0 8.9 %shard_map.60.refs_17_ = bf16[16,8,128,128]{3,2,1,0:T(8,128)(2,1)} custom-call(bf16[2,1024,256]{2,1,0:T(8,128)(2,1)} %copy-done.1, bf16[2,1024,256]{2,1,0:T(8,128)(2,1)} %get-tuple-element.12.refs_1_, bf16[2,1024,256]{2,1,0:T(8,128)(2,1)} %get-tuple-element.13.refs_2_, bf16[1,1024,256]{2,1,0:T(8,128)(2,1)} %copy-done.10, ...), custom_call_target="tpu_custom_call" | custom-call | flops 4294967296 | bytes 10485760 | tf_op jit(solution)/shard_map/pallas_call | solution.py:134
  117.0 9.0 %shard_map.61 = bf16[16,8,128,128]{3,2,1,0:T(8,128)(2,1)} custom-call(bf16[2,1024,256]{2,1,0:T(8,128)(2,1)} %copy-done.1, bf16[2,1024,256]{2,1,0:T(8,128)(2,1)} %get-tuple-element.12.refs_1_, bf16[2,1024,256]{2,1,0:T(8,128)(2,1)} %get-tuple-element.13.refs_2_, bf16[1,1024,256]{2,1,0:T(8,128)(2,1)} %collective-permute-done.7.refs_3_, ...), custom_call_target="tpu_custom_call", output_to_operand_aliasing={{}: (17, {})} | custom-call | flops 4294967296 | bytes 10485760 | tf_op jit(solution)/shard_map/pallas_call | solution.py:134
  126.0 53.6 %all_to_all.10 = bf16[16,8,128,128]{3,2,1,0:T(8,128)(2,1)} all-to-all(bf16[16,8,128,128]{3,2,1,0:T(8,128)(2,1)} %shard_map.61), channel_id=1, replica_groups=mesh['row'=8,'col'=16] {'col'}, dimensions={0} | all-to-all | bytes 8388608 | tf_op jit(solution)/shard_map/all_to_all | solution.py:261
  179.6 5.9 %all-to-all-start.1 = ((bf16[128,128,128]{2,1,0:T(8,128)(2,1)}), bf16[128,128,128]{2,1,0:T(8,128)(2,1)}, u32[]{:S(2)}, u32[]{:S(2)}) async-start(bf16[128,128,128]{2,1,0:T(8,128)(2,1)} %bitcast.13), calls=%async_computation.1 | async-start | bytes 8388608 | tf_op jit(solution)/shard_map/all_to_all | solution.py:262
  185.5 0.1 subtract_bitcast_fusion
  185.6 0.1 dynamic-slice_bitcast_fusion.1
  185.7 0.7 copy.14.row_gap_ref
  186.4 0.7 copy.17
  187.1 50.9 %all-to-all-done.1.mirror_ref = bf16[128,128,128]{2,1,0:T(8,128)(2,1)} async-done(((bf16[128,128,128]{2,1,0:T(8,128)(2,1)}), bf16[128,128,128]{2,1,0:T(8,128)(2,1)}, u32[]{:S(2)}, u32[]{:S(2)}) %all-to-all-start.1) | async-done | bytes 4194336 | tf_op jit(solution)/shard_map/all_to_all | solution.py:262
  238.0 7.0 %shard_map.62 = bf16[128,16384]{1,0:T(8,128)(2,1)} custom-call(f32[128,1]{1,0:T(8,128)} %copy.14.row_gap_ref, f32[1,16384]{1,0:T(1,128)} %bitcast.17, bf16[128,128,128]{2,1,0:T(8,128)(2,1)} %bitcast.14, bf16[128,128,128]{2,1,0:T(8,128)(2,1)} %all-to-all-done.1.mirror_ref), custom_call_target="tpu_custom_call" | custom-call | tf_op jit(solution)/shard_map/pallas_call | solution.py:196
  (42 shorter events, 0.1 us)
Async XLA Ops:
  0.0 3.5 %copy-start = (s32[64,32]{0,1:T(8,128)S(1)}, s32[64,32]{0,1:T(8,128)}, u32[]{:S(2)}) copy-start(s32[64,32]{0,1:T(8,128)} %param.7) | copy-start | bytes 24580
  2.1 7.9 %copy-start.8 = (bf16[1,256,1024]{2,1,0:T(8,128)(2,1)}, bf16[1,256,1024]{2,1,0:T(8,128)(2,1)S(1)}, u32[]{:S(2)}) copy-start(bf16[1,256,1024]{2,1,0:T(8,128)(2,1)S(1)} %get-tuple-element.18.refs_0_) | copy-start | bytes 1572868
  2.1 6.8 %collective-permute-start.5 = (bf16[256,1024]{1,0:T(8,128)(2,1)}, bf16[256,1024]{1,0:T(8,128)(2,1)S(1)}, u32[]{:S(2)}, u32[]{:S(2)}) collective-permute-start(bf16[256,1024]{1,0:T(8,128)(2,1)} %get-tuple-element.17), channel_id=1, source_target_pairs={{0,1},{1,0},{2,3},{3,2},{4,5},{5,4},{6,7},{7,6},{8,9},{9,8},{10,11... | collective-permute-start | bytes 1572872 | tf_op jit(solution)/shard_map/ppermute | solution.py:229
  3.7 1.2 copy-start.2
  5.8 55.6 %copy-start.1 = (bf16[2,1024,256]{2,1,0:T(8,128)(2,1)}, bf16[2,1024,256]{2,1,0:T(8,128)(2,1)S(1)}, u32[]{:S(2)}) copy-start(bf16[2,1024,256]{2,1,0:T(8,128)(2,1)S(1)} %shard_map.55.refs_0_) | copy-start | bytes 3145732
  5.8 24.9 %collective-permute-start.2 = (bf16[2,1024,256]{2,1,0:T(8,128)(2,1)S(1)}, bf16[2,1024,256]{2,1,0:T(8,128)(2,1)}, u32[]{:S(2)}, u32[]{:S(2)}) collective-permute-start(bf16[2,1024,256]{2,1,0:T(8,128)(2,1)S(1)} %shard_map.55.refs_0_), channel_id=1, source_target_pairs={{0,2},{1,3},{2,0},{3,1},{4,6},{5,7},{6,4},{7,5},{8,10},{9,11},{10,... | collective-permute-start | bytes 3145736 | tf_op jit(solution)/shard_map/ppermute | solution.py:229
  7.2 27.2 %collective-permute-start = (bf16[2,1024,256]{2,1,0:T(8,128)(2,1)S(1)}, bf16[2,1024,256]{2,1,0:T(8,128)(2,1)S(1)}, u32[]{:S(2)}, u32[]{:S(2)}) collective-permute-start(bf16[2,1024,256]{2,1,0:T(8,128)(2,1)S(1)} %shard_map.55.refs_0_), channel_id=1, source_target_pairs={{0,4},{1,5},{2,6},{3,7},{4,8},{5,9},{6,10},{7,11},{8,12},{9,13},{1... | collective-permute-start | bytes 3145736 | tf_op jit(solution)/shard_map/ppermute | solution.py:229
  8.8 1.2 copy-start.13
  10.0 25.5 %collective-permute-start.10 = (bf16[2,256,1024]{2,1,0:T(8,128)(2,1)}, bf16[2,256,1024]{2,1,0:T(8,128)(2,1)}, u32[]{:S(2)}, u32[]{:S(2)}) collective-permute-start(bf16[2,256,1024]{2,1,0:T(8,128)(2,1)} %pad_maximum_fusion.refs_8_), channel_id=1, source_target_pairs={{0,96},{16,112},{32,0},{48,16},{64,32},{80,48},{96,64},{112,80},{1... | collective-permute-start | bytes 3145736 | tf_op jit(solution)/shard_map/ppermute | solution.py:229
  12.7 27.1 %collective-permute-start.1 = (bf16[2,1024,256]{2,1,0:T(8,128)(2,1)S(1)}, bf16[2,1024,256]{2,1,0:T(8,128)(2,1)S(1)}, u32[]{:S(2)}, u32[]{:S(2)}) collective-permute-start(bf16[2,1024,256]{2,1,0:T(8,128)(2,1)S(1)} %shard_map.55.refs_0_), channel_id=1, source_target_pairs={{0,12},{1,13},{2,14},{3,15},{4,0},{5,1},{6,2},{7,3},{8,4},{9,5},{1... | collective-permute-start | bytes 3145736 | tf_op jit(solution)/shard_map/ppermute | solution.py:229
  14.9 35.9 %collective-permute-start.9 = (bf16[2,256,1024]{2,1,0:T(8,128)(2,1)}, bf16[2,256,1024]{2,1,0:T(8,128)(2,1)}, u32[]{:S(2)}, u32[]{:S(2)}) collective-permute-start(bf16[2,256,1024]{2,1,0:T(8,128)(2,1)} %pad_maximum_fusion.refs_8_), channel_id=1, source_target_pairs={{0,32},{16,48},{32,64},{48,80},{64,96},{80,112},{96,0},{112,16},{1... | collective-permute-start | bytes 3145736 | tf_op jit(solution)/shard_map/ppermute | solution.py:229
  30.8 26.9 %collective-permute-start.3 = (bf16[2,1024,256]{2,1,0:T(8,128)(2,1)}, bf16[2,1024,256]{2,1,0:T(8,128)(2,1)}, u32[]{:S(2)}, u32[]{:S(2)}) collective-permute-start(bf16[2,1024,256]{2,1,0:T(8,128)(2,1)} %collective-permute-done.2.refs_2_.refs_4_), channel_id=1, source_target_pairs={{0,4},{1,5},{2,6},{3,7},{4,8},{5,9},{6,10},{7,11},{8,12},{9,13},{1... | collective-permute-start | bytes 3145736 | tf_op jit(solution)/shard_map/ppermute | solution.py:229
  34.4 27.0 %copy-start.3 = (bf16[2,1024,256]{2,1,0:T(8,128)(2,1)}, bf16[2,1024,256]{2,1,0:T(8,128)(2,1)S(1)}, u32[]{:S(2)}) copy-start(bf16[2,1024,256]{2,1,0:T(8,128)(2,1)S(1)} %collective-permute-done.refs_0_) | copy-start | bytes 3145732
  34.4 25.6 %collective-permute-start.4 = (bf16[2,1024,256]{2,1,0:T(8,128)(2,1)}, bf16[2,1024,256]{2,1,0:T(8,128)(2,1)}, u32[]{:S(2)}, u32[]{:S(2)}) collective-permute-start(bf16[2,1024,256]{2,1,0:T(8,128)(2,1)} %collective-permute-done.2.refs_2_.refs_4_), channel_id=1, source_target_pairs={{0,12},{1,13},{2,14},{3,15},{4,0},{5,1},{6,2},{7,3},{8,4},{9,5},{1... | collective-permute-start | bytes 3145736 | tf_op jit(solution)/shard_map/ppermute | solution.py:229
  35.5 13.9 %collective-permute-start.6 = (bf16[1,256,1024]{2,1,0:T(8,128)(2,1)}, bf16[1,256,1024]{2,1,0:T(8,128)(2,1)}, u32[]{:S(2)}, u32[]{:S(2)}) collective-permute-start(bf16[1,256,1024]{2,1,0:T(8,128)(2,1)} %get-tuple-element.11), channel_id=1, source_target_pairs={{0,16},{16,0},{32,48},{48,32},{64,80},{80,64},{96,112},{112,96},{1... | collective-permute-start | bytes 1572872 | tf_op jit(solution)/shard_map/ppermute | solution.py:229
  39.8 21.6 %copy-start.4 = (bf16[2,1024,256]{2,1,0:T(8,128)(2,1)}, bf16[2,1024,256]{2,1,0:T(8,128)(2,1)S(1)}, u32[]{:S(2)}) copy-start(bf16[2,1024,256]{2,1,0:T(8,128)(2,1)S(1)} %collective-permute-done.1.refs_1_) | copy-start | bytes 3145732
  39.9 23.7 %collective-permute-start.12 = (bf16[1,256,1024]{2,1,0:T(8,128)(2,1)}, bf16[1,256,1024]{2,1,0:T(8,128)(2,1)}, u32[]{:S(2)}, u32[]{:S(2)}) collective-permute-start(bf16[1,256,1024]{2,1,0:T(8,128)(2,1)} %get-tuple-element.16), channel_id=1, source_target_pairs={{0,16},{16,0},{32,48},{48,32},{64,80},{80,64},{96,112},{112,96},{1... | collective-permute-start | bytes 1572872 | tf_op jit(solution)/shard_map/ppermute | solution.py:229
  49.4 14.2 %collective-permute-start.17 = (bf16[1,256,1024]{2,1,0:T(8,128)(2,1)}, bf16[1,256,1024]{2,1,0:T(8,128)(2,1)}, u32[]{:S(2)}, u32[]{:S(2)}) collective-permute-start(bf16[1,256,1024]{2,1,0:T(8,128)(2,1)} %collective-permute-done.6.refs_4_.refs_12_), channel_id=1, source_target_pairs={{0,32},{16,48},{32,64},{48,80},{64,96},{80,112},{96,0},{112,16},{1... | collective-permute-start | bytes 1572872 | tf_op jit(solution)/shard_map/ppermute | solution.py:229
  50.7 15.6 %collective-permute-start.16 = (bf16[1,256,1024]{2,1,0:T(8,128)(2,1)}, bf16[1,256,1024]{2,1,0:T(8,128)(2,1)}, u32[]{:S(2)}, u32[]{:S(2)}) collective-permute-start(bf16[1,256,1024]{2,1,0:T(8,128)(2,1)} %slice.25), channel_id=1, source_target_pairs={{0,96},{16,112},{32,0},{48,16},{64,32},{80,48},{96,64},{112,80},{1... | collective-permute-start | bytes 1572872 | tf_op jit(solution)/shard_map/ppermute | solution.py:229
  57.6 16.9 %collective-permute-start.11 = (bf16[1,256,1024]{2,1,0:T(8,128)(2,1)}, bf16[1,256,1024]{2,1,0:T(8,128)(2,1)}, u32[]{:S(2)}, u32[]{:S(2)}) collective-permute-start(bf16[1,256,1024]{2,1,0:T(8,128)(2,1)} %slice.24), channel_id=1, source_target_pairs={{0,32},{16,48},{32,64},{48,80},{64,96},{80,112},{96,0},{112,16},{1... | collective-permute-start | bytes 1572872 | tf_op jit(solution)/shard_map/ppermute | solution.py:229
  59.9 14.3 %collective-permute-start.18 = (bf16[1,256,1024]{2,1,0:T(8,128)(2,1)}, bf16[1,256,1024]{2,1,0:T(8,128)(2,1)}, u32[]{:S(2)}, u32[]{:S(2)}) collective-permute-start(bf16[1,256,1024]{2,1,0:T(8,128)(2,1)} %collective-permute-done.6.refs_4_.refs_12_), channel_id=1, source_target_pairs={{0,96},{16,112},{32,0},{48,16},{64,32},{80,48},{96,64},{112,80},{1... | collective-permute-start | bytes 1572872 | tf_op jit(solution)/shard_map/ppermute | solution.py:229
  63.6 13.4 %collective-permute-start.21 = (bf16[1,1024,256]{2,1,0:T(8,128)(2,1)S(1)}, bf16[1,1024,256]{2,1,0:T(8,128)(2,1)S(1)}, u32[]{:S(2)}, u32[]{:S(2)}) collective-permute-start(bf16[1,1024,256]{2,1,0:T(8,128)(2,1)S(1)} %slice.22), channel_id=1, source_target_pairs={{0,4},{1,5},{2,6},{3,7},{4,8},{5,9},{6,10},{7,11},{8,12},{9,13},{1... | collective-permute-start | bytes 1572872 | tf_op jit(solution)/shard_map/ppermute | solution.py:229
  63.7 15.6 %collective-permute-start.22 = (bf16[1,1024,256]{2,1,0:T(8,128)(2,1)S(1)}, bf16[1,1024,256]{2,1,0:T(8,128)(2,1)S(1)}, u32[]{:S(2)}, u32[]{:S(2)}) collective-permute-start(bf16[1,1024,256]{2,1,0:T(8,128)(2,1)S(1)} %slice.23), channel_id=1, source_target_pairs={{0,12},{1,13},{2,14},{3,15},{4,0},{5,1},{6,2},{7,3},{8,4},{9,5},{1... | collective-permute-start | bytes 1572872 | tf_op jit(solution)/shard_map/ppermute | solution.py:229
  66.3 15.4 %collective-permute-start.19 = (bf16[1,256,1024]{2,1,0:T(8,128)(2,1)}, bf16[1,256,1024]{2,1,0:T(8,128)(2,1)S(1)}, u32[]{:S(2)}, u32[]{:S(2)}) collective-permute-start(bf16[1,256,1024]{2,1,0:T(8,128)(2,1)} %collective-permute-done.16.refs_11_), channel_id=1, source_target_pairs={{0,16},{16,0},{32,48},{48,32},{64,80},{80,64},{96,112},{112,96},{1... | collective-permute-start | bytes 1572872 | tf_op jit(solution)/shard_map/ppermute | solution.py:229
  74.2 16.9 %collective-permute-start.13 = (bf16[1,256,1024]{2,1,0:T(8,128)(2,1)}, bf16[1,256,1024]{2,1,0:T(8,128)(2,1)S(1)}, u32[]{:S(2)}, u32[]{:S(2)}) collective-permute-start(bf16[1,256,1024]{2,1,0:T(8,128)(2,1)} %collective-permute-done.12.refs_17_.refs_12_), channel_id=1, source_target_pairs={{0,32},{16,48},{32,64},{48,80},{64,96},{80,112},{96,0},{112,16},{1... | collective-permute-start | bytes 1572872 | tf_op jit(solution)/shard_map/ppermute | solution.py:229
  74.6 20.4 %collective-permute-start.14 = (bf16[1,256,1024]{2,1,0:T(8,128)(2,1)}, bf16[1,256,1024]{2,1,0:T(8,128)(2,1)S(1)}, u32[]{:S(2)}, u32[]{:S(2)}) collective-permute-start(bf16[1,256,1024]{2,1,0:T(8,128)(2,1)} %collective-permute-done.12.refs_17_.refs_12_), channel_id=1, source_target_pairs={{0,96},{16,112},{32,0},{48,16},{64,32},{80,48},{96,64},{112,80},{1... | collective-permute-start | bytes 1572872 | tf_op jit(solution)/shard_map/ppermute | solution.py:229
  76.9 4.8 %copy-start.10 = (bf16[1,1024,256]{2,1,0:T(8,128)(2,1)}, bf16[1,1024,256]{2,1,0:T(8,128)(2,1)S(1)}, u32[]{:S(2)}) copy-start(bf16[1,1024,256]{2,1,0:T(8,128)(2,1)S(1)} %collective-permute-done.21.refs_3_) | copy-start | bytes 1572868
  76.9 18.1 %collective-permute-start.7 = (bf16[1,1024,256]{2,1,0:T(8,128)(2,1)}, bf16[1,1024,256]{2,1,0:T(8,128)(2,1)}, u32[]{:S(2)}, u32[]{:S(2)}) collective-permute-start(bf16[1,1024,256]{2,1,0:T(8,128)(2,1)} %slice.18), channel_id=1, source_target_pairs={{0,12},{1,13},{2,14},{3,15},{4,0},{5,1},{6,2},{7,3},{8,4},{9,5},{1... | collective-permute-start | bytes 1572872 | tf_op jit(solution)/shard_map/ppermute | solution.py:229
  79.2 2.5 %copy-start.11 = (bf16[1,1024,256]{2,1,0:T(8,128)(2,1)}, bf16[1,1024,256]{2,1,0:T(8,128)(2,1)S(1)}, u32[]{:S(2)}) copy-start(bf16[1,1024,256]{2,1,0:T(8,128)(2,1)S(1)} %collective-permute-done.22.refs_7_) | copy-start | bytes 1572868
  79.2 15.7 %collective-permute-start.15 = (bf16[1,256,1024]{2,1,0:T(8,128)(2,1)}, bf16[1,256,1024]{2,1,0:T(8,128)(2,1)S(1)}, u32[]{:S(2)}, u32[]{:S(2)}) collective-permute-start(bf16[1,256,1024]{2,1,0:T(8,128)(2,1)} %collective-permute-done.11.refs_16_.refs_11_), channel_id=1, source_target_pairs={{0,16},{16,0},{32,48},{48,32},{64,80},{80,64},{96,112},{112,96},{1... | collective-permute-start | bytes 1572872 | tf_op jit(solution)/shard_map/ppermute | solution.py:229
  81.7 0.8 copy-start.12
  81.7 13.3 %collective-permute-start.8 = (bf16[1,1024,256]{2,1,0:T(8,128)(2,1)}, bf16[1,1024,256]{2,1,0:T(8,128)(2,1)}, u32[]{:S(2)}, u32[]{:S(2)}) collective-permute-start(bf16[1,1024,256]{2,1,0:T(8,128)(2,1)} %slice.19), channel_id=1, source_target_pairs={{0,4},{1,5},{2,6},{3,7},{4,8},{5,9},{6,10},{7,11},{8,12},{9,13},{1... | collective-permute-start | bytes 1572872 | tf_op jit(solution)/shard_map/ppermute | solution.py:229
  91.2 3.8 %copy-start.5 = (bf16[1,256,1024]{2,1,0:T(8,128)(2,1)}, bf16[1,256,1024]{2,1,0:T(8,128)(2,1)S(1)}, u32[]{:S(2)}) copy-start(bf16[1,256,1024]{2,1,0:T(8,128)(2,1)S(1)} %collective-permute-done.13.refs_17_.refs_13_) | copy-start | bytes 1572868
  91.2 15.4 %collective-permute-start.23 = (bf16[8,8,128,128]{3,2,1,0:T(8,128)(2,1)}, bf16[8,8,128,128]{3,2,1,0:T(8,128)(2,1)S(1)}, u32[]{:S(2)}, u32[]{:S(2)}) collective-permute-start(bf16[8,8,128,128]{3,2,1,0:T(8,128)(2,1)} %shard_map.59), channel_id=1, source_target_pairs={{0,1},{1,0},{2,3},{3,2},{4,5},{5,4},{6,7},{7,6},{8,9},{9,8},{10,11... | collective-permute-start | bytes 6291464 | tf_op jit(solution)/shard_map/ppermute | solution.py:229
  95.0 0.8 copy-start.6
  95.0 1.0 copy-start.7
  104.6 12.3 %collective-permute-start.20 = (bf16[8,8,128,128]{3,2,1,0:T(8,128)(2,1)}, bf16[8,8,128,128]{3,2,1,0:T(8,128)(2,1)}, u32[]{:S(2)}, u32[]{:S(2)}) collective-permute-start(bf16[8,8,128,128]{3,2,1,0:T(8,128)(2,1)} %shard_map.58), channel_id=1, source_target_pairs={{0,1},{1,0},{2,3},{3,2},{4,5},{5,4},{6,7},{7,6},{8,9},{9,8},{10,11... | collective-permute-start | bytes 6291464 | tf_op jit(solution)/shard_map/ppermute | solution.py:229
  106.6 1.4 copy-start.9
  179.6 5.9 %copy-start.14 = (f32[4096]{0:T(1024)S(1)}, f32[4096]{0:T(1024)}, u32[]{:S(2)}) copy-start(f32[4096]{0:T(1024)} %param.9) | copy-start | bytes 49156
  179.6 5.9 %copy-start.15 = (f32[4]{0:T(128)S(1)}, f32[4]{0:T(128)}, u32[]{:S(2)}) copy-start(f32[4]{0:T(128)} %param.8) | copy-start | bytes 52
  179.6 58.4 %all-to-all-start.1 = ((bf16[128,128,128]{2,1,0:T(8,128)(2,1)}), bf16[128,128,128]{2,1,0:T(8,128)(2,1)}, u32[]{:S(2)}, u32[]{:S(2)}) async-start(bf16[128,128,128]{2,1,0:T(8,128)(2,1)} %bitcast.13), calls=%async_computation.1 | async-start | bytes 8388608 | tf_op jit(solution)/shard_map/all_to_all | solution.py:262

commit v6 on v5

--- a/solution.py
+++ b/solution.py
@@ -70,7 +70,7 @@
 def product_kernel(j, h, taken, *refs):
     a_refs, b_refs = refs[:8], refs[8:16]
     out_ref, a_buf, b_buf, total, taken_buf, out_buf, a_sem, b_sem, t_sem, o_sem = refs[-10:]
-    depth, group, wide = 256, 2, 512
+    depth, wide = 256, 512
     cols = total.shape[1]
     base = 8 * j if taken else 0
     row_place, col_place = lax.axis_index("row"), lax.axis_index("col")
@@ -100,7 +100,7 @@
             start_b(t, u)
     if taken:
         pltpu.make_async_copy(refs[16], taken_buf, t_sem).start()
-    for t in range(0, 8, group):
+    for t, group in ((0, 1), (1, 1), (2, 2), (4, 2), (6, 2)):
         for u in range(t, t + group):
             a_copy(u).wait()
             b_copy(b_refs[0].at[0], u).wait()
@@ -155,7 +155,7 @@
     )(*a_shards, *b_shards, *extra)
 
 
-STEPS = 8
+STEPS = 16
 
 
 def finish_kernel(row_gap_ref, gap_ref, direct_ref, mirror_ref, out_ref, direct_buf, mirror_buf, out_buf, sems, out_sem):

time: 246 us -> 247 us (level)
  no operation moved by 1% of the time
where the time goes in v6:
time: 247 us; the launch traced here: 246 us
  waiting for transfers between devices  84 us (34%)
  blocking collectives  53.6 us (22%)
  starting transfers between devices  45 us (18%)
  Pallas kernels  43.8 us (18%)
  local copies, waits for them, and re-layouts  17.8 us (7%)
    all_to_all x1, blocking collectives, local(): lax.all_to_all(made, 'col', split_axis=0, concat_axis=0, tiled=True)  53.6 us
    all_to_all x1, waiting for transfers between devices, local(): lax.all_to_all(direct, ('row', 'col'), split_axis=0, concat_axis=0, tiled...  50.9 us
    ppermute x24, starting transfers between devices, local(): lax.ppermute(block, 'col' if len(pairs) == 16 else 'row', pairs)  39.1 us
    pallas_call x4, Pallas kernels, product(): pl.pallas_call(functools.partial(product_kernel, j, h, taken is not None)...  34.9 us
    ppermute x24, waiting for transfers between devices, local(): lax.ppermute(block, 'col' if len(pairs) == 16 else 'row', pairs)  33.1 us
    pallas_call x1, Pallas kernels, finish(): pl.pallas_call(finish_kernel, out_shape=jax.ShapeDtypeStruct((rows, count...  8 us
    all_to_all x1, starting transfers between devices, local(): lax.all_to_all(direct, ('row', 'col'), split_axis=0, concat_axis=0, tiled...  5.85 us
    unnamed x35, local copies, waits for them, and re-layouts  5.11 us
  transfers between devices with their start and end apart: 25, of which 7 were waited for; matrix products, arithmetic and copies ran while one was open for 5% of the time, Pallas kernels for 11%

profile of v6, /device:TPU:1, one launch (start us, length us, event | category | flops | bytes accessed | tf_op | source)
XLA Modules:
  0.0 245.9 jit_solution(3797117056628490230)
XLA Ops:
  0.0 2.1 constant_dynamic-slice_fusion
  2.1 1.4 collective-permute-start.5
  3.5 0.1 constant_dynamic-slice_fusion.1
  3.6 0.1 copy.15.mask_ref
  3.7 1.2 copy-done.2
  4.9 0.9 shard_map.55.refs_0_
  5.8 1.4 collective-permute-start.2
  7.2 1.6 collective-permute-start
  8.8 0.0 collective-permute-done.5
  8.8 1.1 pad_maximum_fusion.refs_8_
  10.0 2.7 %collective-permute-start.10 = (bf16[2,256,1024]{2,1,0:T(8,128)(2,1)}, bf16[2,256,1024]{2,1,0:T(8,128)(2,1)}, u32[]{:S(2)}, u32[]{:S(2)}) collective-permute-start(bf16[2,256,1024]{2,1,0:T(8,128)(2,1)} %pad_maximum_fusion.refs_8_), channel_id=1, source_target_pairs={{0,96},{16,112},{32,0},{48,16},{64,32},{80,48},{96,64},{112,80},{1... | collective-permute-start | bytes 3145736 | tf_op jit(solution)/shard_map/ppermute | solution.py:229
  12.7 2.1 collective-permute-start.1
  14.9 15.9 %collective-permute-done.2.refs_2_.refs_4_ = bf16[2,1024,256]{2,1,0:T(8,128)(2,1)} collective-permute-done((bf16[2,1024,256]{2,1,0:T(8,128)(2,1)S(1)}, bf16[2,1024,256]{2,1,0:T(8,128)(2,1)}, u32[]{:S(2)}, u32[]{:S(2)}) %collective-permute-start.2) | collective-permute-done | bytes 1048608 | tf_op jit(solution)/shard_map/ppermute | solution.py:229
  30.8 1.7 collective-permute-start.3
  32.5 1.9 collective-permute-done.refs_0_
  34.4 1.1 collective-permute-start.4
  35.5 2.5 collective-permute-start.6
  38.0 1.9 slice.25
  39.9 0.5 collective-permute-start.12
  40.4 9.1 %collective-permute-done.6.refs_4_.refs_12_ = bf16[1,256,1024]{2,1,0:T(8,128)(2,1)} collective-permute-done((bf16[1,256,1024]{2,1,0:T(8,128)(2,1)}, bf16[1,256,1024]{2,1,0:T(8,128)(2,1)}, u32[]{:S(2)}, u32[]{:S(2)}) %collective-permute-start.6) | collective-permute-done | bytes 524320 | tf_op jit(solution)/shard_map/ppermute | solution.py:229
  49.4 1.3 collective-permute-start.17
  50.7 0.0 collective-permute-done.9.refs_9_
  50.7 1.4 collective-permute-start.16
  52.2 1.9 slice.24
  54.0 3.6 %collective-permute-done.3.refs_2_ = bf16[2,1024,256]{2,1,0:T(8,128)(2,1)} collective-permute-done((bf16[2,1024,256]{2,1,0:T(8,128)(2,1)}, bf16[2,1024,256]{2,1,0:T(8,128)(2,1)}, u32[]{:S(2)}, u32[]{:S(2)}) %collective-permute-start.3) | collective-permute-done | bytes 1048608 | tf_op jit(solution)/shard_map/ppermute | solution.py:229
  57.6 1.3 collective-permute-start.11
  58.9 1.0 collective-permute-done.4.refs_3_
  59.9 1.5 collective-permute-start.18
  61.4 1.1 slice.22
  62.5 1.1 slice.23
  63.6 0.1 collective-permute-start.21
  63.7 2.7 %collective-permute-start.22 = (bf16[1,1024,256]{2,1,0:T(8,128)(2,1)S(1)}, bf16[1,1024,256]{2,1,0:T(8,128)(2,1)S(1)}, u32[]{:S(2)}, u32[]{:S(2)}) collective-permute-start(bf16[1,1024,256]{2,1,0:T(8,128)(2,1)S(1)} %slice.23), channel_id=1, source_target_pairs={{0,12},{1,13},{2,14},{3,15},{4,0},{5,1},{6,2},{7,3},{8,4},{9,5},{1... | collective-permute-start | bytes 1572872 | tf_op jit(solution)/shard_map/ppermute | solution.py:229
  66.3 0.0 collective-permute-done.16.refs_11_
  66.3 2.5 collective-permute-start.19
  68.8 1.9 slice.18
  70.7 1.9 slice.19
  72.6 1.7 collective-permute-done.18.refs_14_
  74.2 0.3 collective-permute-start.13
  74.6 0.0 collective-permute-done.11.refs_16_.refs_11_
  74.6 2.4 collective-permute-start.14
  76.9 2.3 collective-permute-start.7
  79.2 2.5 collective-permute-start.15
  81.7 0.0 collective-permute-done.19.refs_15_
  81.7 0.0 collective-permute-start.8
  81.7 0.8 copy-done.12
  82.5 8.6 %shard_map.59 = bf16[8,8,128,128]{3,2,1,0:T(8,128)(2,1)} custom-call(bf16[2,1024,256]{2,1,0:T(8,128)(2,1)} %copy-done.1, bf16[2,1024,256]{2,1,0:T(8,128)(2,1)} %get-tuple-element.12.refs_1_, bf16[2,1024,256]{2,1,0:T(8,128)(2,1)} %get-tuple-element.13.refs_2_, bf16[1,1024,256]{2,1,0:T(8,128)(2,1)} %copy-done.10, ...), custom_call_target="tpu_custom_call" | custom-call | flops 4294967296 | bytes 10485760 | tf_op jit(solution)/shard_map/pallas_call | solution.py:134
  91.1 3.7 %collective-permute-start.23 = (bf16[8,8,128,128]{3,2,1,0:T(8,128)(2,1)}, bf16[8,8,128,128]{3,2,1,0:T(8,128)(2,1)S(1)}, u32[]{:S(2)}, u32[]{:S(2)}) collective-permute-start(bf16[8,8,128,128]{3,2,1,0:T(8,128)(2,1)} %shard_map.59), channel_id=1, source_target_pairs={{0,1},{1,0},{2,3},{3,2},{4,5},{5,4},{6,7},{7,6},{8,9},{9,8},{10,11... | collective-permute-start | bytes 6291464 | tf_op jit(solution)/shard_map/ppermute | solution.py:229
  94.8 0.0 collective-permute-done.14.refs_18_.refs_14_
  94.8 0.0 collective-permute-done.15.refs_16_.refs_15_
  94.9 0.8 copy-done.6
  95.6 0.2 copy-done.7
  95.8 8.6 %shard_map.58 = bf16[8,8,128,128]{3,2,1,0:T(8,128)(2,1)} custom-call(bf16[2,1024,256]{2,1,0:T(8,128)(2,1)} %copy-done.1, bf16[2,1024,256]{2,1,0:T(8,128)(2,1)} %get-tuple-element.12.refs_1_, bf16[2,1024,256]{2,1,0:T(8,128)(2,1)} %get-tuple-element.13.refs_2_, bf16[1,1024,256]{2,1,0:T(8,128)(2,1)} %collective-permute-done.7.refs_3_, ...), custom_call_target="tpu_custom_call" | custom-call | flops 4294967296 | bytes 10485760 | tf_op jit(solution)/shard_map/pallas_call | solution.py:134
  104.4 2.1 collective-permute-start.20
  106.5 1.4 copy-done.9
  107.9 8.9 %shard_map.60.refs_17_ = bf16[16,8,128,128]{3,2,1,0:T(8,128)(2,1)} custom-call(bf16[2,1024,256]{2,1,0:T(8,128)(2,1)} %copy-done.1, bf16[2,1024,256]{2,1,0:T(8,128)(2,1)} %get-tuple-element.12.refs_1_, bf16[2,1024,256]{2,1,0:T(8,128)(2,1)} %get-tuple-element.13.refs_2_, bf16[1,1024,256]{2,1,0:T(8,128)(2,1)} %copy-done.10, ...), custom_call_target="tpu_custom_call" | custom-call | flops 4294967296 | bytes 10485760 | tf_op jit(solution)/shard_map/pallas_call | solution.py:134
  116.8 8.9 %shard_map.61 = bf16[16,8,128,128]{3,2,1,0:T(8,128)(2,1)} custom-call(bf16[2,1024,256]{2,1,0:T(8,128)(2,1)} %copy-done.1, bf16[2,1024,256]{2,1,0:T(8,128)(2,1)} %get-tuple-element.12.refs_1_, bf16[2,1024,256]{2,1,0:T(8,128)(2,1)} %get-tuple-element.13.refs_2_, bf16[1,1024,256]{2,1,0:T(8,128)(2,1)} %collective-permute-done.7.refs_3_, ...), custom_call_target="tpu_custom_call", output_to_operand_aliasing={{}: (17, {})} | custom-call | flops 4294967296 | bytes 10485760 | tf_op jit(solution)/shard_map/pallas_call | solution.py:134
  125.7 53.6 %all_to_all.10 = bf16[16,8,128,128]{3,2,1,0:T(8,128)(2,1)} all-to-all(bf16[16,8,128,128]{3,2,1,0:T(8,128)(2,1)} %shard_map.61), channel_id=1, replica_groups=mesh['row'=8,'col'=16] {'col'}, dimensions={0} | all-to-all | bytes 8388608 | tf_op jit(solution)/shard_map/all_to_all | solution.py:261
  179.3 5.9 %all-to-all-start.1 = ((bf16[128,128,128]{2,1,0:T(8,128)(2,1)}), bf16[128,128,128]{2,1,0:T(8,128)(2,1)}, u32[]{:S(2)}, u32[]{:S(2)}) async-start(bf16[128,128,128]{2,1,0:T(8,128)(2,1)} %bitcast.13), calls=%async_computation.1 | async-start | bytes 8388608 | tf_op jit(solution)/shard_map/all_to_all | solution.py:262
  185.2 0.1 subtract_bitcast_fusion
  185.3 0.1 dynamic-slice_bitcast_fusion.1
  185.4 0.7 copy.14.row_gap_ref
  186.1 0.7 copy.17
  186.8 50.9 %all-to-all-done.1.mirror_ref = bf16[128,128,128]{2,1,0:T(8,128)(2,1)} async-done(((bf16[128,128,128]{2,1,0:T(8,128)(2,1)}), bf16[128,128,128]{2,1,0:T(8,128)(2,1)}, u32[]{:S(2)}, u32[]{:S(2)}) %all-to-all-start.1) | async-done | bytes 4194336 | tf_op jit(solution)/shard_map/all_to_all | solution.py:262
  237.7 8.0 %shard_map.62 = bf16[128,16384]{1,0:T(8,128)(2,1)} custom-call(f32[128,1]{1,0:T(8,128)} %copy.14.row_gap_ref, f32[1,16384]{1,0:T(1,128)} %bitcast.17, bf16[128,128,128]{2,1,0:T(8,128)(2,1)} %bitcast.14, bf16[128,128,128]{2,1,0:T(8,128)(2,1)} %all-to-all-done.1.mirror_ref), custom_call_target="tpu_custom_call" | custom-call | tf_op jit(solution)/shard_map/pallas_call | solution.py:196
  (42 shorter events, 0.1 us)
Async XLA Ops:
  0.0 3.5 %copy-start = (s32[64,32]{0,1:T(8,128)S(1)}, s32[64,32]{0,1:T(8,128)}, u32[]{:S(2)}) copy-start(s32[64,32]{0,1:T(8,128)} %param.7) | copy-start | bytes 24580
  2.1 7.9 %copy-start.8 = (bf16[1,256,1024]{2,1,0:T(8,128)(2,1)}, bf16[1,256,1024]{2,1,0:T(8,128)(2,1)S(1)}, u32[]{:S(2)}) copy-start(bf16[1,256,1024]{2,1,0:T(8,128)(2,1)S(1)} %get-tuple-element.18.refs_0_) | copy-start | bytes 1572868
  2.1 6.8 %collective-permute-start.5 = (bf16[256,1024]{1,0:T(8,128)(2,1)}, bf16[256,1024]{1,0:T(8,128)(2,1)S(1)}, u32[]{:S(2)}, u32[]{:S(2)}) collective-permute-start(bf16[256,1024]{1,0:T(8,128)(2,1)} %get-tuple-element.17), channel_id=1, source_target_pairs={{0,1},{1,0},{2,3},{3,2},{4,5},{5,4},{6,7},{7,6},{8,9},{9,8},{10,11... | collective-permute-start | bytes 1572872 | tf_op jit(solution)/shard_map/ppermute | solution.py:229
  3.7 1.2 copy-start.2
  5.8 55.6 %copy-start.1 = (bf16[2,1024,256]{2,1,0:T(8,128)(2,1)}, bf16[2,1024,256]{2,1,0:T(8,128)(2,1)S(1)}, u32[]{:S(2)}) copy-start(bf16[2,1024,256]{2,1,0:T(8,128)(2,1)S(1)} %shard_map.55.refs_0_) | copy-start | bytes 3145732
  5.8 24.9 %collective-permute-start.2 = (bf16[2,1024,256]{2,1,0:T(8,128)(2,1)S(1)}, bf16[2,1024,256]{2,1,0:T(8,128)(2,1)}, u32[]{:S(2)}, u32[]{:S(2)}) collective-permute-start(bf16[2,1024,256]{2,1,0:T(8,128)(2,1)S(1)} %shard_map.55.refs_0_), channel_id=1, source_target_pairs={{0,2},{1,3},{2,0},{3,1},{4,6},{5,7},{6,4},{7,5},{8,10},{9,11},{10,... | collective-permute-start | bytes 3145736 | tf_op jit(solution)/shard_map/ppermute | solution.py:229
  7.2 27.2 %collective-permute-start = (bf16[2,1024,256]{2,1,0:T(8,128)(2,1)S(1)}, bf16[2,1024,256]{2,1,0:T(8,128)(2,1)S(1)}, u32[]{:S(2)}, u32[]{:S(2)}) collective-permute-start(bf16[2,1024,256]{2,1,0:T(8,128)(2,1)S(1)} %shard_map.55.refs_0_), channel_id=1, source_target_pairs={{0,4},{1,5},{2,6},{3,7},{4,8},{5,9},{6,10},{7,11},{8,12},{9,13},{1... | collective-permute-start | bytes 3145736 | tf_op jit(solution)/shard_map/ppermute | solution.py:229
  8.8 1.2 copy-start.13
  10.0 25.5 %collective-permute-start.10 = (bf16[2,256,1024]{2,1,0:T(8,128)(2,1)}, bf16[2,256,1024]{2,1,0:T(8,128)(2,1)}, u32[]{:S(2)}, u32[]{:S(2)}) collective-permute-start(bf16[2,256,1024]{2,1,0:T(8,128)(2,1)} %pad_maximum_fusion.refs_8_), channel_id=1, source_target_pairs={{0,96},{16,112},{32,0},{48,16},{64,32},{80,48},{96,64},{112,80},{1... | collective-permute-start | bytes 3145736 | tf_op jit(solution)/shard_map/ppermute | solution.py:229
  12.7 27.1 %collective-permute-start.1 = (bf16[2,1024,256]{2,1,0:T(8,128)(2,1)S(1)}, bf16[2,1024,256]{2,1,0:T(8,128)(2,1)S(1)}, u32[]{:S(2)}, u32[]{:S(2)}) collective-permute-start(bf16[2,1024,256]{2,1,0:T(8,128)(2,1)S(1)} %shard_map.55.refs_0_), channel_id=1, source_target_pairs={{0,12},{1,13},{2,14},{3,15},{4,0},{5,1},{6,2},{7,3},{8,4},{9,5},{1... | collective-permute-start | bytes 3145736 | tf_op jit(solution)/shard_map/ppermute | solution.py:229
  14.9 35.9 %collective-permute-start.9 = (bf16[2,256,1024]{2,1,0:T(8,128)(2,1)}, bf16[2,256,1024]{2,1,0:T(8,128)(2,1)}, u32[]{:S(2)}, u32[]{:S(2)}) collective-permute-start(bf16[2,256,1024]{2,1,0:T(8,128)(2,1)} %pad_maximum_fusion.refs_8_), channel_id=1, source_target_pairs={{0,32},{16,48},{32,64},{48,80},{64,96},{80,112},{96,0},{112,16},{1... | collective-permute-start | bytes 3145736 | tf_op jit(solution)/shard_map/ppermute | solution.py:229
  30.8 26.9 %collective-permute-start.3 = (bf16[2,1024,256]{2,1,0:T(8,128)(2,1)}, bf16[2,1024,256]{2,1,0:T(8,128)(2,1)}, u32[]{:S(2)}, u32[]{:S(2)}) collective-permute-start(bf16[2,1024,256]{2,1,0:T(8,128)(2,1)} %collective-permute-done.2.refs_2_.refs_4_), channel_id=1, source_target_pairs={{0,4},{1,5},{2,6},{3,7},{4,8},{5,9},{6,10},{7,11},{8,12},{9,13},{1... | collective-permute-start | bytes 3145736 | tf_op jit(solution)/shard_map/ppermute | solution.py:229
  34.4 27.0 %copy-start.3 = (bf16[2,1024,256]{2,1,0:T(8,128)(2,1)}, bf16[2,1024,256]{2,1,0:T(8,128)(2,1)S(1)}, u32[]{:S(2)}) copy-start(bf16[2,1024,256]{2,1,0:T(8,128)(2,1)S(1)} %collective-permute-done.refs_0_) | copy-start | bytes 3145732
  34.4 25.6 %collective-permute-start.4 = (bf16[2,1024,256]{2,1,0:T(8,128)(2,1)}, bf16[2,1024,256]{2,1,0:T(8,128)(2,1)}, u32[]{:S(2)}, u32[]{:S(2)}) collective-permute-start(bf16[2,1024,256]{2,1,0:T(8,128)(2,1)} %collective-permute-done.2.refs_2_.refs_4_), channel_id=1, source_target_pairs={{0,12},{1,13},{2,14},{3,15},{4,0},{5,1},{6,2},{7,3},{8,4},{9,5},{1... | collective-permute-start | bytes 3145736 | tf_op jit(solution)/shard_map/ppermute | solution.py:229
  35.5 13.9 %collective-permute-start.6 = (bf16[1,256,1024]{2,1,0:T(8,128)(2,1)}, bf16[1,256,1024]{2,1,0:T(8,128)(2,1)}, u32[]{:S(2)}, u32[]{:S(2)}) collective-permute-start(bf16[1,256,1024]{2,1,0:T(8,128)(2,1)} %get-tuple-element.11), channel_id=1, source_target_pairs={{0,16},{16,0},{32,48},{48,32},{64,80},{80,64},{96,112},{112,96},{1... | collective-permute-start | bytes 1572872 | tf_op jit(solution)/shard_map/ppermute | solution.py:229
  39.8 21.6 %copy-start.4 = (bf16[2,1024,256]{2,1,0:T(8,128)(2,1)}, bf16[2,1024,256]{2,1,0:T(8,128)(2,1)S(1)}, u32[]{:S(2)}) copy-start(bf16[2,1024,256]{2,1,0:T(8,128)(2,1)S(1)} %collective-permute-done.1.refs_1_) | copy-start | bytes 3145732
  39.9 23.7 %collective-permute-start.12 = (bf16[1,256,1024]{2,1,0:T(8,128)(2,1)}, bf16[1,256,1024]{2,1,0:T(8,128)(2,1)}, u32[]{:S(2)}, u32[]{:S(2)}) collective-permute-start(bf16[1,256,1024]{2,1,0:T(8,128)(2,1)} %get-tuple-element.16), channel_id=1, source_target_pairs={{0,16},{16,0},{32,48},{48,32},{64,80},{80,64},{96,112},{112,96},{1... | collective-permute-start | bytes 1572872 | tf_op jit(solution)/shard_map/ppermute | solution.py:229
  49.4 14.2 %collective-permute-start.17 = (bf16[1,256,1024]{2,1,0:T(8,128)(2,1)}, bf16[1,256,1024]{2,1,0:T(8,128)(2,1)}, u32[]{:S(2)}, u32[]{:S(2)}) collective-permute-start(bf16[1,256,1024]{2,1,0:T(8,128)(2,1)} %collective-permute-done.6.refs_4_.refs_12_), channel_id=1, source_target_pairs={{0,32},{16,48},{32,64},{48,80},{64,96},{80,112},{96,0},{112,16},{1... | collective-permute-start | bytes 1572872 | tf_op jit(solution)/shard_map/ppermute | solution.py:229
  50.7 15.6 %collective-permute-start.16 = (bf16[1,256,1024]{2,1,0:T(8,128)(2,1)}, bf16[1,256,1024]{2,1,0:T(8,128)(2,1)}, u32[]{:S(2)}, u32[]{:S(2)}) collective-permute-start(bf16[1,256,1024]{2,1,0:T(8,128)(2,1)} %slice.25), channel_id=1, source_target_pairs={{0,96},{16,112},{32,0},{48,16},{64,32},{80,48},{96,64},{112,80},{1... | collective-permute-start | bytes 1572872 | tf_op jit(solution)/shard_map/ppermute | solution.py:229
  57.6 16.9 %collective-permute-start.11 = (bf16[1,256,1024]{2,1,0:T(8,128)(2,1)}, bf16[1,256,1024]{2,1,0:T(8,128)(2,1)}, u32[]{:S(2)}, u32[]{:S(2)}) collective-permute-start(bf16[1,256,1024]{2,1,0:T(8,128)(2,1)} %slice.24), channel_id=1, source_target_pairs={{0,32},{16,48},{32,64},{48,80},{64,96},{80,112},{96,0},{112,16},{1... | collective-permute-start | bytes 1572872 | tf_op jit(solution)/shard_map/ppermute | solution.py:229
  59.9 14.3 %collective-permute-start.18 = (bf16[1,256,1024]{2,1,0:T(8,128)(2,1)}, bf16[1,256,1024]{2,1,0:T(8,128)(2,1)}, u32[]{:S(2)}, u32[]{:S(2)}) collective-permute-start(bf16[1,256,1024]{2,1,0:T(8,128)(2,1)} %collective-permute-done.6.refs_4_.refs_12_), channel_id=1, source_target_pairs={{0,96},{16,112},{32,0},{48,16},{64,32},{80,48},{96,64},{112,80},{1... | collective-permute-start | bytes 1572872 | tf_op jit(solution)/shard_map/ppermute | solution.py:229
  63.6 13.4 %collective-permute-start.21 = (bf16[1,1024,256]{2,1,0:T(8,128)(2,1)S(1)}, bf16[1,1024,256]{2,1,0:T(8,128)(2,1)S(1)}, u32[]{:S(2)}, u32[]{:S(2)}) collective-permute-start(bf16[1,1024,256]{2,1,0:T(8,128)(2,1)S(1)} %slice.22), channel_id=1, source_target_pairs={{0,4},{1,5},{2,6},{3,7},{4,8},{5,9},{6,10},{7,11},{8,12},{9,13},{1... | collective-permute-start | bytes 1572872 | tf_op jit(solution)/shard_map/ppermute | solution.py:229
  63.7 15.6 %collective-permute-start.22 = (bf16[1,1024,256]{2,1,0:T(8,128)(2,1)S(1)}, bf16[1,1024,256]{2,1,0:T(8,128)(2,1)S(1)}, u32[]{:S(2)}, u32[]{:S(2)}) collective-permute-start(bf16[1,1024,256]{2,1,0:T(8,128)(2,1)S(1)} %slice.23), channel_id=1, source_target_pairs={{0,12},{1,13},{2,14},{3,15},{4,0},{5,1},{6,2},{7,3},{8,4},{9,5},{1... | collective-permute-start | bytes 1572872 | tf_op jit(solution)/shard_map/ppermute | solution.py:229
  66.3 15.4 %collective-permute-start.19 = (bf16[1,256,1024]{2,1,0:T(8,128)(2,1)}, bf16[1,256,1024]{2,1,0:T(8,128)(2,1)S(1)}, u32[]{:S(2)}, u32[]{:S(2)}) collective-permute-start(bf16[1,256,1024]{2,1,0:T(8,128)(2,1)} %collective-permute-done.16.refs_11_), channel_id=1, source_target_pairs={{0,16},{16,0},{32,48},{48,32},{64,80},{80,64},{96,112},{112,96},{1... | collective-permute-start | bytes 1572872 | tf_op jit(solution)/shard_map/ppermute | solution.py:229
  74.2 16.8 %collective-permute-start.13 = (bf16[1,256,1024]{2,1,0:T(8,128)(2,1)}, bf16[1,256,1024]{2,1,0:T(8,128)(2,1)S(1)}, u32[]{:S(2)}, u32[]{:S(2)}) collective-permute-start(bf16[1,256,1024]{2,1,0:T(8,128)(2,1)} %collective-permute-done.12.refs_17_.refs_12_), channel_id=1, source_target_pairs={{0,32},{16,48},{32,64},{48,80},{64,96},{80,112},{96,0},{112,16},{1... | collective-permute-start | bytes 1572872 | tf_op jit(solution)/shard_map/ppermute | solution.py:229
  74.6 20.2 %collective-permute-start.14 = (bf16[1,256,1024]{2,1,0:T(8,128)(2,1)}, bf16[1,256,1024]{2,1,0:T(8,128)(2,1)S(1)}, u32[]{:S(2)}, u32[]{:S(2)}) collective-permute-start(bf16[1,256,1024]{2,1,0:T(8,128)(2,1)} %collective-permute-done.12.refs_17_.refs_12_), channel_id=1, source_target_pairs={{0,96},{16,112},{32,0},{48,16},{64,32},{80,48},{96,64},{112,80},{1... | collective-permute-start | bytes 1572872 | tf_op jit(solution)/shard_map/ppermute | solution.py:229
  76.9 4.8 %copy-start.10 = (bf16[1,1024,256]{2,1,0:T(8,128)(2,1)}, bf16[1,1024,256]{2,1,0:T(8,128)(2,1)S(1)}, u32[]{:S(2)}) copy-start(bf16[1,1024,256]{2,1,0:T(8,128)(2,1)S(1)} %collective-permute-done.21.refs_3_) | copy-start | bytes 1572868
  76.9 17.9 %collective-permute-start.7 = (bf16[1,1024,256]{2,1,0:T(8,128)(2,1)}, bf16[1,1024,256]{2,1,0:T(8,128)(2,1)}, u32[]{:S(2)}, u32[]{:S(2)}) collective-permute-start(bf16[1,1024,256]{2,1,0:T(8,128)(2,1)} %slice.18), channel_id=1, source_target_pairs={{0,12},{1,13},{2,14},{3,15},{4,0},{5,1},{6,2},{7,3},{8,4},{9,5},{1... | collective-permute-start | bytes 1572872 | tf_op jit(solution)/shard_map/ppermute | solution.py:229
  79.2 2.5 %copy-start.11 = (bf16[1,1024,256]{2,1,0:T(8,128)(2,1)}, bf16[1,1024,256]{2,1,0:T(8,128)(2,1)S(1)}, u32[]{:S(2)}) copy-start(bf16[1,1024,256]{2,1,0:T(8,128)(2,1)S(1)} %collective-permute-done.22.refs_7_) | copy-start | bytes 1572868
  79.2 15.6 %collective-permute-start.15 = (bf16[1,256,1024]{2,1,0:T(8,128)(2,1)}, bf16[1,256,1024]{2,1,0:T(8,128)(2,1)S(1)}, u32[]{:S(2)}, u32[]{:S(2)}) collective-permute-start(bf16[1,256,1024]{2,1,0:T(8,128)(2,1)} %collective-permute-done.11.refs_16_.refs_11_), channel_id=1, source_target_pairs={{0,16},{16,0},{32,48},{48,32},{64,80},{80,64},{96,112},{112,96},{1... | collective-permute-start | bytes 1572872 | tf_op jit(solution)/shard_map/ppermute | solution.py:229
  81.7 0.8 copy-start.12
  81.7 13.1 %collective-permute-start.8 = (bf16[1,1024,256]{2,1,0:T(8,128)(2,1)}, bf16[1,1024,256]{2,1,0:T(8,128)(2,1)}, u32[]{:S(2)}, u32[]{:S(2)}) collective-permute-start(bf16[1,1024,256]{2,1,0:T(8,128)(2,1)} %slice.19), channel_id=1, source_target_pairs={{0,4},{1,5},{2,6},{3,7},{4,8},{5,9},{6,10},{7,11},{8,12},{9,13},{1... | collective-permute-start | bytes 1572872 | tf_op jit(solution)/shard_map/ppermute | solution.py:229
  91.1 3.8 %copy-start.5 = (bf16[1,256,1024]{2,1,0:T(8,128)(2,1)}, bf16[1,256,1024]{2,1,0:T(8,128)(2,1)S(1)}, u32[]{:S(2)}) copy-start(bf16[1,256,1024]{2,1,0:T(8,128)(2,1)S(1)} %collective-permute-done.13.refs_17_.refs_13_) | copy-start | bytes 1572868
  91.1 15.4 %collective-permute-start.23 = (bf16[8,8,128,128]{3,2,1,0:T(8,128)(2,1)}, bf16[8,8,128,128]{3,2,1,0:T(8,128)(2,1)S(1)}, u32[]{:S(2)}, u32[]{:S(2)}) collective-permute-start(bf16[8,8,128,128]{3,2,1,0:T(8,128)(2,1)} %shard_map.59), channel_id=1, source_target_pairs={{0,1},{1,0},{2,3},{3,2},{4,5},{5,4},{6,7},{7,6},{8,9},{9,8},{10,11... | collective-permute-start | bytes 6291464 | tf_op jit(solution)/shard_map/ppermute | solution.py:229
  94.8 0.8 copy-start.6
  94.8 1.0 copy-start.7
  104.4 12.4 %collective-permute-start.20 = (bf16[8,8,128,128]{3,2,1,0:T(8,128)(2,1)}, bf16[8,8,128,128]{3,2,1,0:T(8,128)(2,1)}, u32[]{:S(2)}, u32[]{:S(2)}) collective-permute-start(bf16[8,8,128,128]{3,2,1,0:T(8,128)(2,1)} %shard_map.58), channel_id=1, source_target_pairs={{0,1},{1,0},{2,3},{3,2},{4,5},{5,4},{6,7},{7,6},{8,9},{9,8},{10,11... | collective-permute-start | bytes 6291464 | tf_op jit(solution)/shard_map/ppermute | solution.py:229
  106.5 1.4 copy-start.9
  179.3 5.9 %copy-start.14 = (f32[4096]{0:T(1024)S(1)}, f32[4096]{0:T(1024)}, u32[]{:S(2)}) copy-start(f32[4096]{0:T(1024)} %param.9) | copy-start | bytes 49156
  179.3 5.9 %copy-start.15 = (f32[4]{0:T(128)S(1)}, f32[4]{0:T(128)}, u32[]{:S(2)}) copy-start(f32[4]{0:T(128)} %param.8) | copy-start | bytes 52
  179.3 58.4 %all-to-all-start.1 = ((bf16[128,128,128]{2,1,0:T(8,128)(2,1)}), bf16[128,128,128]{2,1,0:T(8,128)(2,1)}, u32[]{:S(2)}, u32[]{:S(2)}) async-start(bf16[128,128,128]{2,1,0:T(8,128)(2,1)} %bitcast.13), calls=%async_computation.1 | async-start | bytes 8388608 | tf_op jit(solution)/shard_map/all_to_all | solution.py:262
